TPU v7x, 32 devices: a whole 2x2x4 slice. The times are simulated.
32 devices in a mesh: lat: 8 (over y, x, core), lon: 4 (over z).
Axes of the slice: x: 2, y: 2, z: 4, core: 2. Of those that a mesh axis runs over, the one named last changes fastest.
Arguments:
- tokens: bfloat16 [8, 8, 128, 1024], P('lat', 'lon'), may hold values from -80 to 80
- w_qkv: bfloat16 [1024, 3072], replicated, may hold values from -0.1875 to 0.1875
- w_out: bfloat16 [1024, 1024], replicated, may hold values from -0.1875 to 0.1875
- tele_ids: int32 [8, 8, 8], P('lat', 'lon'), may hold values from 0 to 7, as said below
Outputs:
- mixed: bfloat16 [8, 8, 128, 1024], P('lat', 'lon')
Inputs may be any that keep to these rules, and one draw needn't show every extreme that they name: `tele_ids`: the 16 entries of one device's query tiles name exactly 4 tile columns of each lon device, lon device o holding the tile columns o * 2 to o * 2 + 1.
All inputs are finite; a program needn't handle non-finite values.
Results may differ from a plain program's by a relative error of at most 0.013.
The roundings to bfloat16 on the way count: a program that leaves them out, or rounds other values in their place, can miss the bound.
Values may be sent and summed in bfloat16 or wider, within the bound.
No kernel may reach another device: no remote copies, remote signals or barrier semaphores. Data moves between devices by JAX's collectives and lax.ppermute only.
A program may use at most 128 MiB of HBM per device.

v0:
```python
import jax
import jax.numpy as jnp
from jax import lax
from jax.sharding import PartitionSpec as P

H = 16
HD = 64
BLOCK = 128


def padded_2(array, sides, width, wrap):
    for axis, dim in sides:
        size, length = (lax.axis_size(axis), array.shape[dim])
        up = [(i, (i + 1) % size) for i in range(size if wrap else size - 1)]
        down = [(j, i) for i, j in up]
        last = lax.slice_in_dim(array, length - width, length, axis=dim)
        first = lax.slice_in_dim(array, 0, width, axis=dim)
        before = lax.ppermute(last, axis, up)
        after = lax.ppermute(first, axis, down)
        array = jnp.concatenate([before, array, after], axis=dim)
    return array


def attend(query, pairs, usable):
    tile_count = query.shape[0]
    key_count = pairs.shape[1]
    model_width = query.shape[2]
    group_width = 2 * HD

    def one_group(group_index):
        column_start = group_index * group_width
        queries = lax.dynamic_slice_in_dim(query, column_start, group_width, 2)
        queries = queries.reshape(tile_count, BLOCK, 2, HD)
        key_part = lax.dynamic_slice_in_dim(pairs, column_start, group_width, 2)
        key_part = key_part.reshape(tile_count, key_count, 2, HD)
        value_part = lax.dynamic_slice_in_dim(pairs, model_width + column_start, group_width, 2)
        value_part = value_part.reshape(tile_count, key_count, 2, HD)
        scores = jnp.einsum(
            "tqhd,tkhd->thqk", queries, key_part, preferred_element_type=jnp.float32
        ) * HD ** (-0.5)
        scores = jnp.where(usable[:, None, None, :], scores, -1e30)
        peak = jnp.max(scores, axis=-1, keepdims=True)
        expos = jnp.exp(scores - peak)
        weights = (expos / jnp.sum(expos, axis=-1, keepdims=True)).astype(jnp.bfloat16)
        summed = jnp.einsum(
            "thqk,tkhd->tqhd", weights, value_part, preferred_element_type=jnp.float32
        )
        return summed.astype(jnp.bfloat16).reshape(tile_count, BLOCK, group_width)

    outputs = lax.map(one_group, jnp.arange(H // 2, dtype=jnp.int32))
    return outputs.transpose(1, 2, 0, 3).reshape(tile_count, BLOCK, model_width)


def take_row(panel_row, index_row):
    return jnp.take(panel_row, index_row, axis=0)


def fetch_far(material, tele_ids):
    tile_rows, tile_cols, block_len, carried = material.shape
    tele_count = tele_ids.shape[2]
    row_picks = tele_ids.reshape(tile_rows, tile_cols * tele_count)
    empty = jnp.zeros((tile_rows, tile_cols * tele_count, block_len, carried), material.dtype)
    piece = lax.all_gather(material, "lon", axis=1, tiled=True)
    count = piece.shape[1]
    inside = (row_picks >= 0) & (row_picks < count)
    grabbed = jax.vmap(take_row)(piece, jnp.clip(row_picks, 0, count - 1))
    far_tiles = jnp.where(inside[:, :, None, None], grabbed, empty)
    return far_tiles.reshape(tile_rows, tile_cols, tele_count, block_len, carried)


def on_device(tokens, w_qkv, w_out, tele_ids):
    tile_rows, tile_cols, block_len, model_width = tokens.shape
    tele_count = tele_ids.shape[2]
    pair_width = 2 * model_width
    flat_tokens = tokens.reshape(-1, model_width)
    projected = jnp.dot(flat_tokens, w_qkv, preferred_element_type=jnp.float32).astype(jnp.bfloat16)
    query = projected[:, :model_width]
    material = projected[:, model_width:].reshape(tile_rows, tile_cols, block_len, pair_width)
    query = query.reshape(tile_rows * tile_cols, block_len, model_width)
    beside_all = padded_2(material, (("lon", 1),), 1, True)
    padded = padded_2(beside_all, (("lat", 0),), 1, False)
    far_tiles = fetch_far(material, tele_ids)
    near_tiles = jnp.stack(
        [
            padded[lat_step : lat_step + tile_rows, lon_step : lon_step + tile_cols]
            for lat_step in range(3)
            for lon_step in range(3)
        ],
        axis=2,
    )
    pairs = jnp.concatenate([near_tiles, far_tiles], axis=2)
    pairs = pairs.reshape(tile_rows * tile_cols, (9 + tele_count) * block_len, pair_width)
    first_row = lax.axis_index("lat") * tile_rows
    total_rows = tile_rows * lax.axis_size("lat")
    lat_steps = jnp.array([0, 0, 0, 1, 1, 1, 2, 2, 2], dtype=jnp.int32)
    global_rows = (
        first_row + jnp.arange(tile_rows, dtype=jnp.int32)[:, None] + lat_steps[None, :] - 1
    )
    near_usable = (global_rows >= 0) & (global_rows < total_rows)
    usable = jnp.concatenate([near_usable, jnp.ones((tile_rows, tele_count), jnp.bool_)], axis=1)
    usable = jnp.repeat(usable, block_len, axis=1)
    usable = jnp.broadcast_to(usable[:, None, :], (tile_rows, tile_cols, usable.shape[1]))
    usable = usable.reshape(tile_rows * tile_cols, -1)
    attended = attend(query, pairs, usable)
    mixed = jnp.dot(attended.reshape(-1, model_width), w_out, preferred_element_type=jnp.float32)
    return mixed.astype(jnp.bfloat16).reshape(tokens.shape)


def solution(mesh):
    return jax.shard_map(
        on_device,
        mesh=mesh,
        in_specs=(P("lat", "lon", None, None), P(), P(), P("lat", "lon", None)),
        out_specs=P("lat", "lon", None, None),
        check_vma=False,
    )
```

profile of v0, /device:TPU:12, one launch (start us, length us, event | category | flops | bytes accessed | tf_op | source)
XLA Modules:
  0.0 256.8 jit_solution(12976852504857619743)
XLA Ops:
  6.5 4.9 %convolution_convert_fusion = bf16[256,3072]{1,0:T(8,128)(2,1)S(1)} fusion(bf16[256,1024]{1,0:T(8,128)(2,1)} %bitcast.128, bf16[1024,3072]{1,0:T(8,128)(2,1)} %param.8), kind=kOutput, calls=%fused_computation.21 | convolution fusion | flops 1611399168 | bytes 8388608 | tf_op jit(solution)/shard_map/dot_general | solution.py:76
  11.4 1.1 copy-done.3
  13.8 1.6 collective-permute-start
  15.8 18.2 %collective-permute-done = bf16[1,1,128,2048]{3,2,1,0:T(8,128)(2,1)} collective-permute-done((bf16[1,1,128,2048]{3,2,1,0:T(8,128)(2,1)}, bf16[1,1,128,2048]{3,2,1,0:T(8,128)(2,1)}, u32[]{:S(2)}, u32[]{:S(2)}) %collective-permute-start) | collective-permute-done | bytes 524320 | tf_op jit(solution)/shard_map/ppermute | solution.py:18
  34.0 27.7 %collective-permute-done.1 = bf16[1,1,128,2048]{3,2,1,0:T(8,128)(2,1)} collective-permute-done((bf16[1,1,128,2048]{3,2,1,0:T(8,128)(2,1)}, bf16[1,1,128,2048]{3,2,1,0:T(8,128)(2,1)}, u32[]{:S(2)}, u32[]{:S(2)}) %collective-permute-start.1) | collective-permute-done | bytes 524320 | tf_op jit(solution)/shard_map/ppermute | solution.py:19
  61.7 3.1 %pad_maximum_fusion = bf16[1,4,128,2048]{3,2,1,0:T(8,128)(2,1)} fusion(bf16[1,1,128,2048]{3,2,1,0:T(8,128)(2,1)} %collective-permute-done.1, bf16[1,2,128,2048]{3,2,1,0:T(8,128)(2,1)} %bitcast.114, bf16[1,1,128,2048]{3,2,1,0:T(8,128)(2,1)} %collective-permute-done), kind=kLoop, calls=%fused_computation.22 | loop fusion | flops 2097152 | bytes 4194304 | tf_op jit(solution)/shard_map/concatenate | solution.py:20
  64.8 2.0 collective-permute-start.2
  66.9 1.9 slice.61
  69.0 4.5 %collective-permute-start.3 = (bf16[1,4,128,2048]{3,2,1,0:T(8,128)(2,1)}, bf16[1,4,128,2048]{3,2,1,0:T(8,128)(2,1)S(1)}, u32[]{:S(2)}, u32[]{:S(2)}) collective-permute-start(bf16[1,4,128,2048]{3,2,1,0:T(8,128)(2,1)} %pad_maximum_fusion), channel_id=1, source_target_pairs={{4,0},{8,4},{12,8},{16,12},{20,16},{24,20},{28,24},{5,1},{9,5},{13... | collective-permute-start | bytes 6291464 | tf_op jit(solution)/shard_map/ppermute | solution.py:19
  73.6 37.5 %collective-permute-done.2 = bf16[1,4,128,2048]{3,2,1,0:T(8,128)(2,1)} collective-permute-done((bf16[1,4,128,2048]{3,2,1,0:T(8,128)(2,1)}, bf16[1,4,128,2048]{3,2,1,0:T(8,128)(2,1)}, u32[]{:S(2)}, u32[]{:S(2)}) %collective-permute-start.2) | collective-permute-done | bytes 2097184 | tf_op jit(solution)/shard_map/ppermute | solution.py:18
  111.0 2.3 fusion.25
  113.3 2.3 fusion.24
  115.7 2.3 fusion.23
  118.0 2.1 fusion.22
  121.1 2.1 fusion.20
  123.3 1.1 fusion.18
  124.4 1.1 fusion.17
  125.5 1.1 fusion.16
  126.6 7.0 %gather_fusion = bf16[16,128,2048]{2,1,0:T(8,128)(2,1)} fusion(bf16[1,8,128,2048]{3,2,0,1:T(8,128)(2,1)} %all-gather.2.cloned.1.call-done, s32[16]{0:T(128)S(1)} %or_bitcast_fusion), kind=kCustom, calls=%fused_computation | custom fusion | bytes 16777344 | tf_op jit(solution)/shard_map/vmap(jit(_take))/gather | solution.py:55
  133.5 10.4 %select_dynamic-update-slice_fusion = bf16[1,2,17,128,2048]{4,3,2,1,0:T(8,128)(2,1)} fusion(bf16[1,2,17,128,2048]{4,3,2,1,0:T(8,128)(2,1)} %fusion.16, bf16[1,2,8,128,2048]{4,3,2,1,0:T(8,128)(2,1)} %bitcast.118, pred[2,8]{1,0:T(4,128)(4,1)S(1)} %compare_and_fusion, pred[2,8]{1,0:T(4,128)(4,1)S(1)} %and_bitcast_fusion.1), kind=kLoop, calls=%fused_computation.20 | loop fusion | flops 8388608 | bytes 16777248 | tf_op jit(solution)/shard_map/concatenate | solution.py:91
  144.0 22.1 %copy.37 = bf16[2,2176,2048]{1,2,0:T(8,128)(2,1)} copy(bf16[2,2176,2048]{2,1,0:T(8,128)(2,1)} %bitcast.25) | data formatting | bytes 35651584
  166.1 81.0 %while.13 = (s32[]{:T(128)}, bf16[8,2,128,128]{2,3,1,0:T(8,128)(2,1)}, s32[8]{0:T(128)S(1)}, bf16[2,2176,2048]{1,2,0:T(8,128)(2,1)}, bf16[2,128,1024]{2,1,0:T(8,...) while((s32[]{:T(128)}, ...), condition=%wide.region_3.4_spmd.clone, body=%wide.region_0.0_spmd.clone.sunk | while | flops 437883648 | bytes 8397814 | solution.py:50
  167.3 2.8 %constant_dynamic-slice_fusion.5 = (bf16[2,2176,128]{1,2,0:T(8,128)(2,1)S(1)}, bf16[2,2176,128]{1,2,0:T(8,128)(2,1)}) fusion(bf16[2,2176,2048]{1,2,0:T(8,128)(2,1)} %get-tuple-element.200, s32[]{:T(128)S(6)} %select_n.108, s32[]{:T(128)S(6)} %select_n.109), kind=kLoop, calls=%fused_computation.11.clone.1 | loop fusion | bytes 4456456 | tf_op jit(solution)/shard_map/while/body/eval_jaxpr/dynamic_slice | solution.py:34
  171.1 1.5 fusion.50
  172.5 3.1 %fusion.51 = bf16[2,2,64,128]{3,2,1,0:T(8,128)(2,1)S(1)} fusion(bf16[2,2176,2,64]{1,3,2,0:T(8,128)(2,1)} %bitcast.121, f32[2,2,128]{2,1,0:T(2,128)S(1)} %fusion.50, bf16[2,128,2,64]{1,3,2,0:T(8,128)(2,1)S(1)} %bitcast.123, bf16[2,2176,2,64]{1,3,2,0:T(8,128)(2,1)S(1)} %bitcast.120, pred[2176]{0:T(1024)(128)(4,1)S(1)} %get-tuple-element.202), kind=kOutput, calls=%fused_computation.9.clone.1 | convolution fusion | flops 290818688 | bytes 2363520 | tf_op jit(solution)/shard_map/while/body/eval_jaxpr/thqk,tkhd->tqhd/dot_general | solution.py:45
  177.4 2.8 %constant_dynamic-slice_fusion.5 = (bf16[2,2176,128]{1,2,0:T(8,128)(2,1)S(1)}, bf16[2,2176,128]{1,2,0:T(8,128)(2,1)}) fusion(bf16[2,2176,2048]{1,2,0:T(8,128)(2,1)} %get-tuple-element.200, s32[]{:T(128)S(6)} %select_n.108, s32[]{:T(128)S(6)} %select_n.109), kind=kLoop, calls=%fused_computation.11.clone.1 | loop fusion | bytes 4456456 | tf_op jit(solution)/shard_map/while/body/eval_jaxpr/dynamic_slice | solution.py:34
  181.2 1.5 fusion.50
  182.7 3.1 %fusion.51 = bf16[2,2,64,128]{3,2,1,0:T(8,128)(2,1)S(1)} fusion(bf16[2,2176,2,64]{1,3,2,0:T(8,128)(2,1)} %bitcast.121, f32[2,2,128]{2,1,0:T(2,128)S(1)} %fusion.50, bf16[2,128,2,64]{1,3,2,0:T(8,128)(2,1)S(1)} %bitcast.123, bf16[2,2176,2,64]{1,3,2,0:T(8,128)(2,1)S(1)} %bitcast.120, pred[2176]{0:T(1024)(128)(4,1)S(1)} %get-tuple-element.202), kind=kOutput, calls=%fused_computation.9.clone.1 | convolution fusion | flops 290818688 | bytes 2363520 | tf_op jit(solution)/shard_map/while/body/eval_jaxpr/thqk,tkhd->tqhd/dot_general | solution.py:45
  187.6 2.8 %constant_dynamic-slice_fusion.5 = (bf16[2,2176,128]{1,2,0:T(8,128)(2,1)S(1)}, bf16[2,2176,128]{1,2,0:T(8,128)(2,1)}) fusion(bf16[2,2176,2048]{1,2,0:T(8,128)(2,1)} %get-tuple-element.200, s32[]{:T(128)S(6)} %select_n.108, s32[]{:T(128)S(6)} %select_n.109), kind=kLoop, calls=%fused_computation.11.clone.1 | loop fusion | bytes 4456456 | tf_op jit(solution)/shard_map/while/body/eval_jaxpr/dynamic_slice | solution.py:34
  191.3 1.5 fusion.50
  192.8 3.1 %fusion.51 = bf16[2,2,64,128]{3,2,1,0:T(8,128)(2,1)S(1)} fusion(bf16[2,2176,2,64]{1,3,2,0:T(8,128)(2,1)} %bitcast.121, f32[2,2,128]{2,1,0:T(2,128)S(1)} %fusion.50, bf16[2,128,2,64]{1,3,2,0:T(8,128)(2,1)S(1)} %bitcast.123, bf16[2,2176,2,64]{1,3,2,0:T(8,128)(2,1)S(1)} %bitcast.120, pred[2176]{0:T(1024)(128)(4,1)S(1)} %get-tuple-element.202), kind=kOutput, calls=%fused_computation.9.clone.1 | convolution fusion | flops 290818688 | bytes 2363520 | tf_op jit(solution)/shard_map/while/body/eval_jaxpr/thqk,tkhd->tqhd/dot_general | solution.py:45
  197.7 2.8 %constant_dynamic-slice_fusion.5 = (bf16[2,2176,128]{1,2,0:T(8,128)(2,1)S(1)}, bf16[2,2176,128]{1,2,0:T(8,128)(2,1)}) fusion(bf16[2,2176,2048]{1,2,0:T(8,128)(2,1)} %get-tuple-element.200, s32[]{:T(128)S(6)} %select_n.108, s32[]{:T(128)S(6)} %select_n.109), kind=kLoop, calls=%fused_computation.11.clone.1 | loop fusion | bytes 4456456 | tf_op jit(solution)/shard_map/while/body/eval_jaxpr/dynamic_slice | solution.py:34
  201.4 1.5 fusion.50
  202.9 3.1 %fusion.51 = bf16[2,2,64,128]{3,2,1,0:T(8,128)(2,1)S(1)} fusion(bf16[2,2176,2,64]{1,3,2,0:T(8,128)(2,1)} %bitcast.121, f32[2,2,128]{2,1,0:T(2,128)S(1)} %fusion.50, bf16[2,128,2,64]{1,3,2,0:T(8,128)(2,1)S(1)} %bitcast.123, bf16[2,2176,2,64]{1,3,2,0:T(8,128)(2,1)S(1)} %bitcast.120, pred[2176]{0:T(1024)(128)(4,1)S(1)} %get-tuple-element.202), kind=kOutput, calls=%fused_computation.9.clone.1 | convolution fusion | flops 290818688 | bytes 2363520 | tf_op jit(solution)/shard_map/while/body/eval_jaxpr/thqk,tkhd->tqhd/dot_general | solution.py:45
  207.8 2.8 %constant_dynamic-slice_fusion.5 = (bf16[2,2176,128]{1,2,0:T(8,128)(2,1)S(1)}, bf16[2,2176,128]{1,2,0:T(8,128)(2,1)}) fusion(bf16[2,2176,2048]{1,2,0:T(8,128)(2,1)} %get-tuple-element.200, s32[]{:T(128)S(6)} %select_n.108, s32[]{:T(128)S(6)} %select_n.109), kind=kLoop, calls=%fused_computation.11.clone.1 | loop fusion | bytes 4456456 | tf_op jit(solution)/shard_map/while/body/eval_jaxpr/dynamic_slice | solution.py:34
  211.6 1.5 fusion.50
  213.0 3.1 %fusion.51 = bf16[2,2,64,128]{3,2,1,0:T(8,128)(2,1)S(1)} fusion(bf16[2,2176,2,64]{1,3,2,0:T(8,128)(2,1)} %bitcast.121, f32[2,2,128]{2,1,0:T(2,128)S(1)} %fusion.50, bf16[2,128,2,64]{1,3,2,0:T(8,128)(2,1)S(1)} %bitcast.123, bf16[2,2176,2,64]{1,3,2,0:T(8,128)(2,1)S(1)} %bitcast.120, pred[2176]{0:T(1024)(128)(4,1)S(1)} %get-tuple-element.202), kind=kOutput, calls=%fused_computation.9.clone.1 | convolution fusion | flops 290818688 | bytes 2363520 | tf_op jit(solution)/shard_map/while/body/eval_jaxpr/thqk,tkhd->tqhd/dot_general | solution.py:45
  217.9 2.8 %constant_dynamic-slice_fusion.5 = (bf16[2,2176,128]{1,2,0:T(8,128)(2,1)S(1)}, bf16[2,2176,128]{1,2,0:T(8,128)(2,1)}) fusion(bf16[2,2176,2048]{1,2,0:T(8,128)(2,1)} %get-tuple-element.200, s32[]{:T(128)S(6)} %select_n.108, s32[]{:T(128)S(6)} %select_n.109), kind=kLoop, calls=%fused_computation.11.clone.1 | loop fusion | bytes 4456456 | tf_op jit(solution)/shard_map/while/body/eval_jaxpr/dynamic_slice | solution.py:34
  221.7 1.5 fusion.50
  223.2 3.1 %fusion.51 = bf16[2,2,64,128]{3,2,1,0:T(8,128)(2,1)S(1)} fusion(bf16[2,2176,2,64]{1,3,2,0:T(8,128)(2,1)} %bitcast.121, f32[2,2,128]{2,1,0:T(2,128)S(1)} %fusion.50, bf16[2,128,2,64]{1,3,2,0:T(8,128)(2,1)S(1)} %bitcast.123, bf16[2,2176,2,64]{1,3,2,0:T(8,128)(2,1)S(1)} %bitcast.120, pred[2176]{0:T(1024)(128)(4,1)S(1)} %get-tuple-element.202), kind=kOutput, calls=%fused_computation.9.clone.1 | convolution fusion | flops 290818688 | bytes 2363520 | tf_op jit(solution)/shard_map/while/body/eval_jaxpr/thqk,tkhd->tqhd/dot_general | solution.py:45
  228.0 2.8 %constant_dynamic-slice_fusion.5 = (bf16[2,2176,128]{1,2,0:T(8,128)(2,1)S(1)}, bf16[2,2176,128]{1,2,0:T(8,128)(2,1)}) fusion(bf16[2,2176,2048]{1,2,0:T(8,128)(2,1)} %get-tuple-element.200, s32[]{:T(128)S(6)} %select_n.108, s32[]{:T(128)S(6)} %select_n.109), kind=kLoop, calls=%fused_computation.11.clone.1 | loop fusion | bytes 4456456 | tf_op jit(solution)/shard_map/while/body/eval_jaxpr/dynamic_slice | solution.py:34
  231.8 1.5 fusion.50
  233.3 3.1 %fusion.51 = bf16[2,2,64,128]{3,2,1,0:T(8,128)(2,1)S(1)} fusion(bf16[2,2176,2,64]{1,3,2,0:T(8,128)(2,1)} %bitcast.121, f32[2,2,128]{2,1,0:T(2,128)S(1)} %fusion.50, bf16[2,128,2,64]{1,3,2,0:T(8,128)(2,1)S(1)} %bitcast.123, bf16[2,2176,2,64]{1,3,2,0:T(8,128)(2,1)S(1)} %bitcast.120, pred[2176]{0:T(1024)(128)(4,1)S(1)} %get-tuple-element.202), kind=kOutput, calls=%fused_computation.9.clone.1 | convolution fusion | flops 290818688 | bytes 2363520 | tf_op jit(solution)/shard_map/while/body/eval_jaxpr/thqk,tkhd->tqhd/dot_general | solution.py:45
  238.2 2.8 %constant_dynamic-slice_fusion.5 = (bf16[2,2176,128]{1,2,0:T(8,128)(2,1)S(1)}, bf16[2,2176,128]{1,2,0:T(8,128)(2,1)}) fusion(bf16[2,2176,2048]{1,2,0:T(8,128)(2,1)} %get-tuple-element.200, s32[]{:T(128)S(6)} %select_n.108, s32[]{:T(128)S(6)} %select_n.109), kind=kLoop, calls=%fused_computation.11.clone.1 | loop fusion | bytes 4456456 | tf_op jit(solution)/shard_map/while/body/eval_jaxpr/dynamic_slice | solution.py:34
  241.9 1.5 fusion.50
  243.4 3.1 %fusion.51 = bf16[2,2,64,128]{3,2,1,0:T(8,128)(2,1)S(1)} fusion(bf16[2,2176,2,64]{1,3,2,0:T(8,128)(2,1)} %bitcast.121, f32[2,2,128]{2,1,0:T(2,128)S(1)} %fusion.50, bf16[2,128,2,64]{1,3,2,0:T(8,128)(2,1)S(1)} %bitcast.123, bf16[2,2176,2,64]{1,3,2,0:T(8,128)(2,1)S(1)} %bitcast.120, pred[2176]{0:T(1024)(128)(4,1)S(1)} %get-tuple-element.202), kind=kOutput, calls=%fused_computation.9.clone.1 | convolution fusion | flops 290818688 | bytes 2363520 | tf_op jit(solution)/shard_map/while/body/eval_jaxpr/thqk,tkhd->tqhd/dot_general | solution.py:45
  247.1 1.3 copy.39
  248.5 1.5 convolution_convert_fusion.1
  (63 shorter events, 20.4 us)
Async XLA Ops:
  6.5 241.9 %copy-start = (bf16[1024,1024]{1,0:T(8,128)(2,1)S(1)}, bf16[1024,1024]{1,0:T(8,128)(2,1)}, u32[]{:S(2)}) copy-start(bf16[1024,1024]{1,0:T(8,128)(2,1)} %param.9) | copy-start | bytes 6291460
  6.5 120.0 %all-gather.2.cloned.1.call-start = ((), (), s32[]{:S(2)}) async-start(), calls=%async_computation | async-start | bytes 5242880 | tf_op jit(solution)/shard_map/all_gather | solution.py:63
  11.4 1.1 copy-start.3
  12.7 3.1 %copy-start.1 = (bf16[256,2048]{1,0:T(8,128)(2,1)}, bf16[256,2048]{1,0:T(8,128)(2,1)S(1)}, u32[]{:S(2)}) copy-start(bf16[256,2048]{1,0:T(8,128)(2,1)S(1)} %slice.52) | copy-start | bytes 3145732
  12.7 56.1 %copy-start.4 = (s32[1,2,8]{2,1,0:T(2,128)S(1)}, s32[1,2,8]{2,1,0:T(2,128)}, u32[]{:S(2)}) copy-start(s32[1,2,8]{2,1,0:T(2,128)} %param.10) | copy-start | bytes 196
  12.7 56.2 %copy-start.5 = (s32[9]{0:T(128)S(1)}, s32[9]{0:T(128)}, u32[]{:S(2)}) copy-start(s32[9]{0:T(128)} %constant.95.clone) | copy-start | bytes 112
  13.8 20.3 %collective-permute-start = (bf16[1,1,128,2048]{3,2,1,0:T(8,128)(2,1)}, bf16[1,1,128,2048]{3,2,1,0:T(8,128)(2,1)}, u32[]{:S(2)}, u32[]{:S(2)}) collective-permute-start(bf16[1,1,128,2048]{3,2,1,0:T(8,128)(2,1)} %get-tuple-element.130), channel_id=1, source_target_pairs={{0,1},{1,2},{2,3},{3,0},{4,5},{5,6},{6,7},{7,4},{8,9},{9,10},{10,1... | collective-permute-start | bytes 1572872 | tf_op jit(solution)/shard_map/ppermute | solution.py:18
  15.3 46.4 %collective-permute-start.1 = (bf16[1,1,128,2048]{3,2,1,0:T(8,128)(2,1)}, bf16[1,1,128,2048]{3,2,1,0:T(8,128)(2,1)}, u32[]{:S(2)}, u32[]{:S(2)}) collective-permute-start(bf16[1,1,128,2048]{3,2,1,0:T(8,128)(2,1)} %get-tuple-element.131), channel_id=1, source_target_pairs={{1,0},{2,1},{3,2},{0,3},{5,4},{6,5},{7,6},{4,7},{9,8},{10,9},{11,1... | collective-permute-start | bytes 1572872 | tf_op jit(solution)/shard_map/ppermute | solution.py:19
  64.8 53.2 %copy-start.2 = (bf16[256,2048]{1,0:T(8,128)(2,1)S(1)}, bf16[256,2048]{1,0:T(8,128)(2,1)}, u32[]{:S(2)}) copy-start(bf16[256,2048]{1,0:T(8,128)(2,1)} %copy-done.1) | copy-start | bytes 3145732
  64.8 46.2 %collective-permute-start.2 = (bf16[1,4,128,2048]{3,2,1,0:T(8,128)(2,1)}, bf16[1,4,128,2048]{3,2,1,0:T(8,128)(2,1)}, u32[]{:S(2)}, u32[]{:S(2)}) collective-permute-start(bf16[1,4,128,2048]{3,2,1,0:T(8,128)(2,1)} %pad_maximum_fusion), channel_id=1, source_target_pairs={{0,4},{4,8},{8,12},{12,16},{16,20},{20,24},{24,28},{1,5},{5,9},{9,... | collective-permute-start | bytes 6291464 | tf_op jit(solution)/shard_map/ppermute | solution.py:18
  69.0 54.3 %collective-permute-start.3 = (bf16[1,4,128,2048]{3,2,1,0:T(8,128)(2,1)}, bf16[1,4,128,2048]{3,2,1,0:T(8,128)(2,1)S(1)}, u32[]{:S(2)}, u32[]{:S(2)}) collective-permute-start(bf16[1,4,128,2048]{3,2,1,0:T(8,128)(2,1)} %pad_maximum_fusion), channel_id=1, source_target_pairs={{4,0},{8,4},{12,8},{16,12},{20,16},{24,20},{28,24},{5,1},{9,5},{13... | collective-permute-start | bytes 6291464 | tf_op jit(solution)/shard_map/ppermute | solution.py:19
Sparse Core Ops, SparseCore 0:
  15.9 91.0 all-gather.1
where the time goes:
time: 259 us; the launch traced here: 257 us
  local copies, waits for them, and re-layouts  86 us (33%)
  waiting for transfers between devices  83.4 us (32%)
  matrix products  42.6 us (16%)
  other arithmetic  17.8 us (7%)
  between operations  13.5 us (5%)
  starting transfers between devices  8.6 us (3%)
  loops' own time  4.92 us (2%)
    ppermute x2, waiting for transfers between devices, padded_2(): before = lax.ppermute(last, axis, up)  55.7 us
    unnamed x20, local copies, waits for them, and re-layouts  34.6 us
    ppermute x2, waiting for transfers between devices, padded_2(): after = lax.ppermute(first, axis, down)  27.7 us
    dot_general x8, matrix products, one_group(): jnp.einsum('thqk,tkhd->tqhd', weights, value_part, preferred_element_type...  24.4 us
    dynamic_slice x8, local copies, waits for them, and re-layouts, one_group(): key_part = lax.dynamic_slice_in_dim(pairs, column_start, group_width, 2)  22.4 us
    sub x8, matrix products, one_group(): expos = jnp.exp(scores - peak)  11.7 us
    concatenate x1, other arithmetic, on_device(): pairs = jnp.concatenate([near_tiles, far_tiles], axis=2)  10.4 us
    dynamic_slice x16, local copies, waits for them, and re-layouts, one_group(): queries = lax.dynamic_slice_in_dim(query, column_start, group_width, 2)  7.7 us
  transfers between devices with their start and end apart: 5, of which 3 were waited for; matrix products, arithmetic and copies ran while one was open for 8% of the time, Pallas kernels for 0%

commit v1 on v0

v1 whole, which is shorter than its diff:
```python
import functools
import jax
import jax.numpy as jnp
from jax import lax
from jax.experimental import pallas as pl
from jax.experimental.pallas import tpu as pltpu
from jax.sharding import PartitionSpec as P

HD = 64
BLOCK = 128
PAIR = 2 * HD
NEG = -1e30
CW = 256
VM = 24
UNIT = 1.4426950408889634 * HD ** -0.5


def bias_lanes(value):
    lane = lax.broadcasted_iota(jnp.int32, (BLOCK, PAIR), 1)
    whole = jnp.full((BLOCK, PAIR), value, jnp.float32)
    hi = whole.astype(jnp.bfloat16).astype(jnp.float32)
    mid = (whole - hi).astype(jnp.bfloat16).astype(jnp.float32)
    low = whole - hi - mid
    picked = jnp.where(lane == 0, hi, jnp.where(lane == 1, mid, jnp.where(lane == 2, low, 0.0)))
    return picked.astype(jnp.bfloat16)


def update(q, keys, values, bias_at, users, o_ref, m_ref, l_ref, first):
    left = lax.broadcasted_iota(jnp.int32, (BLOCK, PAIR), 1) < HD
    one = jnp.ones((2 * BLOCK, PAIR), jnp.bfloat16)
    for t in range(2):
        tiles = users[t]
        if not tiles:
            continue
        rows = slice(t * BLOCK, (t + 1) * BLOCK)
        kb = jnp.concatenate([bias_lanes(bias_at(t, j)) for j in tiles], 0)
        for pr in range(CW // PAIR):
            cols = slice(pr * PAIR, (pr + 1) * PAIR)
            qp = q[rows, cols]
            zero = jnp.zeros_like(qp)
            qbd = jnp.concatenate([jnp.where(left, qp, zero), jnp.where(left, zero, qp)], 0)
            qbd = jnp.concatenate([qbd, one], 1)
            kp = jnp.concatenate([keys[j][:, cols] for j in tiles], 0)
            kp = jnp.concatenate([kp, kb], 1)
            s = lax.dot_general(qbd, kp, (((1,), (1,)), ((), ())), preferred_element_type=jnp.float32)
            m = jnp.max(s, axis=1, keepdims=True)
            p = jnp.exp2((s - m) * UNIT).astype(jnp.bfloat16)
            vp = jnp.concatenate([values[j][:, cols] for j in tiles], 0)
            vp = jnp.concatenate([vp, jnp.ones((len(tiles) * BLOCK, PAIR), jnp.bfloat16)], 1)
            r = jnp.dot(p, vp, preferred_element_type=jnp.float32)
            o = jnp.where(left, r[:BLOCK, :PAIR], r[BLOCK:, :PAIR])
            l = jnp.where(left, r[:BLOCK, PAIR:], r[BLOCK:, PAIR:])
            m = jnp.where(left, m[:BLOCK], m[BLOCK:])
            if not first:
                m_old = m_ref[rows, cols]
                peak = jnp.maximum(m, m_old)
                was = jnp.exp2((m_old - peak) * UNIT)
                now = jnp.exp2((m - peak) * UNIT)
                o = o_ref[rows, cols] * was + o * now
                l = l_ref[rows, cols] * was + l * now
                m = peak
            o_ref[rows, cols] = o
            l_ref[rows, cols] = l
            m_ref[rows, cols] = m


def project(xs, w, off):
    flat = jnp.concatenate(xs, 0)
    return jnp.dot(flat, w[:, pl.ds(off, CW)], preferred_element_type=jnp.float32).astype(jnp.bfloat16)


def split(a):
    return [a[i:i + BLOCK] for i in range(0, a.shape[0], BLOCK)]


def groups(width, body):
    if LOOP:
        lax.fori_loop(0, width // CW, lambda i, c: (body(pl.multiple_of(i * CW, CW)), c)[1], 0)
    else:
        for i in range(width // CW):
            body(i * CW)


LOOP = False


def first_kernel(base, bias_ref, x_ref, w, q_ref, o_ref, m_ref, l_ref):
    width = x_ref.shape[-1]

    def body(off):
        here = pl.ds(off, CW)
        xs = [x_ref[j] for j in range(2)]
        q = project(xs, w, off)
        q_ref[:, here] = q
        keys, values = split(project(xs, w, width + off)), split(project(xs, w, 2 * width + off))
        update(q, keys, values, lambda t, j: bias_ref[t, base + j], [[0, 1], [0, 1]],
               o_ref.at[:, here], m_ref.at[:, here], l_ref.at[:, here], True)

    groups(width, body)


def step_kernel(base, users, counts, bias_ref, *refs):
    x_refs, (q_ref, w, o_in, m_in, l_in, o_ref, m_ref, l_ref) = refs[:len(counts)], refs[len(counts):]
    width = q_ref.shape[-1]

    def body(off):
        here = pl.ds(off, CW)
        xs = [r[j] for r, n in zip(x_refs, counts) for j in range(n)]
        keys, values = split(project(xs, w, width + off)), split(project(xs, w, 2 * width + off))
        update(q_ref[:, here], keys, values, lambda t, j: bias_ref[t, base + j], users,
               o_ref.at[:, here], m_ref.at[:, here], l_ref.at[:, here], False)

    groups(width, body)


def last_kernel(base, users, counts, bias_ref, *refs):
    x_refs, (q_ref, w, w_out, o_in, m_in, l_in, out_ref, o_ref, m_ref, l_ref, acc) = refs[:len(counts)], refs[len(counts):]
    width = q_ref.shape[-1]
    acc[...] = jnp.zeros_like(acc)

    def body(off):
        here = pl.ds(off, CW)
        xs = [r[j] for r, n in zip(x_refs, counts) for j in range(n)]
        keys, values = split(project(xs, w, width + off)), split(project(xs, w, 2 * width + off))
        update(q_ref[:, here], keys, values, lambda t, j: bias_ref[t, base + j], users,
               o_ref.at[:, here], m_ref.at[:, here], l_ref.at[:, here], False)
        att = (o_ref[:, here] / l_ref[:, here]).astype(jnp.bfloat16)
        acc[...] += jnp.dot(att, w_out[here, :], preferred_element_type=jnp.float32)

    groups(width, body)
    out_ref[...] = acc[...].astype(jnp.bfloat16)


PARAMS = pltpu.CompilerParams(vmem_limit_bytes=VM * 1024 * 1024)
SMEM = pl.BlockSpec(memory_space=pltpu.SMEM)
VMEM = pl.BlockSpec(memory_space=pltpu.VMEM)


def state_shapes(width):
    return [jax.ShapeDtypeStruct((2 * BLOCK, width), jnp.float32)] * 3


def run_first(base, bias, x, w_qkv):
    width = x.shape[-1]
    return pl.pallas_call(
        functools.partial(first_kernel, base),
        in_specs=[SMEM] + [VMEM] * 2, out_specs=[VMEM] * 4,
        out_shape=[jax.ShapeDtypeStruct((2 * BLOCK, width), jnp.bfloat16)] + state_shapes(width),
        compiler_params=PARAMS, name="own",
    )(bias, x, w_qkv)


def run_step(base, users, bias, xs, q, w_qkv, state, name):
    width = q.shape[-1]
    counts = [x.shape[0] for x in xs]
    n = len(xs)
    return pl.pallas_call(
        functools.partial(step_kernel, base, users, counts),
        in_specs=[SMEM] + [VMEM] * (n + 5), out_specs=[VMEM] * 3, out_shape=state_shapes(width),
        input_output_aliases={n + 3: 0, n + 4: 1, n + 5: 2},
        compiler_params=PARAMS, name=name,
    )(bias, *xs, q, w_qkv, *state)


def run_last(base, users, bias, xs, q, w_qkv, w_out, state):
    width = q.shape[-1]
    counts = [x.shape[0] for x in xs]
    n = len(xs)
    return pl.pallas_call(
        functools.partial(last_kernel, base, users, counts),
        in_specs=[SMEM] + [VMEM] * (n + 6), out_specs=[VMEM] * 4,
        out_shape=[jax.ShapeDtypeStruct((2 * BLOCK, width), jnp.bfloat16)] + state_shapes(width),
        input_output_aliases={n + 4: 1, n + 5: 2, n + 6: 3},
        scratch_shapes=[pltpu.VMEM((2 * BLOCK, width), jnp.float32)],
        compiler_params=PARAMS, name="last",
    )(bias, *xs, q, w_qkv, w_out, *state)[0]


BOTH = [[0, 1], [0, 1]]


def pass_on(array, axis, pairs):
    return lax.ppermute(array, axis, pairs)


def make_bias(tele_ids, columns, usable, in_row, own_first, total):
    query_column = (own_first + jnp.arange(2, dtype=jnp.int32))[:, None]
    told = (tele_ids[:, None, :] == columns[None, :, None]).sum(-1)
    beside = lax.rem(columns[None, :] - query_column + 1 + total, total) <= 2
    times = jnp.where(in_row[None, :], told + beside, 1) * usable[None, :]
    logs = jnp.log(jnp.maximum(times, 1).astype(jnp.float32)) * HD ** 0.5
    return jnp.where(times > 0, logs, NEG)


def lat_swap(array, n_lat):
    same = [(i, i ^ 1) for i in range(n_lat)]
    other = [p for i in range(1, n_lat - 1, 2) for p in ((i, i + 1), (i + 1, i))]
    return pass_on(array, "lat", same), pass_on(array, "lat", other)


def on_device(tokens, w_qkv, w_out, tele_ids):
    n_lat, n_lon = lax.axis_size("lat"), lax.axis_size("lon")
    total = 2 * n_lon
    a, z = lax.axis_index("lat"), lax.axis_index("lon")
    x = tokens[0]
    first, last = z == 0, z == n_lon - 1
    edge_ok = jnp.where(a % 2 == 0, a > 0, a < n_lat - 1)
    i32 = lambda *v: jnp.stack([jnp.asarray(u, jnp.int32) for u in v])
    b = 2 * z
    yes = jnp.int32(1)
    if n_lon == 4:
        across = lax.rem(z + 2, 4) * 2
        columns = i32(b, b + 1, 0, 0, 0, 0, b - 2, b - 1, b + 2, b + 3,
                      jnp.where(first, total - 1, 0), 0, 0, 0, 0, across, across + 1, jnp.where(first, total - 2, 1))
        ends = first | last
        usable = i32(yes, yes, yes, yes, edge_ok, edge_ok, ~first, ~first, ~last, ~last,
                     ends, yes, yes, edge_ok, edge_ok, yes, yes, ends)
        in_row = jnp.array([1, 1, 0, 0, 0, 0, 1, 1, 1, 1, 1, 0, 0, 0, 0, 1, 1, 1], jnp.bool_)
    else:
        everywhere = jnp.arange(total, dtype=jnp.int32)
        columns = jnp.concatenate([i32(b, b + 1, 0, 0, 0, 0, 0, 0, 0, 0), everywhere])
        not_own = ((everywhere < b) | (everywhere > b + 1)).astype(jnp.int32)
        usable = jnp.concatenate([i32(yes, yes, yes, yes, edge_ok, edge_ok, yes, yes, edge_ok, edge_ok), not_own])
        in_row = jnp.array([1, 1] + [0] * 8 + [1] * total, jnp.bool_)
    bias = make_bias(tele_ids[0], columns, usable, in_row, b, total)

    if n_lon == 4:
        wrap = pass_on(jnp.where(first, x[0], x[1])[None], "lon", [(0, 3), (3, 0)])
        up1 = pass_on(x, "lon", [(i, i + 1) for i in range(3)])
        down1 = pass_on(x, "lon", [(i + 1, i) for i in range(3)])
    same, other = lat_swap(x, n_lat)
    q, *state = run_first(0, bias, x, w_qkv)
    state = run_step(2, [[0, 1, 2, 3]] * 2, bias, [same, other], q, w_qkv, state, "rim_own")
    if n_lon == 4:
        up2 = pass_on(up1, "lon", [(1, 2), (2, 3)])
        down2 = pass_on(down1, "lon", [(2, 1), (1, 0)])
        edges = jnp.concatenate([jnp.where(first, wrap, up1[1:]), jnp.where(last, wrap, down1[:1])], 0)
        same_edges, other_edges = lat_swap(edges, n_lat)
        state = run_step(6, [[0, 1, 2, 3]] * 2, bias, [up1, down1], q, w_qkv, state, "beside")
        state = run_step(10, [[0, 1, 3], [0, 2, 4]], bias, [wrap, same_edges, other_edges], q, w_qkv, state, "rim_edge")
        far = jnp.where(z < 2, down2, up2)
        final = pass_on(jnp.where(z < 2, down2[:1], up2[1:]), "lon", [(1, 0), (2, 3)])
        state = run_step(15, BOTH, bias, [far], q, w_qkv, state, "across")
        mixed = run_last(17, [[0], [0]], bias, [final], q, w_qkv, w_out, state)
    else:
        before = pass_on(x[1:], "lon", [(i, (i + 1) % n_lon) for i in range(n_lon)])
        after = pass_on(x[:1], "lon", [((i + 1) % n_lon, i) for i in range(n_lon)])
        same_edges, other_edges = lat_swap(jnp.concatenate([before, after], 0), n_lat)
        state = run_step(6, [[0, 2], [1, 3]], bias, [same_edges, other_edges], q, w_qkv, state, "rim_edge")
        row = lax.all_gather(x, "lon", axis=0, tiled=True)
        for s in range(0, total, 4):
            args = (10 + s, [[0, 1, 2, 3]] * 2, bias, [row[s:s + 4]], q, w_qkv)
            if s + 4 < total:
                state = run_step(*args, state, "columns")
        mixed = run_last(*args, w_out, state)
    return mixed.reshape(tokens.shape)


def solution(mesh):
    return jax.shard_map(
        on_device,
        mesh=mesh,
        in_specs=(P("lat", "lon", None, None), P(), P(), P("lat", "lon", None)),
        out_specs=P("lat", "lon", None, None),
        check_vma=False,
    )
```

time: 259 us -> 74.6 us (0.29)
  the two profiles are of different devices: /device:TPU:12 before, /device:TPU:9 now
where the time goes in v1:
time: 74.6 us; the launch traced here: 74.1 us
  Pallas kernels  33.3 us (45%)
  starting transfers between devices  28.1 us (38%)
  other arithmetic  5.78 us (8%)
  local copies, waits for them, and re-layouts  4.02 us (5%)
  waiting for transfers between devices  2.64 us (4%)
    ppermute x10, starting transfers between devices, pass_on(): return lax.ppermute(array, axis, pairs)  28.1 us
    pallas_call x4, Pallas kernels, run_step(): pl.pallas_call(functools.partial(step_kernel, base, users, counts), in_sp...  22.5 us
    pallas_call x1, Pallas kernels, run_last(): pl.pallas_call(functools.partial(last_kernel, base, users, counts), in_sp...  5.51 us
    pallas_call x1, Pallas kernels, run_first(): pl.pallas_call(functools.partial(first_kernel, base), in_specs=[SMEM] + [...  5.27 us
    unnamed x8, local copies, waits for them, and re-layouts  3.83 us
    ppermute x10, waiting for transfers between devices, pass_on(): return lax.ppermute(array, axis, pairs)  2.64 us
  transfers between devices with their start and end apart: 10, of which 1 were waited for; matrix products, arithmetic and copies ran while one was open for 8% of the time, Pallas kernels for 38%

profile of v1, /device:TPU:9, one launch (start us, length us, event | category | flops | bytes accessed | tf_op | source)
XLA Modules:
  0.0 74.1 jit_solution(7619251513682584326)
XLA Ops:
  0.0 1.9 %collective-permute-start = (bf16[2,128,1024]{2,1,0:T(8,128)(2,1)}, bf16[2,128,1024]{2,1,0:T(8,128)(2,1)S(1)}, u32[]{:S(2)}, u32[]{:S(2)}) collective-permute-start(bf16[2,128,1024]{2,1,0:T(8,128)(2,1)} %bitcast.19), channel_id=1, source_target_pairs={{1,0},{2,1},{3,2},{5,4},{6,5},{7,6},{9,8},{10,9},{11,10},{13,12},{... | collective-permute-start | bytes 1572872 | tf_op jit(solution)/shard_map/ppermute | solution.py:183
  1.9 3.4 %collective-permute-start.2 = (bf16[2,128,1024]{2,1,0:T(8,128)(2,1)}, bf16[2,128,1024]{2,1,0:T(8,128)(2,1)S(1)}, u32[]{:S(2)}, u32[]{:S(2)}) collective-permute-start(bf16[2,128,1024]{2,1,0:T(8,128)(2,1)} %bitcast.20), channel_id=1, source_target_pairs={{0,1},{1,2},{2,3},{4,5},{5,6},{6,7},{8,9},{9,10},{10,11},{12,13},{... | collective-permute-start | bytes 1572872 | tf_op jit(solution)/shard_map/ppermute | solution.py:183
  5.3 1.1 %select_bitcast_fusion = bf16[1,128,1024]{2,1,0:T(8,128)(2,1)S(1)} fusion(bf16[1,2,128,1024]{3,2,1,0:T(8,128)(2,1)} %param.5, pred[]{:T(512)S(6)} %eq.28), kind=kLoop, calls=%fused_computation.5 | loop fusion | flops 131072 | bytes 786433 | tf_op jit(solution)/shard_map/jit(_where)/select_n | solution.py:228
  6.4 0.7 collective-permute-start.5
  7.0 1.3 %collective-permute-start.8 = (bf16[2,128,1024]{2,1,0:T(8,128)(2,1)}, bf16[2,128,1024]{2,1,0:T(8,128)(2,1)S(1)}, u32[]{:S(2)}, u32[]{:S(2)}) collective-permute-start(bf16[2,128,1024]{2,1,0:T(8,128)(2,1)} %bitcast.21), channel_id=1, source_target_pairs={{0,4},{4,0},{8,12},{12,8},{16,20},{20,16},{24,28},{28,24},{1,5},{5... | collective-permute-start | bytes 1572872 | tf_op jit(solution)/shard_map/ppermute | solution.py:183
  8.3 3.0 %collective-permute-start.9 = (bf16[2,128,1024]{2,1,0:T(8,128)(2,1)}, bf16[2,128,1024]{2,1,0:T(8,128)(2,1)S(1)}, u32[]{:S(2)}, u32[]{:S(2)}) collective-permute-start(bf16[2,128,1024]{2,1,0:T(8,128)(2,1)} %bitcast.22), channel_id=1, source_target_pairs={{4,8},{8,4},{12,16},{16,12},{20,24},{24,20},{5,9},{9,5},{13,17},{1... | collective-permute-start | bytes 1572872 | tf_op jit(solution)/shard_map/ppermute | solution.py:183
  11.4 0.1 stack.76
  11.5 0.8 %convert_reduce_fusion = s32[2,18]{1,0:T(2,128)S(1)} fusion(s32[18]{0:T(128)S(1)} %stack.76, s32[2,8]{1,0:T(2,128)} %bitcast.24), kind=kLoop, calls=%fused_computation.6 | loop fusion | flops 828 | bytes 280 | tf_op jit(solution)/shard_map/reduce_sum | solution.py:188
  12.3 2.6 %collective-permute-done.refs_1_ = bf16[2,128,1024]{2,1,0:T(8,128)(2,1)S(1)} collective-permute-done((bf16[2,128,1024]{2,1,0:T(8,128)(2,1)}, bf16[2,128,1024]{2,1,0:T(8,128)(2,1)S(1)}, u32[]{:S(2)}, u32[]{:S(2)}) %collective-permute-start) | collective-permute-done | bytes 524320 | tf_op jit(solution)/shard_map/ppermute | solution.py:183
  14.9 2.2 %collective-permute-start.1 = (bf16[2,128,1024]{2,1,0:T(8,128)(2,1)S(1)}, bf16[2,128,1024]{2,1,0:T(8,128)(2,1)}, u32[]{:S(2)}, u32[]{:S(2)}) collective-permute-start(bf16[2,128,1024]{2,1,0:T(8,128)(2,1)S(1)} %collective-permute-done.refs_1_), channel_id=1, source_target_pairs={{2,1},{1,0},{6,5},{5,4},{10,9},{9,8},{14,13},{13,12},{18,17},{17,1... | collective-permute-start | bytes 1572872 | tf_op jit(solution)/shard_map/ppermute | solution.py:183
  17.1 0.0 collective-permute-done.2.refs_0_
  17.1 4.6 %collective-permute-start.3 = (bf16[2,128,1024]{2,1,0:T(8,128)(2,1)S(1)}, bf16[2,128,1024]{2,1,0:T(8,128)(2,1)}, u32[]{:S(2)}, u32[]{:S(2)}) collective-permute-start(bf16[2,128,1024]{2,1,0:T(8,128)(2,1)S(1)} %collective-permute-done.2.refs_0_), channel_id=1, source_target_pairs={{1,2},{2,3},{5,6},{6,7},{9,10},{10,11},{13,14},{14,15},{17,18},{18... | collective-permute-start | bytes 1572872 | tf_op jit(solution)/shard_map/ppermute | solution.py:183
  21.8 0.0 collective-permute-done.5.refs_0_
  21.8 0.8 %pad_maximum_fusion = bf16[2,128,1024]{2,1,0:T(8,128)(2,1)} fusion(bf16[1,128,1024]{2,1,0:T(8,128)(2,1)S(1)} %get-tuple-element.40, bf16[1,128,1024]{2,1,0:T(8,128)(2,1)S(1)} %get-tuple-element.39), kind=kLoop, calls=%fused_computation | loop fusion | flops 262144 | bytes 1048576 | tf_op jit(solution)/shard_map/concatenate | solution.py:237
  22.7 6.8 %collective-permute-start.6 = (bf16[2,128,1024]{2,1,0:T(8,128)(2,1)}, bf16[2,128,1024]{2,1,0:T(8,128)(2,1)S(1)}, u32[]{:S(2)}, u32[]{:S(2)}) collective-permute-start(bf16[2,128,1024]{2,1,0:T(8,128)(2,1)} %pad_maximum_fusion), channel_id=1, source_target_pairs={{0,4},{4,0},{8,12},{12,8},{16,20},{20,16},{24,28},{28,24},{1,5},{5... | collective-permute-start | bytes 1572872 | tf_op jit(solution)/shard_map/ppermute | solution.py:183
  29.4 0.0 collective-permute-done.8.refs_0_
  29.4 2.9 %collective-permute-start.7 = (bf16[2,128,1024]{2,1,0:T(8,128)(2,1)}, bf16[2,128,1024]{2,1,0:T(8,128)(2,1)S(1)}, u32[]{:S(2)}, u32[]{:S(2)}) collective-permute-start(bf16[2,128,1024]{2,1,0:T(8,128)(2,1)} %pad_maximum_fusion), channel_id=1, source_target_pairs={{4,8},{8,4},{12,16},{16,12},{20,24},{24,20},{5,9},{9,5},{13,17},{1... | collective-permute-start | bytes 1572872 | tf_op jit(solution)/shard_map/ppermute | solution.py:183
  32.4 0.1 stack.85
  32.5 0.7 %compare_select_fusion.2.bias_ref = f32[2,18]{1,0:T(2,128)S(1)} fusion(s32[2,18]{1,0:T(2,128)S(1)} %convert_reduce_fusion, pred[18]{0:T(512)(128)(4,1)} %constant.54.clone, s32[18]{0:T(128)S(1)} %stack.85, s32[18]{0:T(128)S(1)} %stack.76, s32[2]{0:T(128)S(1)} %iota_add_fusion), kind=kLoop, calls=%fused_computation.9 | loop fusion | flops 648 | bytes 458 | tf_op jit(solution)/shard_map/jit(_where)/select_n | solution.py:192
  33.2 0.0 copy-start
  33.2 2.8 %copy-done = bf16[1024,3072]{1,0:T(8,128)(2,1)S(1)} copy-done((bf16[1024,3072]{1,0:T(8,128)(2,1)S(1)}, bf16[1024,3072]{1,0:T(8,128)(2,1)}, u32[]{:S(2)}) %copy-start) | copy-done | bytes 6291480
  36.0 0.0 copy-start.3
  36.0 1.0 %copy-done.3 = bf16[1,2,128,1024]{3,2,1,0:T(8,128)(2,1)S(1)} copy-done((bf16[1,2,128,1024]{3,2,1,0:T(8,128)(2,1)S(1)}, bf16[1,2,128,1024]{3,2,1,0:T(8,128)(2,1)}, u32[]{:S(2)}) %copy-start.3) | copy-done | bytes 524312
  37.1 0.0 copy-start.1
  37.1 5.3 %own.1 = (bf16[256,1024]{1,0:T(8,128)(2,1)S(1)}, f32[256,1024]{1,0:T(8,128)S(1)}, f32[256,1024]{1,0:T(8,128)S(1)}, f32[256,1024]{1,0:T(8,128)S(1)}) custom-call(f32[2,18]{1,0:T(2,128)S(1)} %compare_select_fusion.2.bias_ref, bf16[2,128,1024]{2,1,0:T(8,128)(2,1)S(1)} %bitcast.23, bf16[1024,3072]{1,0:T(8,128)(2,1)S(1)} %copy-done), custom_call_target="tpu_custom_call" | custom-call | tf_op jit(solution)/shard_map/own/pallas_call | solution.py:145
  42.3 0.0 collective-permute-done.9.refs_1_
  42.4 0.0 copy-done.1
  42.4 6.1 %rim_own.1 = (f32[256,1024]{1,0:T(8,128)S(1)}, f32[256,1024]{1,0:T(8,128)S(1)}, f32[256,1024]{1,0:T(8,128)S(1)}) custom-call(f32[2,18]{1,0:T(2,128)S(1)} %compare_select_fusion.2.bias_ref, bf16[2,128,1024]{2,1,0:T(8,128)(2,1)S(1)} %collective-permute-done.8.refs_0_, ...), custom_call_target="tpu_custom_call", output_to_operand_aliasing={{0}: (5, {}), {1}: (6, {}), {2}: (7, {})} | custom-call | tf_op jit(solution)/shard_map/rim_own/pallas_call | solution.py:157
  48.5 6.3 %beside.1 = (f32[256,1024]{1,0:T(8,128)S(1)}, f32[256,1024]{1,0:T(8,128)S(1)}, f32[256,1024]{1,0:T(8,128)S(1)}) custom-call(f32[2,18]{1,0:T(2,128)S(1)} %compare_select_fusion.2.bias_ref, bf16[2,128,1024]{2,1,0:T(8,128)(2,1)S(1)} %collective-permute-done.2.refs_0_, ...), custom_call_target="tpu_custom_call", output_to_operand_aliasing={{0}: (5, {}), {1}: (6, {}), {2}: (7, {})} | custom-call | tf_op jit(solution)/shard_map/beside/pallas_call | solution.py:157
  54.7 0.0 collective-permute-done.1
  54.7 0.0 collective-permute-done.3
  54.7 1.1 %slice_select_fusion.2 = bf16[1,128,1024]{2,1,0:T(8,128)(2,1)S(1)} fusion(bf16[2,128,1024]{2,1,0:T(8,128)(2,1)} %collective-permute-done.3, bf16[2,128,1024]{2,1,0:T(8,128)(2,1)} %collective-permute-done.1, pred[]{:T(512)S(6)} %lt.15), kind=kLoop, calls=%fused_computation.4 | loop fusion | flops 131072 | bytes 786433 | tf_op jit(solution)/shard_map/jit(_where)/select_n | solution.py:242
  55.8 1.3 %collective-permute-start.4 = (bf16[1,128,1024]{2,1,0:T(8,128)(2,1)S(1)}, bf16[1,128,1024]{2,1,0:T(8,128)(2,1)S(1)}, u32[]{:S(2)}, u32[]{:S(2)}) collective-permute-start(bf16[1,128,1024]{2,1,0:T(8,128)(2,1)S(1)} %slice_select_fusion.2), channel_id=1, source_target_pairs={{1,0},{2,3},{5,4},{6,7},{9,8},{10,11},{13,12},{14,15},{17,16},{18,... | collective-permute-start | bytes 786440 | tf_op jit(solution)/shard_map/ppermute | solution.py:183
  57.1 0.0 collective-permute-done.6.refs_1_
  57.1 0.0 collective-permute-done.7.refs_2_
  57.1 6.3 %rim_edge.1 = (f32[256,1024]{1,0:T(8,128)S(1)}, f32[256,1024]{1,0:T(8,128)S(1)}, f32[256,1024]{1,0:T(8,128)S(1)}) custom-call(f32[2,18]{1,0:T(2,128)S(1)} %compare_select_fusion.2.bias_ref, bf16[1,128,1024]{2,1,0:T(8,128)(2,1)S(1)} %collective-permute-done.5.refs_0_, ...), custom_call_target="tpu_custom_call", output_to_operand_aliasing={{0}: (6, {}), {1}: (7, {}), {2}: (8, {})} | custom-call | tf_op jit(solution)/shard_map/rim_edge/pallas_call | solution.py:157
  63.4 0.0 copy-start.2
  63.4 1.3 %broadcast_select_fusion.refs_0_ = bf16[2,128,1024]{2,1,0:T(8,128)(2,1)S(1)} fusion(bf16[2,128,1024]{2,1,0:T(8,128)(2,1)} %collective-permute-done.1, bf16[2,128,1024]{2,1,0:T(8,128)(2,1)} %collective-permute-done.3, pred[]{:T(512)S(6)} %lt.15), kind=kLoop, calls=%fused_computation.1 | loop fusion | flops 262144 | bytes 1572865 | tf_op jit(solution)/shard_map/jit(_where)/select_n | solution.py:241
  64.7 3.9 %across.1 = (f32[256,1024]{1,0:T(8,128)S(1)}, f32[256,1024]{1,0:T(8,128)S(1)}, f32[256,1024]{1,0:T(8,128)S(1)}) custom-call(f32[2,18]{1,0:T(2,128)S(1)} %compare_select_fusion.2.bias_ref, bf16[2,128,1024]{2,1,0:T(8,128)(2,1)S(1)} %broadcast_select_fusion.refs_0_, ...), custom_call_target="tpu_custom_call", output_to_operand_aliasing={{0}: (4, {}), {1}: (5, {}), {2}: (6, {})} | custom-call | tf_op jit(solution)/shard_map/across/pallas_call | solution.py:157
  68.6 0.0 collective-permute-done.4.refs_0_
  68.6 0.0 copy-done.2
  68.6 5.5 %last.1 = (bf16[256,1024]{1,0:T(8,128)(2,1)}, f32[256,1024]{1,0:T(8,128)S(1)}, f32[256,1024]{1,0:T(8,128)S(1)}, f32[256,1024]{1,0:T(8,128)S(1)}) custom-call(f32[2,18]{1,0:T(2,128)S(1)} %compare_select_fusion.2.bias_ref, bf16[1,128,1024]{2,1,0:T(8,128)(2,1)S(1)} %collective-permute-done.4.refs_0_, ...), custom_call_target="tpu_custom_call", output_to_operand_aliasing={{1}: (5, {}), {2}: (6, {}), {3}: (7, {})} | custom-call | tf_op jit(solution)/shard_map/last/pallas_call | solution.py:169
  (5 shorter events, 0.1 us)
Async XLA Ops:
  0.0 14.9 %collective-permute-start = (bf16[2,128,1024]{2,1,0:T(8,128)(2,1)}, bf16[2,128,1024]{2,1,0:T(8,128)(2,1)S(1)}, u32[]{:S(2)}, u32[]{:S(2)}) collective-permute-start(bf16[2,128,1024]{2,1,0:T(8,128)(2,1)} %bitcast.19), channel_id=1, source_target_pairs={{1,0},{2,1},{3,2},{5,4},{6,5},{7,6},{9,8},{10,9},{11,10},{13,12},{... | collective-permute-start | bytes 1572872 | tf_op jit(solution)/shard_map/ppermute | solution.py:183
  1.9 15.2 %collective-permute-start.2 = (bf16[2,128,1024]{2,1,0:T(8,128)(2,1)}, bf16[2,128,1024]{2,1,0:T(8,128)(2,1)S(1)}, u32[]{:S(2)}, u32[]{:S(2)}) collective-permute-start(bf16[2,128,1024]{2,1,0:T(8,128)(2,1)} %bitcast.20), channel_id=1, source_target_pairs={{0,1},{1,2},{2,3},{4,5},{5,6},{6,7},{8,9},{9,10},{10,11},{12,13},{... | collective-permute-start | bytes 1572872 | tf_op jit(solution)/shard_map/ppermute | solution.py:183
  6.4 15.4 %collective-permute-start.5 = (bf16[1,128,1024]{2,1,0:T(8,128)(2,1)S(1)}, bf16[1,128,1024]{2,1,0:T(8,128)(2,1)S(1)}, u32[]{:S(2)}, u32[]{:S(2)}) collective-permute-start(bf16[1,128,1024]{2,1,0:T(8,128)(2,1)S(1)} %select_bitcast_fusion), channel_id=1, source_target_pairs={{0,3},{3,0},{4,7},{7,4},{8,11},{11,8},{12,15},{15,12},{16,19},{19,... | collective-permute-start | bytes 786440 | tf_op jit(solution)/shard_map/ppermute | solution.py:183
  7.0 22.4 %collective-permute-start.8 = (bf16[2,128,1024]{2,1,0:T(8,128)(2,1)}, bf16[2,128,1024]{2,1,0:T(8,128)(2,1)S(1)}, u32[]{:S(2)}, u32[]{:S(2)}) collective-permute-start(bf16[2,128,1024]{2,1,0:T(8,128)(2,1)} %bitcast.21), channel_id=1, source_target_pairs={{0,4},{4,0},{8,12},{12,8},{16,20},{20,16},{24,28},{28,24},{1,5},{5... | collective-permute-start | bytes 1572872 | tf_op jit(solution)/shard_map/ppermute | solution.py:183
  8.3 34.0 %collective-permute-start.9 = (bf16[2,128,1024]{2,1,0:T(8,128)(2,1)}, bf16[2,128,1024]{2,1,0:T(8,128)(2,1)S(1)}, u32[]{:S(2)}, u32[]{:S(2)}) collective-permute-start(bf16[2,128,1024]{2,1,0:T(8,128)(2,1)} %bitcast.22), channel_id=1, source_target_pairs={{4,8},{8,4},{12,16},{16,12},{20,24},{24,20},{5,9},{9,5},{13,17},{1... | collective-permute-start | bytes 1572872 | tf_op jit(solution)/shard_map/ppermute | solution.py:183
  14.9 39.8 %collective-permute-start.1 = (bf16[2,128,1024]{2,1,0:T(8,128)(2,1)S(1)}, bf16[2,128,1024]{2,1,0:T(8,128)(2,1)}, u32[]{:S(2)}, u32[]{:S(2)}) collective-permute-start(bf16[2,128,1024]{2,1,0:T(8,128)(2,1)S(1)} %collective-permute-done.refs_1_), channel_id=1, source_target_pairs={{2,1},{1,0},{6,5},{5,4},{10,9},{9,8},{14,13},{13,12},{18,17},{17,1... | collective-permute-start | bytes 1572872 | tf_op jit(solution)/shard_map/ppermute | solution.py:183
  17.1 37.6 %collective-permute-start.3 = (bf16[2,128,1024]{2,1,0:T(8,128)(2,1)S(1)}, bf16[2,128,1024]{2,1,0:T(8,128)(2,1)}, u32[]{:S(2)}, u32[]{:S(2)}) collective-permute-start(bf16[2,128,1024]{2,1,0:T(8,128)(2,1)S(1)} %collective-permute-done.2.refs_0_), channel_id=1, source_target_pairs={{1,2},{2,3},{5,6},{6,7},{9,10},{10,11},{13,14},{14,15},{17,18},{18... | collective-permute-start | bytes 1572872 | tf_op jit(solution)/shard_map/ppermute | solution.py:183
  22.7 34.5 %collective-permute-start.6 = (bf16[2,128,1024]{2,1,0:T(8,128)(2,1)}, bf16[2,128,1024]{2,1,0:T(8,128)(2,1)S(1)}, u32[]{:S(2)}, u32[]{:S(2)}) collective-permute-start(bf16[2,128,1024]{2,1,0:T(8,128)(2,1)} %pad_maximum_fusion), channel_id=1, source_target_pairs={{0,4},{4,0},{8,12},{12,8},{16,20},{20,16},{24,28},{28,24},{1,5},{5... | collective-permute-start | bytes 1572872 | tf_op jit(solution)/shard_map/ppermute | solution.py:183
  29.4 27.7 %collective-permute-start.7 = (bf16[2,128,1024]{2,1,0:T(8,128)(2,1)}, bf16[2,128,1024]{2,1,0:T(8,128)(2,1)S(1)}, u32[]{:S(2)}, u32[]{:S(2)}) collective-permute-start(bf16[2,128,1024]{2,1,0:T(8,128)(2,1)} %pad_maximum_fusion), channel_id=1, source_target_pairs={{4,8},{8,4},{12,16},{16,12},{20,24},{24,20},{5,9},{9,5},{13,17},{1... | collective-permute-start | bytes 1572872 | tf_op jit(solution)/shard_map/ppermute | solution.py:183
  33.2 2.8 %copy-start = (bf16[1024,3072]{1,0:T(8,128)(2,1)S(1)}, bf16[1024,3072]{1,0:T(8,128)(2,1)}, u32[]{:S(2)}) copy-start(bf16[1024,3072]{1,0:T(8,128)(2,1)} %refs_2_.3) | copy-start | bytes 18874372
  36.0 1.0 %copy-start.3 = (bf16[1,2,128,1024]{3,2,1,0:T(8,128)(2,1)S(1)}, bf16[1,2,128,1024]{3,2,1,0:T(8,128)(2,1)}, u32[]{:S(2)}) copy-start(bf16[1,2,128,1024]{3,2,1,0:T(8,128)(2,1)} %param.5) | copy-start | bytes 1572868
  37.1 5.3 %copy-start.1 = (bf16[1024,3072]{1,0:T(8,128)(2,1)S(1)}, bf16[1024,3072]{1,0:T(8,128)(2,1)}, u32[]{:S(2)}) copy-start(bf16[1024,3072]{1,0:T(8,128)(2,1)} %refs_2_.3) | copy-start | bytes 18874372
  55.8 12.8 %collective-permute-start.4 = (bf16[1,128,1024]{2,1,0:T(8,128)(2,1)S(1)}, bf16[1,128,1024]{2,1,0:T(8,128)(2,1)S(1)}, u32[]{:S(2)}, u32[]{:S(2)}) collective-permute-start(bf16[1,128,1024]{2,1,0:T(8,128)(2,1)S(1)} %slice_select_fusion.2), channel_id=1, source_target_pairs={{1,0},{2,3},{5,4},{6,7},{9,8},{10,11},{13,12},{14,15},{17,16},{18,... | collective-permute-start | bytes 786440 | tf_op jit(solution)/shard_map/ppermute | solution.py:183
  63.4 5.2 %copy-start.2 = (bf16[1024,1024]{1,0:T(8,128)(2,1)S(1)}, bf16[1024,1024]{1,0:T(8,128)(2,1)}, u32[]{:S(2)}) copy-start(bf16[1024,1024]{1,0:T(8,128)(2,1)} %refs_3_.5) | copy-start | bytes 6291460

commit v2 on v1

v2 whole, which is shorter than its diff:
```python
import functools
import math
import jax
import jax.numpy as jnp
from jax import lax
from jax.experimental import pallas as pl
from jax.experimental.pallas import tpu as pltpu
from jax.sharding import PartitionSpec as P

HD = 64
BLOCK = 128
PAIR = 2 * HD
NEG = -1e30
CW = 256
VM = 24
COST = 1_200_000_000
UNIT = 1.4426950408889634 * HD ** -0.5


def log_times(times):
    value = jnp.float32(NEG)
    for k in range(1, 12):
        value = jnp.where(times == k, jnp.float32(math.log(k) * HD ** 0.5), value)
    return value


def row_bias(tele_ref, own, total, column, t):
    told = jnp.int32(0)
    for k in range(tele_ref.shape[2]):
        told = told + (tele_ref[0, t, k] == column).astype(jnp.int32)
    beside = lax.rem(column - (own + t) + 1 + total, total) <= 2
    return log_times(told + beside.astype(jnp.int32))


def bias_lanes(value):
    lane = lax.broadcasted_iota(jnp.int32, (BLOCK, PAIR), 1)
    whole = jnp.full((BLOCK, PAIR), value, jnp.float32)
    hi = whole.astype(jnp.bfloat16).astype(jnp.float32)
    mid = (whole - hi).astype(jnp.bfloat16).astype(jnp.float32)
    low = whole - hi - mid
    picked = jnp.where(lane == 0, hi, jnp.where(lane == 1, mid, jnp.where(lane == 2, low, 0.0)))
    return picked.astype(jnp.bfloat16)


def update(q, keys, values, bias, users, o_ref, m_ref, l_ref, first):
    left = lax.broadcasted_iota(jnp.int32, (BLOCK, PAIR), 1) < HD
    one = jnp.ones((2 * BLOCK, PAIR), jnp.bfloat16)
    for t in range(2):
        tiles = users[t]
        if not tiles:
            continue
        rows = slice(t * BLOCK, (t + 1) * BLOCK)
        kb = jnp.concatenate([bias_lanes(bias[t][j]) for j in tiles], 0)
        for pr in range(CW // PAIR):
            cols = slice(pr * PAIR, (pr + 1) * PAIR)
            qp = q[rows, cols]
            zero = jnp.zeros_like(qp)
            qbd = jnp.concatenate([jnp.where(left, qp, zero), jnp.where(left, zero, qp)], 0)
            qbd = jnp.concatenate([qbd, one], 1)
            kp = jnp.concatenate([keys[j][:, cols] for j in tiles], 0)
            kp = jnp.concatenate([kp, kb], 1)
            s = lax.dot_general(qbd, kp, (((1,), (1,)), ((), ())), preferred_element_type=jnp.float32)
            m = jnp.max(s, axis=1, keepdims=True)
            p = jnp.exp2((s - m) * UNIT).astype(jnp.bfloat16)
            vp = jnp.concatenate([values[j][:, cols] for j in tiles], 0)
            vp = jnp.concatenate([vp, jnp.ones((len(tiles) * BLOCK, PAIR), jnp.bfloat16)], 1)
            r = jnp.dot(p, vp, preferred_element_type=jnp.float32)
            o = jnp.where(left, r[:BLOCK, :PAIR], r[BLOCK:, :PAIR])
            l = jnp.where(left, r[:BLOCK, PAIR:], r[BLOCK:, PAIR:])
            m = jnp.where(left, m[:BLOCK], m[BLOCK:])
            if not first:
                m_old = m_ref[rows, cols]
                peak = jnp.maximum(m, m_old)
                was = jnp.exp2((m_old - peak) * UNIT)
                now = jnp.exp2((m - peak) * UNIT)
                o = o_ref[rows, cols] * was + o * now
                l = l_ref[rows, cols] * was + l * now
                m = peak
            o_ref[rows, cols] = o
            l_ref[rows, cols] = l
            m_ref[rows, cols] = m


def project(xs, w, off):
    flat = jnp.concatenate(xs, 0)
    return jnp.dot(flat, w[:, pl.ds(off, CW)], preferred_element_type=jnp.float32).astype(jnp.bfloat16)


def split(a):
    return [a[i:i + BLOCK] for i in range(0, a.shape[0], BLOCK)]


def groups(width, body):
    if LOOP:
        lax.fori_loop(0, width // CW, lambda i, c: (body(pl.multiple_of(i * CW, CW)), c)[1], 0)
    else:
        for i in range(width // CW):
            body(i * CW)


LOOP = False


class Place:
    def __init__(self, tele_ref, n_lat, n_lon):
        self.tele_ref, self.n_lon = tele_ref, n_lon
        a, self.z = lax.axis_index("lat"), lax.axis_index("lon")
        self.first, self.last = self.z == 0, self.z == n_lon - 1
        self.other_ok = jnp.where(lax.rem(a, 2) == 0, a > 0, a < n_lat - 1)

    def row(self, column):
        return [row_bias(self.tele_ref, 2 * self.z, 2 * self.n_lon, column, t) for t in range(2)]

    def rim(self, same):
        value = jnp.float32(0.0) if same else jnp.where(self.other_ok, jnp.float32(0.0), jnp.float32(NEG))
        return [value, value]


def attend_kernel(gather, users, n_x, kind, place, tele_ref, *refs):
    x_refs, refs = refs[:n_x], refs[n_x:]
    at = Place(tele_ref, *place)
    xs, tiles_bias = gather(at, *x_refs)
    bias = [[both[t] for both in tiles_bias] for t in range(2)]
    width = xs[0].shape[-1]
    if kind == "first":
        w, q_ref, o_ref, m_ref, l_ref = refs
    elif kind == "last":
        q_ref, w, w_out, o_in, m_in, l_in, out_ref, o_ref, m_ref, l_ref, att = refs
    else:
        q_ref, w, o_in, m_in, l_in, o_ref, m_ref, l_ref = refs

    def body(off):
        here = pl.ds(off, CW)
        if kind == "first":
            q = project(xs[:2], w, off)
            q_ref[:, here] = q
        else:
            q = q_ref[:, here]
        keys, values = split(project(xs, w, width + off)), split(project(xs, w, 2 * width + off))
        update(q, keys, values, bias, users, o_ref.at[:, here], m_ref.at[:, here], l_ref.at[:, here], kind == "first")
        if kind == "last":
            att[:, here] = (o_ref[:, here] / l_ref[:, here]).astype(jnp.bfloat16)

    groups(width, body)
    if kind == "last":
        out_ref[...] = jnp.dot(att[...], w_out[...], preferred_element_type=jnp.float32).astype(jnp.bfloat16)


SMEM = pl.BlockSpec(memory_space=pltpu.SMEM)
VMEM = pl.BlockSpec(memory_space=pltpu.VMEM)


def state_shapes(width):
    return [jax.ShapeDtypeStruct((2 * BLOCK, width), jnp.float32)] * 3


def attend(gather, users, tiles, place, tele_ids, xs, w_qkv, name, q=None, state=None, w_out=None):
    kind = "first" if state is None else "step" if w_out is None else "last"
    width = xs[0].shape[-1]
    q_shape = jax.ShapeDtypeStruct((2 * BLOCK, width), jnp.bfloat16)
    out_shape = state_shapes(width)
    args = [tele_ids, *xs]
    aliases, scratch = {}, []
    if kind == "first":
        args += [w_qkv]
        out_shape = [q_shape] + out_shape
    else:
        args += [q, w_qkv] + ([w_out] if kind == "last" else []) + list(state)
        out_shape = ([q_shape] if kind == "last" else []) + out_shape
        aliases = {len(args) - 3 + k: len(out_shape) - 3 + k for k in range(3)}
        if kind == "last":
            scratch = [pltpu.VMEM((2 * BLOCK, width), jnp.bfloat16)]
    spent = tiles * COST
    return pl.pallas_call(
        functools.partial(attend_kernel, gather, users, len(xs), kind, place),
        in_specs=[SMEM] + [VMEM] * (len(args) - 1), out_specs=[VMEM] * len(out_shape), out_shape=out_shape,
        input_output_aliases=aliases, scratch_shapes=scratch, name=name,
        compiler_params=pltpu.CompilerParams(vmem_limit_bytes=VM * 1024 * 1024),
        cost_estimate=pl.CostEstimate(flops=spent, bytes_accessed=tiles * 500_000, transcendentals=0),
    )(*args)


def gate_kernel(count, *refs):
    del count, refs


def gate(arrays, after):
    count = len(arrays)
    return pl.pallas_call(
        functools.partial(gate_kernel, count),
        in_specs=[pl.BlockSpec(memory_space=pl.ANY)] * (count + len(after)),
        out_specs=[pl.BlockSpec(memory_space=pl.ANY)] * count,
        out_shape=[jax.ShapeDtypeStruct(v.shape, v.dtype) for v in arrays],
        input_output_aliases={k: k for k in range(count)}, name="gate",
        compiler_params=pltpu.CompilerParams(vmem_limit_bytes=1024 * 1024),
    )(*arrays, *after)


PAIRS = [[0, 1], [0, 1]]
BOTH = [[0, 1, 2, 3], [0, 1, 2, 3]]


def lat_swap(array, n_lat):
    same = [(i, i ^ 1) for i in range(n_lat)]
    other = [p for i in range(1, n_lat - 1, 2) for p in ((i, i + 1), (i + 1, i))]
    return lax.ppermute(array, "lat", same), lax.ppermute(array, "lat", other)


def own_alone(at, x):
    b = 2 * at.z
    return [x[0], x[1]], [at.row(b), at.row(b + 1)]


def lon_step(at, which):
    step = jnp.where(lax.rem(at.z, 2) == which, 1, -1)
    b = 2 * lax.rem(at.z + step + at.n_lon, at.n_lon)
    return [at.row(b), at.row(b + 1)]


def near_tiles(at, near, ring, same, other):
    return ([near[0], near[1], ring[0], ring[1], same[0], same[1], other[0], other[1]],
            lon_step(at, 0) + lon_step(at, 1) + [at.rim(True)] * 2 + [at.rim(False)] * 2)


def corner_tiles(at, same, other):
    return [same[0], other[0], same[1], other[1]], [at.rim(True), at.rim(False)] * 2


def across_tiles(at, far):
    b = lax.rem(2 * at.z + 4, 8)
    return [far[0], far[1]], [at.row(b), at.row(b + 1)]


def rim_tiles(at, same, other, same_edges, other_edges):
    return ([same[0], same[1], other[0], other[1], same_edges[0], same_edges[1], other_edges[0], other_edges[1]],
            [at.rim(True)] * 2 + [at.rim(False)] * 2 + [at.rim(True)] * 2 + [at.rim(False)] * 2)


def column_tiles(start, at, row):
    found = []
    for j in range(row.shape[0]):
        own = (start + j >= 2 * at.z) & (start + j <= 2 * at.z + 1)
        found.append([jnp.where(own, jnp.float32(NEG), v) for v in at.row(jnp.int32(start + j))])
    return [row[j] for j in range(row.shape[0])], found


def on_device(tokens, w_qkv, w_out, tele_ids):
    n_lat, n_lon = lax.axis_size("lat"), lax.axis_size("lon")
    place = (n_lat, n_lon)
    z = lax.axis_index("lon")
    x = tokens[0]
    if n_lon == 4:
        near_pairs = [(i, i ^ 1) for i in range(4)]
        same, other = lat_swap(x, n_lat)
        ring = lax.ppermute(x, "lon", [(0, 3), (3, 0), (1, 2), (2, 1)])
        near = lax.ppermute(x, "lon", near_pairs)
        q, *state = attend(own_alone, PAIRS, 3, place, tele_ids, [x], w_qkv, "own")
        near, ring, same, other = gate([near, ring, same, other], [state[0]])
        even = lax.rem(z, 2) == 0
        edges = jnp.concatenate([jnp.where(even, ring[1:], near[1:]), jnp.where(even, near[:1], ring[:1])], 0)
        same_edges, other_edges = lat_swap(edges, n_lat)
        far = lax.ppermute(ring, "lon", near_pairs)
        state = attend(near_tiles, [list(range(8))] * 2, 8, place, tele_ids, [near, ring, same, other], w_qkv, "near", q, state)
        state = attend(corner_tiles, [[0, 1], [2, 3]], 4, place, tele_ids,
                       [same_edges, other_edges], w_qkv, "corner", q, state)
        mixed = attend(across_tiles, PAIRS, 3, place, tele_ids, [far], w_qkv, "across", q, state, w_out)[0]
    else:
        q, *state = attend(own_alone, PAIRS, 2, place, tele_ids, [x], w_qkv, "own")
        same, other = lat_swap(x, n_lat)
        before = lax.ppermute(x[1:], "lon", [(i, (i + 1) % n_lon) for i in range(n_lon)])
        after = lax.ppermute(x[:1], "lon", [((i + 1) % n_lon, i) for i in range(n_lon)])
        same_edges, other_edges = lat_swap(jnp.concatenate([before, after], 0), n_lat)
        state = attend(rim_tiles, [[0, 1, 2, 3, 4, 6], [0, 1, 2, 3, 5, 7]], 8, place, tele_ids,
                       [same, other, same_edges, other_edges], w_qkv, "rim", q, state)
        row = lax.all_gather(x, "lon", axis=0, tiled=True)
        for s in range(0, 2 * n_lon, 4):
            state = attend(functools.partial(column_tiles, s), BOTH, 4, place, tele_ids, [row[s:s + 4]], w_qkv,
                           "columns", q, state, w_out if s + 4 == 2 * n_lon else None)
        mixed = state[0]
    return mixed.reshape(tokens.shape)


def solution(mesh):
    return jax.shard_map(
        on_device,
        mesh=mesh,
        in_specs=(P("lat", "lon", None, None), P(), P(), P("lat", "lon", None)),
        out_specs=P("lat", "lon", None, None),
        check_vma=False,
    )
```

time: 74.6 us -> 55.3 us (0.74)
  the two profiles are of different devices: /device:TPU:9 before, /device:TPU:1 now
where the time goes in v2:
time: 55.3 us; the launch traced here: 55.1 us
  Pallas kernels  26.1 us (47%)
  starting transfers between devices  13.8 us (25%)
  waiting for transfers between devices  10.4 us (19%)
  local copies, waits for them, and re-layouts  4.5 us (8%)
    pallas_call x4, Pallas kernels, attend(): pl.pallas_call(functools.partial(attend_kernel, gather, users, len(xs), k...  26.1 us
    ppermute x4, starting transfers between devices, lat_swap(): return (lax.ppermute(array, 'lat', same), lax.ppermute(array, 'lat', other))  9.1 us
    ppermute x1, waiting for transfers between devices, on_device(): ring = lax.ppermute(x, 'lon', [(0, 3), (3, 0), (1, 2), (2, 1)])  8.8 us
    unnamed x10, local copies, waits for them, and re-layouts  4.5 us
    ppermute x1, starting transfers between devices, on_device(): ring = lax.ppermute(x, 'lon', [(0, 3), (3, 0), (1, 2), (2, 1)])  2.19 us
    ppermute x1, starting transfers between devices, on_device(): near = lax.ppermute(x, 'lon', near_pairs)  2.13 us
    ppermute x4, waiting for transfers between devices, lat_swap(): return (lax.ppermute(array, 'lat', same), lax.ppermute(array, 'lat', other))  1.64 us
  transfers between devices with their start and end apart: 7, of which 2 were waited for; matrix products, arithmetic and copies ran while one was open for 0% of the time, Pallas kernels for 38%

profile of v2, /device:TPU:1, one launch (start us, length us, event | category | flops | bytes accessed | tf_op | source)
XLA Modules:
  0.0 55.1 jit_solution(15784078126007676906)
XLA Ops:
  0.0 2.1 %collective-permute-start = (bf16[2,128,1024]{2,1,0:T(8,128)(2,1)}, bf16[2,128,1024]{2,1,0:T(8,128)(2,1)S(1)}, u32[]{:S(2)}, u32[]{:S(2)}) collective-permute-start(bf16[2,128,1024]{2,1,0:T(8,128)(2,1)} %bitcast.2), channel_id=1, source_target_pairs={{0,1},{1,0},{2,3},{3,2},{4,5},{5,4},{6,7},{7,6},{8,9},{9,8},{10,11... | collective-permute-start | bytes 1572872 | tf_op jit(solution)/shard_map/ppermute | solution.py:256
  2.1 2.2 %collective-permute-start.1 = (bf16[2,128,1024]{2,1,0:T(8,128)(2,1)}, bf16[2,128,1024]{2,1,0:T(8,128)(2,1)S(1)}, u32[]{:S(2)}, u32[]{:S(2)}) collective-permute-start(bf16[2,128,1024]{2,1,0:T(8,128)(2,1)} %bitcast.3), channel_id=1, source_target_pairs={{0,3},{3,0},{1,2},{2,1},{4,7},{7,4},{5,6},{6,5},{8,11},{11,8},{9,1... | collective-permute-start | bytes 1572872 | tf_op jit(solution)/shard_map/ppermute | solution.py:255
  4.3 1.2 %collective-permute-start.2 = (bf16[2,128,1024]{2,1,0:T(8,128)(2,1)}, bf16[2,128,1024]{2,1,0:T(8,128)(2,1)S(1)}, u32[]{:S(2)}, u32[]{:S(2)}) collective-permute-start(bf16[2,128,1024]{2,1,0:T(8,128)(2,1)} %bitcast.4), channel_id=1, source_target_pairs={{0,4},{4,0},{8,12},{12,8},{16,20},{20,16},{24,28},{28,24},{1,5},{5... | collective-permute-start | bytes 1572872 | tf_op jit(solution)/shard_map/ppermute | solution.py:206
  5.6 3.0 %collective-permute-start.3 = (bf16[2,128,1024]{2,1,0:T(8,128)(2,1)}, bf16[2,128,1024]{2,1,0:T(8,128)(2,1)S(1)}, u32[]{:S(2)}, u32[]{:S(2)}) collective-permute-start(bf16[2,128,1024]{2,1,0:T(8,128)(2,1)} %bitcast.5), channel_id=1, source_target_pairs={{4,8},{8,4},{12,16},{16,12},{20,24},{24,20},{5,9},{9,5},{13,17},{1... | collective-permute-start | bytes 1572872 | tf_op jit(solution)/shard_map/ppermute | solution.py:206
  8.6 0.0 copy-start
  8.6 2.8 %copy-done = bf16[1024,3072]{1,0:T(8,128)(2,1)S(1)} copy-done((bf16[1024,3072]{1,0:T(8,128)(2,1)S(1)}, bf16[1024,3072]{1,0:T(8,128)(2,1)}, u32[]{:S(2)}) %copy-start) | copy-done | bytes 6291480
  11.4 0.0 copy-start.3
  11.4 1.0 %copy-done.3 = bf16[1,2,128,1024]{3,2,1,0:T(8,128)(2,1)S(1)} copy-done((bf16[1,2,128,1024]{3,2,1,0:T(8,128)(2,1)S(1)}, bf16[1,2,128,1024]{3,2,1,0:T(8,128)(2,1)}, u32[]{:S(2)}) %copy-start.3) | copy-done | bytes 524312
  12.4 0.0 copy-start.4
  12.4 0.7 %copy-done.4 = s32[1,2,8]{2,1,0:T(2,128)S(1)} copy-done((s32[1,2,8]{2,1,0:T(2,128)S(1)}, s32[1,2,8]{2,1,0:T(2,128)}, u32[]{:S(2)}) %copy-start.4) | copy-done | bytes 88
  13.1 0.0 copy-start.1
  13.1 5.2 %own.1 = (bf16[256,1024]{1,0:T(8,128)(2,1)S(1)}, f32[256,1024]{1,0:T(8,128)S(1)}, f32[256,1024]{1,0:T(8,128)S(1)}, f32[256,1024]{1,0:T(8,128)S(1)}) custom-call(s32[1,2,8]{2,1,0:T(2,128)S(1)} %copy-done.4, bf16[2,128,1024]{2,1,0:T(8,128)(2,1)S(1)} %bitcast.6, bf16[1024,3072]{1,0:T(8,128)(2,1)S(1)} %copy-done), custom_call_target="tpu_custom_call" | custom-call | flops 3600000000 | bytes 1500000 | tf_op jit(solution)/shard_map/own/pallas_call | solution.py:174
  18.3 0.0 collective-permute-done.refs_0_
  18.3 8.8 %collective-permute-done.1.refs_1_ = bf16[2,128,1024]{2,1,0:T(8,128)(2,1)S(1)} collective-permute-done((bf16[2,128,1024]{2,1,0:T(8,128)(2,1)}, bf16[2,128,1024]{2,1,0:T(8,128)(2,1)S(1)}, u32[]{:S(2)}, u32[]{:S(2)}) %collective-permute-start.1) | collective-permute-done | bytes 524320 | tf_op jit(solution)/shard_map/ppermute | solution.py:255
  27.1 0.0 collective-permute-done.2.refs_2_
  27.1 0.0 collective-permute-done.3.refs_3_
  27.1 0.1 slice_select_fusion.1
  27.2 0.1 pad_maximum_fusion
  27.3 1.7 %collective-permute-start.5 = (bf16[2,128,1024]{2,1,0:T(8,128)(2,1)S(1)}, bf16[2,128,1024]{2,1,0:T(8,128)(2,1)S(1)}, u32[]{:S(2)}, u32[]{:S(2)}) collective-permute-start(bf16[2,128,1024]{2,1,0:T(8,128)(2,1)S(1)} %pad_maximum_fusion), channel_id=1, source_target_pairs={{0,4},{4,0},{8,12},{12,8},{16,20},{20,16},{24,28},{28,24},{1,5},{5... | collective-permute-start | bytes 1572872 | tf_op jit(solution)/shard_map/ppermute | solution.py:206
  28.9 3.2 %collective-permute-start.6 = (bf16[2,128,1024]{2,1,0:T(8,128)(2,1)S(1)}, bf16[2,128,1024]{2,1,0:T(8,128)(2,1)S(1)}, u32[]{:S(2)}, u32[]{:S(2)}) collective-permute-start(bf16[2,128,1024]{2,1,0:T(8,128)(2,1)S(1)} %pad_maximum_fusion), channel_id=1, source_target_pairs={{4,8},{8,4},{12,16},{16,12},{20,24},{24,20},{5,9},{9,5},{13,17},{1... | collective-permute-start | bytes 1572872 | tf_op jit(solution)/shard_map/ppermute | solution.py:206
  32.1 0.4 collective-permute-start.4
  32.5 0.0 copy-done.1
  32.5 10.6 %near.1 = (f32[256,1024]{1,0:T(8,128)S(1)}, f32[256,1024]{1,0:T(8,128)S(1)}, f32[256,1024]{1,0:T(8,128)S(1)}) custom-call(s32[1,2,8]{2,1,0:T(2,128)S(1)} %copy-done.4, bf16[2,128,1024]{2,1,0:T(8,128)(2,1)S(1)} %get-tuple-element.23.refs_0_, ...), custom_call_target="tpu_custom_call", output_to_operand_aliasing={{0}: (7, {}), {1}: (8, {}), {2}: (9, {})} | custom-call | flops 9600000000 | bytes 4000000 | tf_op jit(solution)/shard_map/near/pallas_call | solution.py:174
  43.1 0.0 collective-permute-done.5.refs_0_
  43.1 1.6 %collective-permute-done.6.refs_1_ = bf16[2,128,1024]{2,1,0:T(8,128)(2,1)S(1)} collective-permute-done((bf16[2,128,1024]{2,1,0:T(8,128)(2,1)S(1)}, bf16[2,128,1024]{2,1,0:T(8,128)(2,1)S(1)}, u32[]{:S(2)}, u32[]{:S(2)}) %collective-permute-start.6) | collective-permute-done | bytes 524320 | tf_op jit(solution)/shard_map/ppermute | solution.py:206
  44.8 0.0 copy-start.2
  44.8 4.9 %corner.1 = (f32[256,1024]{1,0:T(8,128)S(1)}, f32[256,1024]{1,0:T(8,128)S(1)}, f32[256,1024]{1,0:T(8,128)S(1)}) custom-call(s32[1,2,8]{2,1,0:T(2,128)S(1)} %copy-done.4, bf16[2,128,1024]{2,1,0:T(8,128)(2,1)S(1)} %collective-permute-done.5.refs_0_, ...), custom_call_target="tpu_custom_call", output_to_operand_aliasing={{0}: (5, {}), {1}: (6, {}), {2}: (7, {})} | custom-call | flops 4800000000 | bytes 2000000 | tf_op jit(solution)/shard_map/corner/pallas_call | solution.py:174
  49.7 0.0 collective-permute-done.4.refs_0_
  49.7 0.0 copy-done.2
  49.7 5.4 %across.1 = (bf16[256,1024]{1,0:T(8,128)(2,1)}, f32[256,1024]{1,0:T(8,128)S(1)}, f32[256,1024]{1,0:T(8,128)S(1)}, f32[256,1024]{1,0:T(8,128)S(1)}) custom-call(s32[1,2,8]{2,1,0:T(2,128)S(1)} %copy-done.4, bf16[2,128,1024]{2,1,0:T(8,128)(2,1)S(1)} %collective-permute-done.4.refs_0_, ...), custom_call_target="tpu_custom_call", output_to_operand_aliasing={{1}: (5, {}), {2}: (6, {}), {3}: (7, {})} | custom-call | flops 3600000000 | bytes 1500000 | tf_op jit(solution)/shard_map/across/pallas_call | solution.py:174
  (1 shorter events, 0.0 us)
Async XLA Ops:
  0.0 18.3 %collective-permute-start = (bf16[2,128,1024]{2,1,0:T(8,128)(2,1)}, bf16[2,128,1024]{2,1,0:T(8,128)(2,1)S(1)}, u32[]{:S(2)}, u32[]{:S(2)}) collective-permute-start(bf16[2,128,1024]{2,1,0:T(8,128)(2,1)} %bitcast.2), channel_id=1, source_target_pairs={{0,1},{1,0},{2,3},{3,2},{4,5},{5,4},{6,7},{7,6},{8,9},{9,8},{10,11... | collective-permute-start | bytes 1572872 | tf_op jit(solution)/shard_map/ppermute | solution.py:256
  2.1 25.0 %collective-permute-start.1 = (bf16[2,128,1024]{2,1,0:T(8,128)(2,1)}, bf16[2,128,1024]{2,1,0:T(8,128)(2,1)S(1)}, u32[]{:S(2)}, u32[]{:S(2)}) collective-permute-start(bf16[2,128,1024]{2,1,0:T(8,128)(2,1)} %bitcast.3), channel_id=1, source_target_pairs={{0,3},{3,0},{1,2},{2,1},{4,7},{7,4},{5,6},{6,5},{8,11},{11,8},{9,1... | collective-permute-start | bytes 1572872 | tf_op jit(solution)/shard_map/ppermute | solution.py:255
  4.3 22.8 %collective-permute-start.2 = (bf16[2,128,1024]{2,1,0:T(8,128)(2,1)}, bf16[2,128,1024]{2,1,0:T(8,128)(2,1)S(1)}, u32[]{:S(2)}, u32[]{:S(2)}) collective-permute-start(bf16[2,128,1024]{2,1,0:T(8,128)(2,1)} %bitcast.4), channel_id=1, source_target_pairs={{0,4},{4,0},{8,12},{12,8},{16,20},{20,16},{24,28},{28,24},{1,5},{5... | collective-permute-start | bytes 1572872 | tf_op jit(solution)/shard_map/ppermute | solution.py:206
  5.6 21.6 %collective-permute-start.3 = (bf16[2,128,1024]{2,1,0:T(8,128)(2,1)}, bf16[2,128,1024]{2,1,0:T(8,128)(2,1)S(1)}, u32[]{:S(2)}, u32[]{:S(2)}) collective-permute-start(bf16[2,128,1024]{2,1,0:T(8,128)(2,1)} %bitcast.5), channel_id=1, source_target_pairs={{4,8},{8,4},{12,16},{16,12},{20,24},{24,20},{5,9},{9,5},{13,17},{1... | collective-permute-start | bytes 1572872 | tf_op jit(solution)/shard_map/ppermute | solution.py:206
  8.6 2.8 %copy-start = (bf16[1024,3072]{1,0:T(8,128)(2,1)S(1)}, bf16[1024,3072]{1,0:T(8,128)(2,1)}, u32[]{:S(2)}) copy-start(bf16[1024,3072]{1,0:T(8,128)(2,1)} %refs_2_.1) | copy-start | bytes 18874372
  11.4 1.0 %copy-start.3 = (bf16[1,2,128,1024]{3,2,1,0:T(8,128)(2,1)S(1)}, bf16[1,2,128,1024]{3,2,1,0:T(8,128)(2,1)}, u32[]{:S(2)}) copy-start(bf16[1,2,128,1024]{3,2,1,0:T(8,128)(2,1)} %param.4) | copy-start | bytes 1572868
  12.4 0.7 %copy-start.4 = (s32[1,2,8]{2,1,0:T(2,128)S(1)}, s32[1,2,8]{2,1,0:T(2,128)}, u32[]{:S(2)}) copy-start(s32[1,2,8]{2,1,0:T(2,128)} %tele_ref.7) | copy-start | bytes 196
  13.1 19.5 %copy-start.1 = (bf16[1024,3072]{1,0:T(8,128)(2,1)S(1)}, bf16[1024,3072]{1,0:T(8,128)(2,1)}, u32[]{:S(2)}) copy-start(bf16[1024,3072]{1,0:T(8,128)(2,1)} %refs_2_.1) | copy-start | bytes 18874372
  27.3 15.8 %collective-permute-start.5 = (bf16[2,128,1024]{2,1,0:T(8,128)(2,1)S(1)}, bf16[2,128,1024]{2,1,0:T(8,128)(2,1)S(1)}, u32[]{:S(2)}, u32[]{:S(2)}) collective-permute-start(bf16[2,128,1024]{2,1,0:T(8,128)(2,1)S(1)} %pad_maximum_fusion), channel_id=1, source_target_pairs={{0,4},{4,0},{8,12},{12,8},{16,20},{20,16},{24,28},{28,24},{1,5},{5... | collective-permute-start | bytes 1572872 | tf_op jit(solution)/shard_map/ppermute | solution.py:206
  28.9 15.8 %collective-permute-start.6 = (bf16[2,128,1024]{2,1,0:T(8,128)(2,1)S(1)}, bf16[2,128,1024]{2,1,0:T(8,128)(2,1)S(1)}, u32[]{:S(2)}, u32[]{:S(2)}) collective-permute-start(bf16[2,128,1024]{2,1,0:T(8,128)(2,1)S(1)} %pad_maximum_fusion), channel_id=1, source_target_pairs={{4,8},{8,4},{12,16},{16,12},{20,24},{24,20},{5,9},{9,5},{13,17},{1... | collective-permute-start | bytes 1572872 | tf_op jit(solution)/shard_map/ppermute | solution.py:206
  32.1 17.5 %collective-permute-start.4 = (bf16[2,128,1024]{2,1,0:T(8,128)(2,1)S(1)}, bf16[2,128,1024]{2,1,0:T(8,128)(2,1)S(1)}, u32[]{:S(2)}, u32[]{:S(2)}) collective-permute-start(bf16[2,128,1024]{2,1,0:T(8,128)(2,1)S(1)} %get-tuple-element.21.refs_1_), channel_id=1, source_target_pairs={{0,1},{1,0},{2,3},{3,2},{4,5},{5,4},{6,7},{7,6},{8,9},{9,8},{10,11... | collective-permute-start | bytes 1572872 | tf_op jit(solution)/shard_map/ppermute | solution.py:262
  44.8 4.9 %copy-start.2 = (bf16[1024,1024]{1,0:T(8,128)(2,1)S(1)}, bf16[1024,1024]{1,0:T(8,128)(2,1)}, u32[]{:S(2)}) copy-start(bf16[1024,1024]{1,0:T(8,128)(2,1)} %refs_3_.3) | copy-start | bytes 6291460

commit v3 on v2

--- a/solution.py
+++ b/solution.py
@@ -13,7 +13,7 @@
 NEG = -1e30
 CW = 256
 VM = 24
-COST = 1_200_000_000
+COST = 0
 UNIT = 1.4426950408889634 * HD ** -0.5
 
 
@@ -32,53 +32,69 @@
     return log_times(told + beside.astype(jnp.int32))
 
 
-def bias_lanes(value):
+def bias_lanes(values):
     lane = lax.broadcasted_iota(jnp.int32, (BLOCK, PAIR), 1)
-    whole = jnp.full((BLOCK, PAIR), value, jnp.float32)
-    hi = whole.astype(jnp.bfloat16).astype(jnp.float32)
-    mid = (whole - hi).astype(jnp.bfloat16).astype(jnp.float32)
-    low = whole - hi - mid
-    picked = jnp.where(lane == 0, hi, jnp.where(lane == 1, mid, jnp.where(lane == 2, low, 0.0)))
+    picked = jnp.zeros((BLOCK, PAIR), jnp.float32)
+    for t, value in enumerate(values):
+        whole = jnp.full((BLOCK, PAIR), value, jnp.float32)
+        hi = whole.astype(jnp.bfloat16).astype(jnp.float32)
+        mid = (whole - hi).astype(jnp.bfloat16).astype(jnp.float32)
+        for k, part in enumerate((hi, mid, whole - hi - mid)):
+            picked = jnp.where(lane == 3 * t + k, part, picked)
     return picked.astype(jnp.bfloat16)
 
 
+def stacked(parts):
+    return parts[0] if len(parts) == 1 else jnp.concatenate(parts, 0)
+
+
 def update(q, keys, values, bias, users, o_ref, m_ref, l_ref, first):
-    left = lax.broadcasted_iota(jnp.int32, (BLOCK, PAIR), 1) < HD
-    one = jnp.ones((2 * BLOCK, PAIR), jnp.bfloat16)
-    for t in range(2):
-        tiles = users[t]
-        if not tiles:
-            continue
-        rows = slice(t * BLOCK, (t + 1) * BLOCK)
-        kb = jnp.concatenate([bias_lanes(bias[t][j]) for j in tiles], 0)
-        for pr in range(CW // PAIR):
-            cols = slice(pr * PAIR, (pr + 1) * PAIR)
-            qp = q[rows, cols]
+    if users[0] == users[1]:
+        update_some(q, keys, values, bias, users, o_ref, m_ref, l_ref, first, (0, 1))
+    else:
+        for t in range(2):
+            update_some(q, keys, values, bias, users, o_ref, m_ref, l_ref, first, (t,))
+
+
+def update_some(q, keys, values, bias, users, o_ref, m_ref, l_ref, first, which):
+    lane = lax.broadcasted_iota(jnp.int32, (BLOCK, PAIR), 1)
+    left = lane < HD
+    picks = [((lane >= 3 * t) & (lane < 3 * t + 3)).astype(jnp.float32).astype(jnp.bfloat16) for t in range(2)]
+    tiles = users[which[0]]
+    lanes = [bias_lanes([bias[t][j] for t in range(2)]) for j in tiles]
+    rows = [slice(t * BLOCK, (t + 1) * BLOCK) for t in range(2)]
+    two = 2 * BLOCK
+    for pr in range(CW // PAIR):
+        cols = slice(pr * PAIR, (pr + 1) * PAIR)
+        wide = []
+        for t in which:
+            qp = q[rows[t], cols]
             zero = jnp.zeros_like(qp)
-            qbd = jnp.concatenate([jnp.where(left, qp, zero), jnp.where(left, zero, qp)], 0)
-            qbd = jnp.concatenate([qbd, one], 1)
-            kp = jnp.concatenate([keys[j][:, cols] for j in tiles], 0)
-            kp = jnp.concatenate([kp, kb], 1)
-            s = lax.dot_general(qbd, kp, (((1,), (1,)), ((), ())), preferred_element_type=jnp.float32)
-            m = jnp.max(s, axis=1, keepdims=True)
-            p = jnp.exp2((s - m) * UNIT).astype(jnp.bfloat16)
-            vp = jnp.concatenate([values[j][:, cols] for j in tiles], 0)
-            vp = jnp.concatenate([vp, jnp.ones((len(tiles) * BLOCK, PAIR), jnp.bfloat16)], 1)
-            r = jnp.dot(p, vp, preferred_element_type=jnp.float32)
+            both = jnp.concatenate([jnp.where(left, qp, zero), jnp.where(left, zero, qp)], 0)
+            wide.append(jnp.concatenate([both, jnp.concatenate([picks[t], picks[t]], 0)], 1))
+        kp = stacked([jnp.concatenate([keys[j][:, cols], b], 1) for j, b in zip(tiles, lanes)])
+        s = lax.dot_general(stacked(wide), kp, (((1,), (1,)), ((), ())), preferred_element_type=jnp.float32)
+        peaks = jnp.max(s, axis=1, keepdims=True)
+        p = jnp.exp2((s - peaks) * UNIT).astype(jnp.bfloat16)
+        vp = stacked([values[j][:, cols] for j in tiles])
+        vp = jnp.concatenate([vp, jnp.ones((len(tiles) * BLOCK, PAIR), jnp.bfloat16)], 1)
+        sums = jnp.dot(p, vp, preferred_element_type=jnp.float32)
+        for i, t in enumerate(which):
+            r, m = sums[i * two:(i + 1) * two], peaks[i * two:(i + 1) * two]
             o = jnp.where(left, r[:BLOCK, :PAIR], r[BLOCK:, :PAIR])
             l = jnp.where(left, r[:BLOCK, PAIR:], r[BLOCK:, PAIR:])
             m = jnp.where(left, m[:BLOCK], m[BLOCK:])
             if not first:
-                m_old = m_ref[rows, cols]
+                m_old = m_ref[rows[t], cols]
                 peak = jnp.maximum(m, m_old)
                 was = jnp.exp2((m_old - peak) * UNIT)
                 now = jnp.exp2((m - peak) * UNIT)
-                o = o_ref[rows, cols] * was + o * now
-                l = l_ref[rows, cols] * was + l * now
+                o = o_ref[rows[t], cols] * was + o * now
+                l = l_ref[rows[t], cols] * was + l * now
                 m = peak
-            o_ref[rows, cols] = o
-            l_ref[rows, cols] = l
-            m_ref[rows, cols] = m
+            o_ref[rows[t], cols] = o
+            l_ref[rows[t], cols] = l
+            m_ref[rows[t], cols] = m
 
 
 def project(xs, w, off):
@@ -123,7 +139,8 @@
     bias = [[both[t] for both in tiles_bias] for t in range(2)]
     width = xs[0].shape[-1]
     if kind == "first":
-        w, q_ref, o_ref, m_ref, l_ref = refs
+        w, q_ref, rest_ref, o_ref, m_ref, l_ref = refs
+        rest_ref[0] = jnp.where(lax.rem(at.z, 2) == 0, x_refs[0][1], x_refs[0][0])
     elif kind == "last":
         q_ref, w, w_out, o_in, m_in, l_in, out_ref, o_ref, m_ref, l_ref, att = refs
     else:
@@ -163,7 +180,7 @@
     aliases, scratch = {}, []
     if kind == "first":
         args += [w_qkv]
-        out_shape = [q_shape] + out_shape
+        out_shape = [q_shape, jax.ShapeDtypeStruct((1,) + xs[0].shape[1:], xs[0].dtype)] + out_shape
     else:
         args += [q, w_qkv] + ([w_out] if kind == "last" else []) + list(state)
         out_shape = ([q_shape] if kind == "last" else []) + out_shape
@@ -176,7 +193,7 @@
         in_specs=[SMEM] + [VMEM] * (len(args) - 1), out_specs=[VMEM] * len(out_shape), out_shape=out_shape,
         input_output_aliases=aliases, scratch_shapes=scratch, name=name,
         compiler_params=pltpu.CompilerParams(vmem_limit_bytes=VM * 1024 * 1024),
-        cost_estimate=pl.CostEstimate(flops=spent, bytes_accessed=tiles * 500_000, transcendentals=0),
+        cost_estimate=pl.CostEstimate(flops=spent, bytes_accessed=0, transcendentals=0),
     )(*args)
 
 
@@ -211,29 +228,26 @@
     return [x[0], x[1]], [at.row(b), at.row(b + 1)]
 
 
-def lon_step(at, which):
-    step = jnp.where(lax.rem(at.z, 2) == which, 1, -1)
-    b = 2 * lax.rem(at.z + step + at.n_lon, at.n_lon)
-    return [at.row(b), at.row(b + 1)]
-
-
-def near_tiles(at, near, ring, same, other):
-    return ([near[0], near[1], ring[0], ring[1], same[0], same[1], other[0], other[1]],
-            lon_step(at, 0) + lon_step(at, 1) + [at.rim(True)] * 2 + [at.rim(False)] * 2)
+def lon_tiles(at, near, ring_edge, ring_rest):
+    odd = lax.rem(at.z, 2)
+    b = 2 * (at.z + 1 - 2 * odd)
+    c = 2 * lax.rem(at.z - 1 + 2 * odd + at.n_lon, at.n_lon)
+    return ([near[0], near[1], ring_edge[0], ring_rest[0]],
+            [at.row(b), at.row(b + 1), at.row(c + 1 - odd), at.row(c + odd)])
+
+
+def across_tiles(at, far_edge, far_rest):
+    odd = lax.rem(at.z, 2)
+    b = 2 * lax.rem(at.z + 2, at.n_lon)
+    return [far_edge[0], far_rest[0]], [at.row(b + odd), at.row(b + 1 - odd)]
 
 
 def corner_tiles(at, same, other):
     return [same[0], other[0], same[1], other[1]], [at.rim(True), at.rim(False)] * 2
 
 
-def across_tiles(at, far):
-    b = lax.rem(2 * at.z + 4, 8)
-    return [far[0], far[1]], [at.row(b), at.row(b + 1)]
-
-
-def rim_tiles(at, same, other, same_edges, other_edges):
-    return ([same[0], same[1], other[0], other[1], same_edges[0], same_edges[1], other_edges[0], other_edges[1]],
-            [at.rim(True)] * 2 + [at.rim(False)] * 2 + [at.rim(True)] * 2 + [at.rim(False)] * 2)
+def rim_tiles(at, same, other):
+    return [same[0], same[1], other[0], other[1]], [at.rim(True)] * 2 + [at.rim(False)] * 2
 
 
 def column_tiles(start, at, row):
@@ -251,27 +265,33 @@
     x = tokens[0]
     if n_lon == 4:
         near_pairs = [(i, i ^ 1) for i in range(4)]
+        ring_pairs = [(0, 3), (3, 0), (1, 2), (2, 1)]
+        even = lax.rem(z, 2) == 0
+        near = lax.ppermute(x, "lon", near_pairs)
+        ring_edge = lax.ppermute(jnp.where(even, x[:1], x[1:]), "lon", ring_pairs)
         same, other = lat_swap(x, n_lat)
-        ring = lax.ppermute(x, "lon", [(0, 3), (3, 0), (1, 2), (2, 1)])
-        near = lax.ppermute(x, "lon", near_pairs)
-        q, *state = attend(own_alone, PAIRS, 3, place, tele_ids, [x], w_qkv, "own")
-        near, ring, same, other = gate([near, ring, same, other], [state[0]])
-        even = lax.rem(z, 2) == 0
-        edges = jnp.concatenate([jnp.where(even, ring[1:], near[1:]), jnp.where(even, near[:1], ring[:1])], 0)
+        q, rest, *state = attend(own_alone, PAIRS, 3, place, tele_ids, [x], w_qkv, "own")
+        ring_rest = lax.ppermute(rest, "lon", ring_pairs)
+        near, ring_edge = gate([near, ring_edge], [q])
+        edges = jnp.concatenate([jnp.where(even, ring_edge, near[1:]), jnp.where(even, near[:1], ring_edge)], 0)
         same_edges, other_edges = lat_swap(edges, n_lat)
-        far = lax.ppermute(ring, "lon", near_pairs)
-        state = attend(near_tiles, [list(range(8))] * 2, 8, place, tele_ids, [near, ring, same, other], w_qkv, "near", q, state)
+        state = attend(rim_tiles, BOTH, 4, place, tele_ids, [same, other], w_qkv, "rim", q, state)
+        ring_edge, ring_rest = gate([ring_edge, ring_rest], [state[1]])
+        far_edge = lax.ppermute(ring_edge, "lon", near_pairs)
+        far_rest = lax.ppermute(ring_rest, "lon", near_pairs)
+        state = attend(lon_tiles, BOTH, 4, place, tele_ids, [near, ring_edge, ring_rest], w_qkv, "lon", q, state)
         state = attend(corner_tiles, [[0, 1], [2, 3]], 4, place, tele_ids,
                        [same_edges, other_edges], w_qkv, "corner", q, state)
-        mixed = attend(across_tiles, PAIRS, 3, place, tele_ids, [far], w_qkv, "across", q, state, w_out)[0]
-    else:
-        q, *state = attend(own_alone, PAIRS, 2, place, tele_ids, [x], w_qkv, "own")
+        mixed = attend(across_tiles, PAIRS, 3, place, tele_ids, [far_edge, far_rest], w_qkv, "across", q, state, w_out)[0]
+    else:
+        q, _, *state = attend(own_alone, PAIRS, 2, place, tele_ids, [x], w_qkv, "own")
         same, other = lat_swap(x, n_lat)
         before = lax.ppermute(x[1:], "lon", [(i, (i + 1) % n_lon) for i in range(n_lon)])
         after = lax.ppermute(x[:1], "lon", [((i + 1) % n_lon, i) for i in range(n_lon)])
         same_edges, other_edges = lat_swap(jnp.concatenate([before, after], 0), n_lat)
-        state = attend(rim_tiles, [[0, 1, 2, 3, 4, 6], [0, 1, 2, 3, 5, 7]], 8, place, tele_ids,
-                       [same, other, same_edges, other_edges], w_qkv, "rim", q, state)
+        state = attend(rim_tiles, BOTH, 4, place, tele_ids, [same, other], w_qkv, "rim", q, state)
+        state = attend(corner_tiles, [[0, 1], [2, 3]], 4, place, tele_ids,
+                       [same_edges, other_edges], w_qkv, "corner", q, state)
         row = lax.all_gather(x, "lon", axis=0, tiled=True)
         for s in range(0, 2 * n_lon, 4):
             state = attend(functools.partial(column_tiles, s), BOTH, 4, place, tele_ids, [row[s:s + 4]], w_qkv,

time: 55.3 us -> 53.5 us (0.967)
  the two profiles are of different devices: /device:TPU:1 before, /device:TPU:29 now
where the time goes in v3:
time: 53.5 us; the launch traced here: 53.3 us
  Pallas kernels  26.9 us (50%)
  starting transfers between devices  20 us (37%)
  local copies, waits for them, and re-layouts  4.51 us (8%)
  other arithmetic  1.16 us (2%)
  waiting for transfers between devices  0.6 us (1%)
    pallas_call x5, Pallas kernels, attend(): pl.pallas_call(functools.partial(attend_kernel, gather, users, len(xs), k...  26.9 us
    ppermute x4, starting transfers between devices, lat_swap(): return (lax.ppermute(array, 'lat', same), lax.ppermute(array, 'lat', other))  14.9 us
    unnamed x10, local copies, waits for them, and re-layouts  4.51 us
    ppermute x1, starting transfers between devices, on_device(): ring_rest = lax.ppermute(rest, 'lon', ring_pairs)  2.26 us
    ppermute x1, starting transfers between devices, on_device(): far_rest = lax.ppermute(ring_rest, 'lon', near_pairs)  1.45 us
    ppermute x1, starting transfers between devices, on_device(): ring_edge = lax.ppermute(jnp.where(even, x[:1], x[1:]), 'lon', ring_pairs)  1.13 us
  transfers between devices with their start and end apart: 9, of which 1 were waited for; matrix products, arithmetic and copies ran while one was open for 2% of the time, Pallas kernels for 40%

profile of v3, /device:TPU:29, one launch (start us, length us, event | category | flops | bytes accessed | tf_op | source)
XLA Modules:
  0.0 53.3 jit_solution(8886520175689140928)
XLA Ops:
  0.0 0.2 collective-permute-start
  0.2 1.1 %select_bitcast_fusion = bf16[1,128,1024]{2,1,0:T(8,128)(2,1)S(1)} fusion(bf16[1,2,128,1024]{3,2,1,0:T(8,128)(2,1)} %param.4, pred[]{:T(512)S(6)} %eq.3), kind=kLoop, calls=%fused_computation.3 | loop fusion | flops 131072 | bytes 786433 | tf_op jit(solution)/shard_map/jit(_where)/select_n | solution.py:271
  1.2 1.1 %collective-permute-start.1 = (bf16[1,128,1024]{2,1,0:T(8,128)(2,1)S(1)}, bf16[1,128,1024]{2,1,0:T(8,128)(2,1)S(1)}, u32[]{:S(2)}, u32[]{:S(2)}) collective-permute-start(bf16[1,128,1024]{2,1,0:T(8,128)(2,1)S(1)} %select_bitcast_fusion), channel_id=1, source_target_pairs={{0,3},{3,0},{1,2},{2,1},{4,7},{7,4},{5,6},{6,5},{8,11},{11,8},{9,1... | collective-permute-start | bytes 786440 | tf_op jit(solution)/shard_map/ppermute | solution.py:271
  2.4 1.2 %collective-permute-start.3 = (bf16[2,128,1024]{2,1,0:T(8,128)(2,1)}, bf16[2,128,1024]{2,1,0:T(8,128)(2,1)S(1)}, u32[]{:S(2)}, u32[]{:S(2)}) collective-permute-start(bf16[2,128,1024]{2,1,0:T(8,128)(2,1)} %bitcast.5), channel_id=1, source_target_pairs={{0,4},{4,0},{8,12},{12,8},{16,20},{20,16},{24,28},{28,24},{1,5},{5... | collective-permute-start | bytes 1572872 | tf_op jit(solution)/shard_map/ppermute | solution.py:223
  3.6 3.0 %collective-permute-start.4 = (bf16[2,128,1024]{2,1,0:T(8,128)(2,1)}, bf16[2,128,1024]{2,1,0:T(8,128)(2,1)S(1)}, u32[]{:S(2)}, u32[]{:S(2)}) collective-permute-start(bf16[2,128,1024]{2,1,0:T(8,128)(2,1)} %bitcast.6), channel_id=1, source_target_pairs={{4,8},{8,4},{12,16},{16,12},{20,24},{24,20},{5,9},{9,5},{13,17},{1... | collective-permute-start | bytes 1572872 | tf_op jit(solution)/shard_map/ppermute | solution.py:223
  6.6 0.0 copy-start
  6.6 2.8 %copy-done = bf16[1024,3072]{1,0:T(8,128)(2,1)S(1)} copy-done((bf16[1024,3072]{1,0:T(8,128)(2,1)S(1)}, bf16[1024,3072]{1,0:T(8,128)(2,1)}, u32[]{:S(2)}) %copy-start) | copy-done | bytes 6291480
  9.4 0.0 copy-start.3
  9.4 1.0 %copy-done.3 = bf16[1,2,128,1024]{3,2,1,0:T(8,128)(2,1)S(1)} copy-done((bf16[1,2,128,1024]{3,2,1,0:T(8,128)(2,1)S(1)}, bf16[1,2,128,1024]{3,2,1,0:T(8,128)(2,1)}, u32[]{:S(2)}) %copy-start.3) | copy-done | bytes 524312
  10.4 0.0 copy-start.4
  10.4 0.7 %copy-done.4 = s32[1,2,8]{2,1,0:T(2,128)S(1)} copy-done((s32[1,2,8]{2,1,0:T(2,128)S(1)}, s32[1,2,8]{2,1,0:T(2,128)}, u32[]{:S(2)}) %copy-start.4) | copy-done | bytes 88
  11.1 0.0 copy-start.1
  11.1 4.4 %own.1 = (bf16[256,1024]{1,0:T(8,128)(2,1)S(1)}, bf16[1,128,1024]{2,1,0:T(8,128)(2,1)S(1)}, f32[256,1024]{1,0:T(8,128)S(1)}, f32[256,1024]{1,0:T(8,128)S(1)}, f32[256,1024]{1,0:T(8,128)S(1)}) custom-call(s32[1,2,8]{2,1,0:T(2,128)S(1)} %copy-done.4, bf16[2,128,1024]{2,1,0:T(8,128)(2,1)S(1)} %bitcast.7, bf16[1024,3072]{1,0:T(8,128)(2,1)S(1)} %copy-done), custom_call_target="tpu_custom_call" | custom-call | tf_op jit(solution)/shard_map/own/pallas_call | solution.py:191
  15.6 2.3 %collective-permute-start.2 = (bf16[1,128,1024]{2,1,0:T(8,128)(2,1)S(1)}, bf16[1,128,1024]{2,1,0:T(8,128)(2,1)S(1)}, u32[]{:S(2)}, u32[]{:S(2)}) collective-permute-start(bf16[1,128,1024]{2,1,0:T(8,128)(2,1)S(1)} %get-tuple-element.26), channel_id=1, source_target_pairs={{0,3},{3,0},{1,2},{2,1},{4,7},{7,4},{5,6},{6,5},{8,11},{11,8},{9,1... | collective-permute-start | bytes 786440 | tf_op jit(solution)/shard_map/ppermute | solution.py:274
  17.8 0.6 %collective-permute-done.1.refs_1_ = bf16[1,128,1024]{2,1,0:T(8,128)(2,1)S(1)} collective-permute-done((bf16[1,128,1024]{2,1,0:T(8,128)(2,1)S(1)}, bf16[1,128,1024]{2,1,0:T(8,128)(2,1)S(1)}, u32[]{:S(2)}, u32[]{:S(2)}) %collective-permute-start.1) | collective-permute-done | bytes 262176 | tf_op jit(solution)/shard_map/ppermute | solution.py:271
  18.4 0.0 collective-permute-done.refs_0_
  18.4 0.1 slice_select_fusion.1
  18.5 0.1 pad_maximum_fusion
  18.5 1.8 %collective-permute-start.7 = (bf16[2,128,1024]{2,1,0:T(8,128)(2,1)S(1)}, bf16[2,128,1024]{2,1,0:T(8,128)(2,1)S(1)}, u32[]{:S(2)}, u32[]{:S(2)}) collective-permute-start(bf16[2,128,1024]{2,1,0:T(8,128)(2,1)S(1)} %pad_maximum_fusion), channel_id=1, source_target_pairs={{0,4},{4,0},{8,12},{12,8},{16,20},{20,16},{24,28},{28,24},{1,5},{5... | collective-permute-start | bytes 1572872 | tf_op jit(solution)/shard_map/ppermute | solution.py:223
  20.3 8.8 %collective-permute-start.8 = (bf16[2,128,1024]{2,1,0:T(8,128)(2,1)S(1)}, bf16[2,128,1024]{2,1,0:T(8,128)(2,1)S(1)}, u32[]{:S(2)}, u32[]{:S(2)}) collective-permute-start(bf16[2,128,1024]{2,1,0:T(8,128)(2,1)S(1)} %pad_maximum_fusion), channel_id=1, source_target_pairs={{4,8},{8,4},{12,16},{16,12},{20,24},{24,20},{5,9},{9,5},{13,17},{1... | collective-permute-start | bytes 1572872 | tf_op jit(solution)/shard_map/ppermute | solution.py:223
  29.2 0.0 collective-permute-done.3.refs_0_
  29.2 0.0 collective-permute-done.4.refs_1_
  29.2 0.0 copy-done.1
  29.2 6.1 %rim.1 = (f32[256,1024]{1,0:T(8,128)S(1)}, f32[256,1024]{1,0:T(8,128)S(1)}, f32[256,1024]{1,0:T(8,128)S(1)}) custom-call(s32[1,2,8]{2,1,0:T(2,128)S(1)} %copy-done.4, bf16[2,128,1024]{2,1,0:T(8,128)(2,1)S(1)} %collective-permute-done.3.refs_0_, ...), custom_call_target="tpu_custom_call", output_to_operand_aliasing={{0}: (5, {}), {1}: (6, {}), {2}: (7, {})} | custom-call | tf_op jit(solution)/shard_map/rim/pallas_call | solution.py:191
  35.3 0.0 collective-permute-done.2.refs_1_
  35.3 0.1 collective-permute-start.5
  35.4 1.5 %collective-permute-start.6 = (bf16[1,128,1024]{2,1,0:T(8,128)(2,1)S(1)}, bf16[1,128,1024]{2,1,0:T(8,128)(2,1)S(1)}, u32[]{:S(2)}, u32[]{:S(2)}) collective-permute-start(bf16[1,128,1024]{2,1,0:T(8,128)(2,1)S(1)} %get-tuple-element.32.refs_2_), channel_id=1, source_target_pairs={{0,1},{1,0},{2,3},{3,2},{4,5},{5,4},{6,7},{7,6},{8,9},{9,8},{10,11... | collective-permute-start | bytes 786440 | tf_op jit(solution)/shard_map/ppermute | solution.py:281
  36.8 6.1 %lon.1 = (f32[256,1024]{1,0:T(8,128)S(1)}, f32[256,1024]{1,0:T(8,128)S(1)}, f32[256,1024]{1,0:T(8,128)S(1)}) custom-call(s32[1,2,8]{2,1,0:T(2,128)S(1)} %copy-done.4, bf16[2,128,1024]{2,1,0:T(8,128)(2,1)S(1)} %get-tuple-element.33.refs_0_, ...), custom_call_target="tpu_custom_call", output_to_operand_aliasing={{0}: (6, {}), {1}: (7, {}), {2}: (8, {})} | custom-call | tf_op jit(solution)/shard_map/lon/pallas_call | solution.py:191
  42.9 0.0 copy-start.2
  43.0 0.0 collective-permute-done.7.refs_0_
  43.0 0.0 collective-permute-done.8.refs_1_
  43.0 4.9 %corner.1 = (f32[256,1024]{1,0:T(8,128)S(1)}, f32[256,1024]{1,0:T(8,128)S(1)}, f32[256,1024]{1,0:T(8,128)S(1)}) custom-call(s32[1,2,8]{2,1,0:T(2,128)S(1)} %copy-done.4, bf16[2,128,1024]{2,1,0:T(8,128)(2,1)S(1)} %collective-permute-done.7.refs_0_, ...), custom_call_target="tpu_custom_call", output_to_operand_aliasing={{0}: (5, {}), {1}: (6, {}), {2}: (7, {})} | custom-call | tf_op jit(solution)/shard_map/corner/pallas_call | solution.py:191
  47.9 0.0 collective-permute-done.5.refs_0_
  47.9 0.0 collective-permute-done.6.refs_1_
  47.9 0.0 copy-done.2
  47.9 5.4 %across.1 = (bf16[256,1024]{1,0:T(8,128)(2,1)}, f32[256,1024]{1,0:T(8,128)S(1)}, f32[256,1024]{1,0:T(8,128)S(1)}, f32[256,1024]{1,0:T(8,128)S(1)}) custom-call(s32[1,2,8]{2,1,0:T(2,128)S(1)} %copy-done.4, bf16[1,128,1024]{2,1,0:T(8,128)(2,1)S(1)} %collective-permute-done.5.refs_0_, ...), custom_call_target="tpu_custom_call", output_to_operand_aliasing={{1}: (6, {}), {2}: (7, {}), {3}: (8, {})} | custom-call | tf_op jit(solution)/shard_map/across/pallas_call | solution.py:191
  (2 shorter events, 0.0 us)
Async XLA Ops:
  0.0 18.4 %collective-permute-start = (bf16[2,128,1024]{2,1,0:T(8,128)(2,1)}, bf16[2,128,1024]{2,1,0:T(8,128)(2,1)S(1)}, u32[]{:S(2)}, u32[]{:S(2)}) collective-permute-start(bf16[2,128,1024]{2,1,0:T(8,128)(2,1)} %bitcast.4), channel_id=1, source_target_pairs={{0,1},{1,0},{2,3},{3,2},{4,5},{5,4},{6,7},{7,6},{8,9},{9,8},{10,11... | collective-permute-start | bytes 1572872 | tf_op jit(solution)/shard_map/ppermute | solution.py:270
  1.2 17.2 %collective-permute-start.1 = (bf16[1,128,1024]{2,1,0:T(8,128)(2,1)S(1)}, bf16[1,128,1024]{2,1,0:T(8,128)(2,1)S(1)}, u32[]{:S(2)}, u32[]{:S(2)}) collective-permute-start(bf16[1,128,1024]{2,1,0:T(8,128)(2,1)S(1)} %select_bitcast_fusion), channel_id=1, source_target_pairs={{0,3},{3,0},{1,2},{2,1},{4,7},{7,4},{5,6},{6,5},{8,11},{11,8},{9,1... | collective-permute-start | bytes 786440 | tf_op jit(solution)/shard_map/ppermute | solution.py:271
  2.4 26.8 %collective-permute-start.3 = (bf16[2,128,1024]{2,1,0:T(8,128)(2,1)}, bf16[2,128,1024]{2,1,0:T(8,128)(2,1)S(1)}, u32[]{:S(2)}, u32[]{:S(2)}) collective-permute-start(bf16[2,128,1024]{2,1,0:T(8,128)(2,1)} %bitcast.5), channel_id=1, source_target_pairs={{0,4},{4,0},{8,12},{12,8},{16,20},{20,16},{24,28},{28,24},{1,5},{5... | collective-permute-start | bytes 1572872 | tf_op jit(solution)/shard_map/ppermute | solution.py:223
  3.6 25.6 %collective-permute-start.4 = (bf16[2,128,1024]{2,1,0:T(8,128)(2,1)}, bf16[2,128,1024]{2,1,0:T(8,128)(2,1)S(1)}, u32[]{:S(2)}, u32[]{:S(2)}) collective-permute-start(bf16[2,128,1024]{2,1,0:T(8,128)(2,1)} %bitcast.6), channel_id=1, source_target_pairs={{4,8},{8,4},{12,16},{16,12},{20,24},{24,20},{5,9},{9,5},{13,17},{1... | collective-permute-start | bytes 1572872 | tf_op jit(solution)/shard_map/ppermute | solution.py:223
  6.6 2.8 %copy-start = (bf16[1024,3072]{1,0:T(8,128)(2,1)S(1)}, bf16[1024,3072]{1,0:T(8,128)(2,1)}, u32[]{:S(2)}) copy-start(bf16[1024,3072]{1,0:T(8,128)(2,1)} %refs_3_.5) | copy-start | bytes 18874372
  9.4 1.0 %copy-start.3 = (bf16[1,2,128,1024]{3,2,1,0:T(8,128)(2,1)S(1)}, bf16[1,2,128,1024]{3,2,1,0:T(8,128)(2,1)}, u32[]{:S(2)}) copy-start(bf16[1,2,128,1024]{3,2,1,0:T(8,128)(2,1)} %param.4) | copy-start | bytes 1572868
  10.4 0.7 %copy-start.4 = (s32[1,2,8]{2,1,0:T(2,128)S(1)}, s32[1,2,8]{2,1,0:T(2,128)}, u32[]{:S(2)}) copy-start(s32[1,2,8]{2,1,0:T(2,128)} %tele_ref.9) | copy-start | bytes 196
  11.1 18.1 %copy-start.1 = (bf16[1024,3072]{1,0:T(8,128)(2,1)S(1)}, bf16[1024,3072]{1,0:T(8,128)(2,1)}, u32[]{:S(2)}) copy-start(bf16[1024,3072]{1,0:T(8,128)(2,1)} %refs_3_.5) | copy-start | bytes 18874372
  15.6 19.7 %collective-permute-start.2 = (bf16[1,128,1024]{2,1,0:T(8,128)(2,1)S(1)}, bf16[1,128,1024]{2,1,0:T(8,128)(2,1)S(1)}, u32[]{:S(2)}, u32[]{:S(2)}) collective-permute-start(bf16[1,128,1024]{2,1,0:T(8,128)(2,1)S(1)} %get-tuple-element.26), channel_id=1, source_target_pairs={{0,3},{3,0},{1,2},{2,1},{4,7},{7,4},{5,6},{6,5},{8,11},{11,8},{9,1... | collective-permute-start | bytes 786440 | tf_op jit(solution)/shard_map/ppermute | solution.py:274
  18.5 24.4 %collective-permute-start.7 = (bf16[2,128,1024]{2,1,0:T(8,128)(2,1)S(1)}, bf16[2,128,1024]{2,1,0:T(8,128)(2,1)S(1)}, u32[]{:S(2)}, u32[]{:S(2)}) collective-permute-start(bf16[2,128,1024]{2,1,0:T(8,128)(2,1)S(1)} %pad_maximum_fusion), channel_id=1, source_target_pairs={{0,4},{4,0},{8,12},{12,8},{16,20},{20,16},{24,28},{28,24},{1,5},{5... | collective-permute-start | bytes 1572872 | tf_op jit(solution)/shard_map/ppermute | solution.py:223
  20.3 22.6 %collective-permute-start.8 = (bf16[2,128,1024]{2,1,0:T(8,128)(2,1)S(1)}, bf16[2,128,1024]{2,1,0:T(8,128)(2,1)S(1)}, u32[]{:S(2)}, u32[]{:S(2)}) collective-permute-start(bf16[2,128,1024]{2,1,0:T(8,128)(2,1)S(1)} %pad_maximum_fusion), channel_id=1, source_target_pairs={{4,8},{8,4},{12,16},{16,12},{20,24},{24,20},{5,9},{9,5},{13,17},{1... | collective-permute-start | bytes 1572872 | tf_op jit(solution)/shard_map/ppermute | solution.py:223
  35.3 12.6 %collective-permute-start.5 = (bf16[1,128,1024]{2,1,0:T(8,128)(2,1)S(1)}, bf16[1,128,1024]{2,1,0:T(8,128)(2,1)S(1)}, u32[]{:S(2)}, u32[]{:S(2)}) collective-permute-start(bf16[1,128,1024]{2,1,0:T(8,128)(2,1)S(1)} %get-tuple-element.31.refs_1_), channel_id=1, source_target_pairs={{0,1},{1,0},{2,3},{3,2},{4,5},{5,4},{6,7},{7,6},{8,9},{9,8},{10,11... | collective-permute-start | bytes 786440 | tf_op jit(solution)/shard_map/ppermute | solution.py:280
  35.4 12.5 %collective-permute-start.6 = (bf16[1,128,1024]{2,1,0:T(8,128)(2,1)S(1)}, bf16[1,128,1024]{2,1,0:T(8,128)(2,1)S(1)}, u32[]{:S(2)}, u32[]{:S(2)}) collective-permute-start(bf16[1,128,1024]{2,1,0:T(8,128)(2,1)S(1)} %get-tuple-element.32.refs_2_), channel_id=1, source_target_pairs={{0,1},{1,0},{2,3},{3,2},{4,5},{5,4},{6,7},{7,6},{8,9},{9,8},{10,11... | collective-permute-start | bytes 786440 | tf_op jit(solution)/shard_map/ppermute | solution.py:281
  42.9 5.0 %copy-start.2 = (bf16[1024,1024]{1,0:T(8,128)(2,1)S(1)}, bf16[1024,1024]{1,0:T(8,128)(2,1)}, u32[]{:S(2)}) copy-start(bf16[1024,1024]{1,0:T(8,128)(2,1)} %refs_4_.3) | copy-start | bytes 6291460

commit v4 on v3

--- a/solution.py
+++ b/solution.py
@@ -11,7 +11,7 @@
 BLOCK = 128
 PAIR = 2 * HD
 NEG = -1e30
-CW = 256
+CW = 1024
 VM = 24
 COST = 0
 UNIT = 1.4426950408889634 * HD ** -0.5
@@ -139,8 +139,7 @@
     bias = [[both[t] for both in tiles_bias] for t in range(2)]
     width = xs[0].shape[-1]
     if kind == "first":
-        w, q_ref, rest_ref, o_ref, m_ref, l_ref = refs
-        rest_ref[0] = jnp.where(lax.rem(at.z, 2) == 0, x_refs[0][1], x_refs[0][0])
+        w, q_ref, o_ref, m_ref, l_ref = refs
     elif kind == "last":
         q_ref, w, w_out, o_in, m_in, l_in, out_ref, o_ref, m_ref, l_ref, att = refs
     else:
@@ -180,7 +179,7 @@
     aliases, scratch = {}, []
     if kind == "first":
         args += [w_qkv]
-        out_shape = [q_shape, jax.ShapeDtypeStruct((1,) + xs[0].shape[1:], xs[0].dtype)] + out_shape
+        out_shape = [q_shape] + out_shape
     else:
         args += [q, w_qkv] + ([w_out] if kind == "last" else []) + list(state)
         out_shape = ([q_shape] if kind == "last" else []) + out_shape
@@ -228,12 +227,12 @@
     return [x[0], x[1]], [at.row(b), at.row(b + 1)]
 
 
-def lon_tiles(at, near, ring_edge, ring_rest):
+def lon_tiles(at, near_edge, near_rest, ring_edge, ring_rest):
     odd = lax.rem(at.z, 2)
     b = 2 * (at.z + 1 - 2 * odd)
     c = 2 * lax.rem(at.z - 1 + 2 * odd + at.n_lon, at.n_lon)
-    return ([near[0], near[1], ring_edge[0], ring_rest[0]],
-            [at.row(b), at.row(b + 1), at.row(c + 1 - odd), at.row(c + odd)])
+    return ([near_edge[0], near_rest[0], ring_edge[0], ring_rest[0]],
+            [at.row(b + odd), at.row(b + 1 - odd), at.row(c + 1 - odd), at.row(c + odd)])
 
 
 def across_tiles(at, far_edge, far_rest):
@@ -267,24 +266,26 @@
         near_pairs = [(i, i ^ 1) for i in range(4)]
         ring_pairs = [(0, 3), (3, 0), (1, 2), (2, 1)]
         even = lax.rem(z, 2) == 0
-        near = lax.ppermute(x, "lon", near_pairs)
-        ring_edge = lax.ppermute(jnp.where(even, x[:1], x[1:]), "lon", ring_pairs)
+        inner, outer = jnp.where(even, x[1:], x[:1]), jnp.where(even, x[:1], x[1:])
+        near_edge = lax.ppermute(inner, "lon", near_pairs)
+        ring_edge = lax.ppermute(outer, "lon", ring_pairs)
         same, other = lat_swap(x, n_lat)
-        q, rest, *state = attend(own_alone, PAIRS, 3, place, tele_ids, [x], w_qkv, "own")
-        ring_rest = lax.ppermute(rest, "lon", ring_pairs)
-        near, ring_edge = gate([near, ring_edge], [q])
-        edges = jnp.concatenate([jnp.where(even, ring_edge, near[1:]), jnp.where(even, near[:1], ring_edge)], 0)
+        q, *state = attend(own_alone, PAIRS, 3, place, tele_ids, [x], w_qkv, "own")
+        near_rest = lax.ppermute(outer, "lon", near_pairs)
+        ring_rest = lax.ppermute(inner, "lon", ring_pairs)
+        near_edge, ring_edge = gate([near_edge, ring_edge], [q])
+        edges = jnp.concatenate([jnp.where(even, ring_edge, near_edge), jnp.where(even, near_edge, ring_edge)], 0)
         same_edges, other_edges = lat_swap(edges, n_lat)
         state = attend(rim_tiles, BOTH, 4, place, tele_ids, [same, other], w_qkv, "rim", q, state)
-        ring_edge, ring_rest = gate([ring_edge, ring_rest], [state[1]])
+        ring_edge, ring_rest, near_rest = gate([ring_edge, ring_rest, near_rest], [state[1]])
         far_edge = lax.ppermute(ring_edge, "lon", near_pairs)
         far_rest = lax.ppermute(ring_rest, "lon", near_pairs)
-        state = attend(lon_tiles, BOTH, 4, place, tele_ids, [near, ring_edge, ring_rest], w_qkv, "lon", q, state)
+        state = attend(lon_tiles, BOTH, 4, place, tele_ids, [near_edge, near_rest, ring_edge, ring_rest], w_qkv, "lon", q, state)
         state = attend(corner_tiles, [[0, 1], [2, 3]], 4, place, tele_ids,
                        [same_edges, other_edges], w_qkv, "corner", q, state)
         mixed = attend(across_tiles, PAIRS, 3, place, tele_ids, [far_edge, far_rest], w_qkv, "across", q, state, w_out)[0]
     else:
-        q, _, *state = attend(own_alone, PAIRS, 2, place, tele_ids, [x], w_qkv, "own")
+        q, *state = attend(own_alone, PAIRS, 2, place, tele_ids, [x], w_qkv, "own")
         same, other = lat_swap(x, n_lat)
         before = lax.ppermute(x[1:], "lon", [(i, (i + 1) % n_lon) for i in range(n_lon)])
         after = lax.ppermute(x[:1], "lon", [((i + 1) % n_lon, i) for i in range(n_lon)])

time: 53.5 us -> 48.9 us (0.914)
  the two profiles are of different devices: /device:TPU:29 before, /device:TPU:0 now
where the time goes in v4:
time: 48.9 us; the launch traced here: 48.7 us
  Pallas kernels  25.7 us (53%)
  starting transfers between devices  16.3 us (33%)
  local copies, waits for them, and re-layouts  4.51 us (9%)
  other arithmetic  1.16 us (2%)
  waiting for transfers between devices  0.87 us (2%)
    pallas_call x5, Pallas kernels, attend(): pl.pallas_call(functools.partial(attend_kernel, gather, users, len(xs), k...  25.7 us
    ppermute x4, starting transfers between devices, lat_swap(): return (lax.ppermute(array, 'lat', same), lax.ppermute(array, 'lat', other))  6.98 us
    ppermute x1, starting transfers between devices, on_device(): ring_edge = lax.ppermute(outer, 'lon', ring_pairs)  5.11 us
    unnamed x10, local copies, waits for them, and re-layouts  4.51 us
    ppermute x1, starting transfers between devices, on_device(): near_rest = lax.ppermute(outer, 'lon', near_pairs)  2.09 us
    ppermute x1, starting transfers between devices, on_device(): far_edge = lax.ppermute(ring_edge, 'lon', near_pairs)  1.28 us
    select_n x1, other arithmetic, on_device(): jnp.where(even, x[:1], x[1:])  1.07 us
  transfers between devices with their start and end apart: 10, of which 1 were waited for; matrix products, arithmetic and copies ran while one was open for 0% of the time, Pallas kernels for 43%

profile of v4, /device:TPU:0, one launch (start us, length us, event | category | flops | bytes accessed | tf_op | source)
XLA Modules:
  0.0 48.7 jit_solution(1159391598462508604)
XLA Ops:
  0.0 1.1 %select_bitcast_fusion = (bf16[1,128,1024]{2,1,0:T(8,128)(2,1)S(1)}, bf16[1,128,1024]{2,1,0:T(8,128)(2,1)S(1)}) fusion(pred[]{:T(512)S(6)} %eq.3, bf16[1,2,128,1024]{3,2,1,0:T(8,128)(2,1)} %param.4), kind=kLoop, calls=%fused_computation.1 | loop fusion | flops 262144 | bytes 1048577 | tf_op jit(solution)/shard_map/jit(_where)/select_n | solution.py:269
  1.1 5.1 %collective-permute-start.1 = (bf16[1,128,1024]{2,1,0:T(8,128)(2,1)S(1)}, bf16[1,128,1024]{2,1,0:T(8,128)(2,1)S(1)}, u32[]{:S(2)}, u32[]{:S(2)}) collective-permute-start(bf16[1,128,1024]{2,1,0:T(8,128)(2,1)S(1)} %get-tuple-element.45), channel_id=1, source_target_pairs={{0,3},{3,0},{1,2},{2,1},{4,7},{7,4},{5,6},{6,5},{8,11},{11,8},{9,1... | collective-permute-start | bytes 786440 | tf_op jit(solution)/shard_map/ppermute | solution.py:271
  6.2 0.0 collective-permute-start
  6.2 0.7 %collective-permute-start.5 = (bf16[2,128,1024]{2,1,0:T(8,128)(2,1)}, bf16[2,128,1024]{2,1,0:T(8,128)(2,1)S(1)}, u32[]{:S(2)}, u32[]{:S(2)}) collective-permute-start(bf16[2,128,1024]{2,1,0:T(8,128)(2,1)} %bitcast.6), channel_id=1, source_target_pairs={{4,8},{8,4},{12,16},{16,12},{20,24},{24,20},{5,9},{9,5},{13,17},{1... | collective-permute-start | bytes 1572872 | tf_op jit(solution)/shard_map/ppermute | solution.py:222
  6.9 2.1 %collective-permute-start.3 = (bf16[1,128,1024]{2,1,0:T(8,128)(2,1)S(1)}, bf16[1,128,1024]{2,1,0:T(8,128)(2,1)S(1)}, u32[]{:S(2)}, u32[]{:S(2)}) collective-permute-start(bf16[1,128,1024]{2,1,0:T(8,128)(2,1)S(1)} %get-tuple-element.45), channel_id=1, source_target_pairs={{0,1},{1,0},{2,3},{3,2},{4,5},{5,4},{6,7},{7,6},{8,9},{9,8},{10,11... | collective-permute-start | bytes 786440 | tf_op jit(solution)/shard_map/ppermute | solution.py:274
  9.0 0.1 collective-permute-start.2
  9.0 0.0 copy-start
  9.0 2.8 %copy-done = bf16[1024,3072]{1,0:T(8,128)(2,1)S(1)} copy-done((bf16[1024,3072]{1,0:T(8,128)(2,1)S(1)}, bf16[1024,3072]{1,0:T(8,128)(2,1)}, u32[]{:S(2)}) %copy-start) | copy-done | bytes 6291480
  11.8 0.0 copy-start.3
  11.8 1.0 %copy-done.3 = bf16[1,2,128,1024]{3,2,1,0:T(8,128)(2,1)S(1)} copy-done((bf16[1,2,128,1024]{3,2,1,0:T(8,128)(2,1)S(1)}, bf16[1,2,128,1024]{3,2,1,0:T(8,128)(2,1)}, u32[]{:S(2)}) %copy-start.3) | copy-done | bytes 524312
  12.9 0.0 copy-start.4
  12.9 0.7 %copy-done.4 = s32[1,2,8]{2,1,0:T(2,128)S(1)} copy-done((s32[1,2,8]{2,1,0:T(2,128)S(1)}, s32[1,2,8]{2,1,0:T(2,128)}, u32[]{:S(2)}) %copy-start.4) | copy-done | bytes 88
  13.6 0.0 copy-start.1
  13.6 3.7 %own.1 = (bf16[256,1024]{1,0:T(8,128)(2,1)S(1)}, f32[256,1024]{1,0:T(8,128)S(1)}, f32[256,1024]{1,0:T(8,128)S(1)}, f32[256,1024]{1,0:T(8,128)S(1)}) custom-call(s32[1,2,8]{2,1,0:T(2,128)S(1)} %copy-done.4, bf16[2,128,1024]{2,1,0:T(8,128)(2,1)S(1)} %bitcast.7, bf16[1024,3072]{1,0:T(8,128)(2,1)S(1)} %copy-done), custom_call_target="tpu_custom_call" | custom-call | tf_op jit(solution)/shard_map/own/pallas_call | solution.py:190
  17.2 0.0 collective-permute-done.1.refs_1_
  17.2 2.5 %collective-permute-start.4 = (bf16[2,128,1024]{2,1,0:T(8,128)(2,1)S(1)}, bf16[2,128,1024]{2,1,0:T(8,128)(2,1)S(1)}, u32[]{:S(2)}, u32[]{:S(2)}) collective-permute-start(bf16[2,128,1024]{2,1,0:T(8,128)(2,1)S(1)} %bitcast.8), channel_id=1, source_target_pairs={{0,4},{4,0},{8,12},{12,8},{16,20},{20,16},{24,28},{28,24},{1,5},{5... | collective-permute-start | bytes 1572872 | tf_op jit(solution)/shard_map/ppermute | solution.py:222
  19.8 0.0 collective-permute-done.refs_0_
  19.8 0.1 pad_maximum_fusion
  19.9 0.9 %collective-permute-start.9 = (bf16[2,128,1024]{2,1,0:T(8,128)(2,1)S(1)}, bf16[2,128,1024]{2,1,0:T(8,128)(2,1)S(1)}, u32[]{:S(2)}, u32[]{:S(2)}) collective-permute-start(bf16[2,128,1024]{2,1,0:T(8,128)(2,1)S(1)} %pad_maximum_fusion), channel_id=1, source_target_pairs={{4,8},{8,4},{12,16},{16,12},{20,24},{24,20},{5,9},{9,5},{13,17},{1... | collective-permute-start | bytes 1572872 | tf_op jit(solution)/shard_map/ppermute | solution.py:222
  20.8 0.0 collective-permute-done.5.refs_1_
  20.8 2.9 %collective-permute-start.8 = (bf16[2,128,1024]{2,1,0:T(8,128)(2,1)S(1)}, bf16[2,128,1024]{2,1,0:T(8,128)(2,1)S(1)}, u32[]{:S(2)}, u32[]{:S(2)}) collective-permute-start(bf16[2,128,1024]{2,1,0:T(8,128)(2,1)S(1)} %pad_maximum_fusion), channel_id=1, source_target_pairs={{0,4},{4,0},{8,12},{12,8},{16,20},{20,16},{24,28},{28,24},{1,5},{5... | collective-permute-start | bytes 1572872 | tf_op jit(solution)/shard_map/ppermute | solution.py:222
  23.7 0.0 collective-permute-done.4.refs_0_
  23.7 0.0 copy-done.1
  23.7 6.1 %rim.1 = (f32[256,1024]{1,0:T(8,128)S(1)}, f32[256,1024]{1,0:T(8,128)S(1)}, f32[256,1024]{1,0:T(8,128)S(1)}) custom-call(s32[1,2,8]{2,1,0:T(2,128)S(1)} %copy-done.4, bf16[2,128,1024]{2,1,0:T(8,128)(2,1)S(1)} %collective-permute-done.4.refs_0_, ...), custom_call_target="tpu_custom_call", output_to_operand_aliasing={{0}: (5, {}), {1}: (6, {}), {2}: (7, {})} | custom-call | tf_op jit(solution)/shard_map/rim/pallas_call | solution.py:190
  29.8 0.0 collective-permute-done.3.refs_2_
  29.8 0.0 collective-permute-done.2.refs_1_
  29.8 1.3 %collective-permute-start.6 = (bf16[1,128,1024]{2,1,0:T(8,128)(2,1)S(1)}, bf16[1,128,1024]{2,1,0:T(8,128)(2,1)S(1)}, u32[]{:S(2)}, u32[]{:S(2)}) collective-permute-start(bf16[1,128,1024]{2,1,0:T(8,128)(2,1)S(1)} %get-tuple-element.30.refs_2_), channel_id=1, source_target_pairs={{0,1},{1,0},{2,3},{3,2},{4,5},{5,4},{6,7},{7,6},{8,9},{9,8},{10,11... | collective-permute-start | bytes 786440 | tf_op jit(solution)/shard_map/ppermute | solution.py:281
  31.1 0.8 %collective-permute-start.7 = (bf16[1,128,1024]{2,1,0:T(8,128)(2,1)S(1)}, bf16[1,128,1024]{2,1,0:T(8,128)(2,1)S(1)}, u32[]{:S(2)}, u32[]{:S(2)}) collective-permute-start(bf16[1,128,1024]{2,1,0:T(8,128)(2,1)S(1)} %get-tuple-element.31.refs_3_), channel_id=1, source_target_pairs={{0,1},{1,0},{2,3},{3,2},{4,5},{5,4},{6,7},{7,6},{8,9},{9,8},{10,11... | collective-permute-start | bytes 786440 | tf_op jit(solution)/shard_map/ppermute | solution.py:282
  31.9 6.1 %lon.1 = (f32[256,1024]{1,0:T(8,128)S(1)}, f32[256,1024]{1,0:T(8,128)S(1)}, f32[256,1024]{1,0:T(8,128)S(1)}) custom-call(s32[1,2,8]{2,1,0:T(2,128)S(1)} %copy-done.4, bf16[1,128,1024]{2,1,0:T(8,128)(2,1)S(1)} %get-tuple-element.32.refs_0_, ...), custom_call_target="tpu_custom_call", output_to_operand_aliasing={{0}: (7, {}), {1}: (8, {}), {2}: (9, {})} | custom-call | tf_op jit(solution)/shard_map/lon/pallas_call | solution.py:190
  38.0 0.0 copy-start.2
  38.0 0.0 collective-permute-done.9.refs_1_
  38.0 0.0 collective-permute-done.8.refs_0_
  38.0 4.8 %corner.1 = (f32[256,1024]{1,0:T(8,128)S(1)}, f32[256,1024]{1,0:T(8,128)S(1)}, f32[256,1024]{1,0:T(8,128)S(1)}) custom-call(s32[1,2,8]{2,1,0:T(2,128)S(1)} %copy-done.4, bf16[2,128,1024]{2,1,0:T(8,128)(2,1)S(1)} %collective-permute-done.8.refs_0_, ...), custom_call_target="tpu_custom_call", output_to_operand_aliasing={{0}: (5, {}), {1}: (6, {}), {2}: (7, {})} | custom-call | tf_op jit(solution)/shard_map/corner/pallas_call | solution.py:190
  42.9 0.0 collective-permute-done.6.refs_0_
  42.9 0.8 %collective-permute-done.7.refs_1_ = bf16[1,128,1024]{2,1,0:T(8,128)(2,1)S(1)} collective-permute-done((bf16[1,128,1024]{2,1,0:T(8,128)(2,1)S(1)}, bf16[1,128,1024]{2,1,0:T(8,128)(2,1)S(1)}, u32[]{:S(2)}, u32[]{:S(2)}) %collective-permute-start.7) | collective-permute-done | bytes 262176 | tf_op jit(solution)/shard_map/ppermute | solution.py:282
  43.7 0.0 copy-done.2
  43.7 4.9 %across.1 = (bf16[256,1024]{1,0:T(8,128)(2,1)}, f32[256,1024]{1,0:T(8,128)S(1)}, f32[256,1024]{1,0:T(8,128)S(1)}, f32[256,1024]{1,0:T(8,128)S(1)}) custom-call(s32[1,2,8]{2,1,0:T(2,128)S(1)} %copy-done.4, bf16[1,128,1024]{2,1,0:T(8,128)(2,1)S(1)} %collective-permute-done.6.refs_0_, ...), custom_call_target="tpu_custom_call", output_to_operand_aliasing={{1}: (6, {}), {2}: (7, {}), {3}: (8, {})} | custom-call | tf_op jit(solution)/shard_map/across/pallas_call | solution.py:190
  (3 shorter events, 0.0 us)
Async XLA Ops:
  1.1 16.2 %collective-permute-start.1 = (bf16[1,128,1024]{2,1,0:T(8,128)(2,1)S(1)}, bf16[1,128,1024]{2,1,0:T(8,128)(2,1)S(1)}, u32[]{:S(2)}, u32[]{:S(2)}) collective-permute-start(bf16[1,128,1024]{2,1,0:T(8,128)(2,1)S(1)} %get-tuple-element.45), channel_id=1, source_target_pairs={{0,3},{3,0},{1,2},{2,1},{4,7},{7,4},{5,6},{6,5},{8,11},{11,8},{9,1... | collective-permute-start | bytes 786440 | tf_op jit(solution)/shard_map/ppermute | solution.py:271
  6.2 13.6 %collective-permute-start = (bf16[1,128,1024]{2,1,0:T(8,128)(2,1)S(1)}, bf16[1,128,1024]{2,1,0:T(8,128)(2,1)S(1)}, u32[]{:S(2)}, u32[]{:S(2)}) collective-permute-start(bf16[1,128,1024]{2,1,0:T(8,128)(2,1)S(1)} %get-tuple-element.46), channel_id=1, source_target_pairs={{0,1},{1,0},{2,3},{3,2},{4,5},{5,4},{6,7},{7,6},{8,9},{9,8},{10,11... | collective-permute-start | bytes 786440 | tf_op jit(solution)/shard_map/ppermute | solution.py:270
  6.2 14.6 %collective-permute-start.5 = (bf16[2,128,1024]{2,1,0:T(8,128)(2,1)}, bf16[2,128,1024]{2,1,0:T(8,128)(2,1)S(1)}, u32[]{:S(2)}, u32[]{:S(2)}) collective-permute-start(bf16[2,128,1024]{2,1,0:T(8,128)(2,1)} %bitcast.6), channel_id=1, source_target_pairs={{4,8},{8,4},{12,16},{16,12},{20,24},{24,20},{5,9},{9,5},{13,17},{1... | collective-permute-start | bytes 1572872 | tf_op jit(solution)/shard_map/ppermute | solution.py:222
  6.9 22.9 %collective-permute-start.3 = (bf16[1,128,1024]{2,1,0:T(8,128)(2,1)S(1)}, bf16[1,128,1024]{2,1,0:T(8,128)(2,1)S(1)}, u32[]{:S(2)}, u32[]{:S(2)}) collective-permute-start(bf16[1,128,1024]{2,1,0:T(8,128)(2,1)S(1)} %get-tuple-element.45), channel_id=1, source_target_pairs={{0,1},{1,0},{2,3},{3,2},{4,5},{5,4},{6,7},{7,6},{8,9},{9,8},{10,11... | collective-permute-start | bytes 786440 | tf_op jit(solution)/shard_map/ppermute | solution.py:274
  9.0 20.8 %collective-permute-start.2 = (bf16[1,128,1024]{2,1,0:T(8,128)(2,1)S(1)}, bf16[1,128,1024]{2,1,0:T(8,128)(2,1)S(1)}, u32[]{:S(2)}, u32[]{:S(2)}) collective-permute-start(bf16[1,128,1024]{2,1,0:T(8,128)(2,1)S(1)} %get-tuple-element.46), channel_id=1, source_target_pairs={{0,3},{3,0},{1,2},{2,1},{4,7},{7,4},{5,6},{6,5},{8,11},{11,8},{9,1... | collective-permute-start | bytes 786440 | tf_op jit(solution)/shard_map/ppermute | solution.py:275
  9.0 2.8 %copy-start = (bf16[1024,3072]{1,0:T(8,128)(2,1)S(1)}, bf16[1024,3072]{1,0:T(8,128)(2,1)}, u32[]{:S(2)}) copy-start(bf16[1024,3072]{1,0:T(8,128)(2,1)} %refs_3_.5) | copy-start | bytes 18874372
  11.8 1.0 %copy-start.3 = (bf16[1,2,128,1024]{3,2,1,0:T(8,128)(2,1)S(1)}, bf16[1,2,128,1024]{3,2,1,0:T(8,128)(2,1)}, u32[]{:S(2)}) copy-start(bf16[1,2,128,1024]{3,2,1,0:T(8,128)(2,1)} %param.4) | copy-start | bytes 1572868
  12.9 0.7 %copy-start.4 = (s32[1,2,8]{2,1,0:T(2,128)S(1)}, s32[1,2,8]{2,1,0:T(2,128)}, u32[]{:S(2)}) copy-start(s32[1,2,8]{2,1,0:T(2,128)} %tele_ref.9) | copy-start | bytes 196
  13.6 10.1 %copy-start.1 = (bf16[1024,3072]{1,0:T(8,128)(2,1)S(1)}, bf16[1024,3072]{1,0:T(8,128)(2,1)}, u32[]{:S(2)}) copy-start(bf16[1024,3072]{1,0:T(8,128)(2,1)} %refs_3_.5) | copy-start | bytes 18874372
  17.2 6.4 %collective-permute-start.4 = (bf16[2,128,1024]{2,1,0:T(8,128)(2,1)S(1)}, bf16[2,128,1024]{2,1,0:T(8,128)(2,1)S(1)}, u32[]{:S(2)}, u32[]{:S(2)}) collective-permute-start(bf16[2,128,1024]{2,1,0:T(8,128)(2,1)S(1)} %bitcast.8), channel_id=1, source_target_pairs={{0,4},{4,0},{8,12},{12,8},{16,20},{20,16},{24,28},{28,24},{1,5},{5... | collective-permute-start | bytes 1572872 | tf_op jit(solution)/shard_map/ppermute | solution.py:222
  19.9 18.1 %collective-permute-start.9 = (bf16[2,128,1024]{2,1,0:T(8,128)(2,1)S(1)}, bf16[2,128,1024]{2,1,0:T(8,128)(2,1)S(1)}, u32[]{:S(2)}, u32[]{:S(2)}) collective-permute-start(bf16[2,128,1024]{2,1,0:T(8,128)(2,1)S(1)} %pad_maximum_fusion), channel_id=1, source_target_pairs={{4,8},{8,4},{12,16},{16,12},{20,24},{24,20},{5,9},{9,5},{13,17},{1... | collective-permute-start | bytes 1572872 | tf_op jit(solution)/shard_map/ppermute | solution.py:222
  20.8 17.3 %collective-permute-start.8 = (bf16[2,128,1024]{2,1,0:T(8,128)(2,1)S(1)}, bf16[2,128,1024]{2,1,0:T(8,128)(2,1)S(1)}, u32[]{:S(2)}, u32[]{:S(2)}) collective-permute-start(bf16[2,128,1024]{2,1,0:T(8,128)(2,1)S(1)} %pad_maximum_fusion), channel_id=1, source_target_pairs={{0,4},{4,0},{8,12},{12,8},{16,20},{20,16},{24,28},{28,24},{1,5},{5... | collective-permute-start | bytes 1572872 | tf_op jit(solution)/shard_map/ppermute | solution.py:222
  29.8 13.1 %collective-permute-start.6 = (bf16[1,128,1024]{2,1,0:T(8,128)(2,1)S(1)}, bf16[1,128,1024]{2,1,0:T(8,128)(2,1)S(1)}, u32[]{:S(2)}, u32[]{:S(2)}) collective-permute-start(bf16[1,128,1024]{2,1,0:T(8,128)(2,1)S(1)} %get-tuple-element.30.refs_2_), channel_id=1, source_target_pairs={{0,1},{1,0},{2,3},{3,2},{4,5},{5,4},{6,7},{7,6},{8,9},{9,8},{10,11... | collective-permute-start | bytes 786440 | tf_op jit(solution)/shard_map/ppermute | solution.py:281
  31.1 12.6 %collective-permute-start.7 = (bf16[1,128,1024]{2,1,0:T(8,128)(2,1)S(1)}, bf16[1,128,1024]{2,1,0:T(8,128)(2,1)S(1)}, u32[]{:S(2)}, u32[]{:S(2)}) collective-permute-start(bf16[1,128,1024]{2,1,0:T(8,128)(2,1)S(1)} %get-tuple-element.31.refs_3_), channel_id=1, source_target_pairs={{0,1},{1,0},{2,3},{3,2},{4,5},{5,4},{6,7},{7,6},{8,9},{9,8},{10,11... | collective-permute-start | bytes 786440 | tf_op jit(solution)/shard_map/ppermute | solution.py:282
  38.0 5.7 %copy-start.2 = (bf16[1024,1024]{1,0:T(8,128)(2,1)S(1)}, bf16[1024,1024]{1,0:T(8,128)(2,1)}, u32[]{:S(2)}) copy-start(bf16[1024,1024]{1,0:T(8,128)(2,1)} %refs_4_.1) | copy-start | bytes 6291460

commit v5 on v4

--- a/solution.py
+++ b/solution.py
@@ -13,6 +13,7 @@
 NEG = -1e30
 CW = 1024
 VM = 24
+FIRST_VM = 46
 COST = 0
 UNIT = 1.4426950408889634 * HD ** -0.5
 
@@ -191,7 +192,7 @@
         functools.partial(attend_kernel, gather, users, len(xs), kind, place),
         in_specs=[SMEM] + [VMEM] * (len(args) - 1), out_specs=[VMEM] * len(out_shape), out_shape=out_shape,
         input_output_aliases=aliases, scratch_shapes=scratch, name=name,
-        compiler_params=pltpu.CompilerParams(vmem_limit_bytes=VM * 1024 * 1024),
+        compiler_params=pltpu.CompilerParams(vmem_limit_bytes=(FIRST_VM if kind == "first" else VM) * 1024 * 1024),
         cost_estimate=pl.CostEstimate(flops=spent, bytes_accessed=0, transcendentals=0),
     )(*args)
 

time: 48.9 us -> 48.6 us (level)
  local copies, waits for them, and re-layouts: 4.51 us -> 1.73 us
  Pallas kernels: 25.7 us -> 27.9 us
    unnamed x10 -> x8, local copies, waits for them, and re-layouts: 4.51 us -> 1.73 us
    pallas_call x5, Pallas kernels: 25.7 us -> 27.9 us  [attend(): pl.pallas_call(functools.partial(attend_kernel, gather, users, len(xs), k...]
  transfers between devices with their start and end apart: 10 -> 10, of which waited for: 1 -> 2; matrix products, arithmetic and copies ran while one was open for 0% -> 0% of each run, Pallas kernels for 43% -> 47%
where the time goes in v5:
time: 48.6 us; the launch traced here: 48.3 us
  Pallas kernels  27.9 us (57%)
  starting transfers between devices  16.3 us (34%)
  local copies, waits for them, and re-layouts  1.73 us (4%)
  other arithmetic  1.31 us (3%)
  waiting for transfers between devices  0.99 us (2%)
    pallas_call x5, Pallas kernels, attend(): pl.pallas_call(functools.partial(attend_kernel, gather, users, len(xs), k...  27.9 us
    ppermute x4, starting transfers between devices, lat_swap(): return (lax.ppermute(array, 'lat', same), lax.ppermute(array, 'lat', other))  6.97 us
    ppermute x1, starting transfers between devices, on_device(): ring_edge = lax.ppermute(outer, 'lon', ring_pairs)  5.11 us
    ppermute x1, starting transfers between devices, on_device(): near_rest = lax.ppermute(outer, 'lon', near_pairs)  2.09 us
    unnamed x8, local copies, waits for them, and re-layouts  1.73 us
    ppermute x1, starting transfers between devices, on_device(): far_edge = lax.ppermute(ring_edge, 'lon', near_pairs)  1.65 us
    select_n x1, other arithmetic, on_device(): jnp.where(even, x[:1], x[1:])  1.22 us
  transfers between devices with their start and end apart: 10, of which 2 were waited for; matrix products, arithmetic and copies ran while one was open for 0% of the time, Pallas kernels for 47%

profile of v5, /device:TPU:0, one launch (start us, length us, event | category | flops | bytes accessed | tf_op | source)
XLA Modules:
  0.0 48.3 jit_solution(13705457128070101071)
XLA Ops:
  0.0 0.0 copy-start
  0.0 1.2 %select_bitcast_fusion = (bf16[1,128,1024]{2,1,0:T(8,128)(2,1)S(1)}, bf16[1,128,1024]{2,1,0:T(8,128)(2,1)S(1)}) fusion(pred[]{:T(512)S(6)} %eq.3, bf16[1,2,128,1024]{3,2,1,0:T(8,128)(2,1)} %param.4), kind=kLoop, calls=%fused_computation.1 | loop fusion | flops 262144 | bytes 1048577 | tf_op jit(solution)/shard_map/jit(_where)/select_n | solution.py:270
  1.2 5.1 %collective-permute-start.1 = (bf16[1,128,1024]{2,1,0:T(8,128)(2,1)S(1)}, bf16[1,128,1024]{2,1,0:T(8,128)(2,1)S(1)}, u32[]{:S(2)}, u32[]{:S(2)}) collective-permute-start(bf16[1,128,1024]{2,1,0:T(8,128)(2,1)S(1)} %get-tuple-element.45), channel_id=1, source_target_pairs={{0,3},{3,0},{1,2},{2,1},{4,7},{7,4},{5,6},{6,5},{8,11},{11,8},{9,1... | collective-permute-start | bytes 786440 | tf_op jit(solution)/shard_map/ppermute | solution.py:272
  6.3 0.0 collective-permute-start
  6.3 0.7 %collective-permute-start.5 = (bf16[2,128,1024]{2,1,0:T(8,128)(2,1)}, bf16[2,128,1024]{2,1,0:T(8,128)(2,1)S(1)}, u32[]{:S(2)}, u32[]{:S(2)}) collective-permute-start(bf16[2,128,1024]{2,1,0:T(8,128)(2,1)} %bitcast.6), channel_id=1, source_target_pairs={{4,8},{8,4},{12,16},{16,12},{20,24},{24,20},{5,9},{9,5},{13,17},{1... | collective-permute-start | bytes 1572872 | tf_op jit(solution)/shard_map/ppermute | solution.py:223
  7.0 2.1 %collective-permute-start.3 = (bf16[1,128,1024]{2,1,0:T(8,128)(2,1)S(1)}, bf16[1,128,1024]{2,1,0:T(8,128)(2,1)S(1)}, u32[]{:S(2)}, u32[]{:S(2)}) collective-permute-start(bf16[1,128,1024]{2,1,0:T(8,128)(2,1)S(1)} %get-tuple-element.45), channel_id=1, source_target_pairs={{0,1},{1,0},{2,3},{3,2},{4,5},{5,4},{6,7},{7,6},{8,9},{9,8},{10,11... | collective-permute-start | bytes 786440 | tf_op jit(solution)/shard_map/ppermute | solution.py:275
  9.1 0.1 collective-permute-start.2
  9.2 0.0 copy-start.2
  9.2 1.0 %copy-done.2 = bf16[1,2,128,1024]{3,2,1,0:T(8,128)(2,1)S(1)} copy-done((bf16[1,2,128,1024]{3,2,1,0:T(8,128)(2,1)S(1)}, bf16[1,2,128,1024]{3,2,1,0:T(8,128)(2,1)}, u32[]{:S(2)}) %copy-start.2) | copy-done | bytes 524312
  10.2 0.0 copy-start.3
  10.2 0.7 %copy-done.3 = s32[1,2,8]{2,1,0:T(2,128)S(1)} copy-done((s32[1,2,8]{2,1,0:T(2,128)S(1)}, s32[1,2,8]{2,1,0:T(2,128)}, u32[]{:S(2)}) %copy-start.3) | copy-done | bytes 88
  10.9 5.9 %own.1 = (bf16[256,1024]{1,0:T(8,128)(2,1)S(1)}, f32[256,1024]{1,0:T(8,128)S(1)}, f32[256,1024]{1,0:T(8,128)S(1)}, f32[256,1024]{1,0:T(8,128)S(1)}) custom-call(s32[1,2,8]{2,1,0:T(2,128)S(1)} %copy-done.3, bf16[2,128,1024]{2,1,0:T(8,128)(2,1)S(1)} %bitcast.7, bf16[1024,3072]{1,0:T(8,128)(2,1)} %refs_3_.5), custom_call_target="tpu_custom_call" | custom-call | tf_op jit(solution)/shard_map/own/pallas_call | solution.py:191
  16.8 0.0 collective-permute-done.1.refs_1_
  16.8 2.5 %collective-permute-start.4 = (bf16[2,128,1024]{2,1,0:T(8,128)(2,1)S(1)}, bf16[2,128,1024]{2,1,0:T(8,128)(2,1)S(1)}, u32[]{:S(2)}, u32[]{:S(2)}) collective-permute-start(bf16[2,128,1024]{2,1,0:T(8,128)(2,1)S(1)} %bitcast.8), channel_id=1, source_target_pairs={{0,4},{4,0},{8,12},{12,8},{16,20},{20,16},{24,28},{28,24},{1,5},{5... | collective-permute-start | bytes 1572872 | tf_op jit(solution)/shard_map/ppermute | solution.py:223
  19.4 0.0 collective-permute-done.refs_0_
  19.4 0.1 pad_maximum_fusion
  19.5 0.9 %collective-permute-start.9 = (bf16[2,128,1024]{2,1,0:T(8,128)(2,1)S(1)}, bf16[2,128,1024]{2,1,0:T(8,128)(2,1)S(1)}, u32[]{:S(2)}, u32[]{:S(2)}) collective-permute-start(bf16[2,128,1024]{2,1,0:T(8,128)(2,1)S(1)} %pad_maximum_fusion), channel_id=1, source_target_pairs={{4,8},{8,4},{12,16},{16,12},{20,24},{24,20},{5,9},{9,5},{13,17},{1... | collective-permute-start | bytes 1572872 | tf_op jit(solution)/shard_map/ppermute | solution.py:223
  20.4 0.0 collective-permute-done.5.refs_1_
  20.4 2.9 %collective-permute-start.8 = (bf16[2,128,1024]{2,1,0:T(8,128)(2,1)S(1)}, bf16[2,128,1024]{2,1,0:T(8,128)(2,1)S(1)}, u32[]{:S(2)}, u32[]{:S(2)}) collective-permute-start(bf16[2,128,1024]{2,1,0:T(8,128)(2,1)S(1)} %pad_maximum_fusion), channel_id=1, source_target_pairs={{0,4},{4,0},{8,12},{12,8},{16,20},{20,16},{24,28},{28,24},{1,5},{5... | collective-permute-start | bytes 1572872 | tf_op jit(solution)/shard_map/ppermute | solution.py:223
  23.3 0.0 collective-permute-done.4.refs_0_
  23.3 0.0 copy-done
  23.3 6.1 %rim.1 = (f32[256,1024]{1,0:T(8,128)S(1)}, f32[256,1024]{1,0:T(8,128)S(1)}, f32[256,1024]{1,0:T(8,128)S(1)}) custom-call(s32[1,2,8]{2,1,0:T(2,128)S(1)} %copy-done.3, bf16[2,128,1024]{2,1,0:T(8,128)(2,1)S(1)} %collective-permute-done.4.refs_0_, ...), custom_call_target="tpu_custom_call", output_to_operand_aliasing={{0}: (5, {}), {1}: (6, {}), {2}: (7, {})} | custom-call | tf_op jit(solution)/shard_map/rim/pallas_call | solution.py:191
  29.4 0.0 collective-permute-done.3.refs_2_
  29.4 0.2 collective-permute-done.2.refs_1_
  29.6 1.6 %collective-permute-start.6 = (bf16[1,128,1024]{2,1,0:T(8,128)(2,1)S(1)}, bf16[1,128,1024]{2,1,0:T(8,128)(2,1)S(1)}, u32[]{:S(2)}, u32[]{:S(2)}) collective-permute-start(bf16[1,128,1024]{2,1,0:T(8,128)(2,1)S(1)} %get-tuple-element.30.refs_2_), channel_id=1, source_target_pairs={{0,1},{1,0},{2,3},{3,2},{4,5},{5,4},{6,7},{7,6},{8,9},{9,8},{10,11... | collective-permute-start | bytes 786440 | tf_op jit(solution)/shard_map/ppermute | solution.py:282
  31.2 0.4 collective-permute-start.7
  31.6 6.1 %lon.1 = (f32[256,1024]{1,0:T(8,128)S(1)}, f32[256,1024]{1,0:T(8,128)S(1)}, f32[256,1024]{1,0:T(8,128)S(1)}) custom-call(s32[1,2,8]{2,1,0:T(2,128)S(1)} %copy-done.3, bf16[1,128,1024]{2,1,0:T(8,128)(2,1)S(1)} %get-tuple-element.32.refs_0_, ...), custom_call_target="tpu_custom_call", output_to_operand_aliasing={{0}: (7, {}), {1}: (8, {}), {2}: (9, {})} | custom-call | tf_op jit(solution)/shard_map/lon/pallas_call | solution.py:191
  37.7 0.0 copy-start.1
  37.7 0.0 collective-permute-done.9.refs_1_
  37.8 0.0 collective-permute-done.8.refs_0_
  37.8 4.8 %corner.1 = (f32[256,1024]{1,0:T(8,128)S(1)}, f32[256,1024]{1,0:T(8,128)S(1)}, f32[256,1024]{1,0:T(8,128)S(1)}) custom-call(s32[1,2,8]{2,1,0:T(2,128)S(1)} %copy-done.3, bf16[2,128,1024]{2,1,0:T(8,128)(2,1)S(1)} %collective-permute-done.8.refs_0_, ...), custom_call_target="tpu_custom_call", output_to_operand_aliasing={{0}: (5, {}), {1}: (6, {}), {2}: (7, {})} | custom-call | tf_op jit(solution)/shard_map/corner/pallas_call | solution.py:191
  42.6 0.0 collective-permute-done.6.refs_0_
  42.6 0.8 %collective-permute-done.7.refs_1_ = bf16[1,128,1024]{2,1,0:T(8,128)(2,1)S(1)} collective-permute-done((bf16[1,128,1024]{2,1,0:T(8,128)(2,1)S(1)}, bf16[1,128,1024]{2,1,0:T(8,128)(2,1)S(1)}, u32[]{:S(2)}, u32[]{:S(2)}) %collective-permute-start.7) | collective-permute-done | bytes 262176 | tf_op jit(solution)/shard_map/ppermute | solution.py:283
  43.4 0.0 copy-done.1
  43.4 5.0 %across.1 = (bf16[256,1024]{1,0:T(8,128)(2,1)}, f32[256,1024]{1,0:T(8,128)S(1)}, f32[256,1024]{1,0:T(8,128)S(1)}, f32[256,1024]{1,0:T(8,128)S(1)}) custom-call(s32[1,2,8]{2,1,0:T(2,128)S(1)} %copy-done.3, bf16[1,128,1024]{2,1,0:T(8,128)(2,1)S(1)} %collective-permute-done.6.refs_0_, ...), custom_call_target="tpu_custom_call", output_to_operand_aliasing={{1}: (6, {}), {2}: (7, {}), {3}: (8, {})} | custom-call | tf_op jit(solution)/shard_map/across/pallas_call | solution.py:191
  (3 shorter events, 0.0 us)
Async XLA Ops:
  0.0 23.3 %copy-start = (bf16[1024,3072]{1,0:T(8,128)(2,1)S(1)}, bf16[1024,3072]{1,0:T(8,128)(2,1)}, u32[]{:S(2)}) copy-start(bf16[1024,3072]{1,0:T(8,128)(2,1)} %refs_3_.5) | copy-start | bytes 18874372
  1.2 15.6 %collective-permute-start.1 = (bf16[1,128,1024]{2,1,0:T(8,128)(2,1)S(1)}, bf16[1,128,1024]{2,1,0:T(8,128)(2,1)S(1)}, u32[]{:S(2)}, u32[]{:S(2)}) collective-permute-start(bf16[1,128,1024]{2,1,0:T(8,128)(2,1)S(1)} %get-tuple-element.45), channel_id=1, source_target_pairs={{0,3},{3,0},{1,2},{2,1},{4,7},{7,4},{5,6},{6,5},{8,11},{11,8},{9,1... | collective-permute-start | bytes 786440 | tf_op jit(solution)/shard_map/ppermute | solution.py:272
  6.3 13.0 %collective-permute-start = (bf16[1,128,1024]{2,1,0:T(8,128)(2,1)S(1)}, bf16[1,128,1024]{2,1,0:T(8,128)(2,1)S(1)}, u32[]{:S(2)}, u32[]{:S(2)}) collective-permute-start(bf16[1,128,1024]{2,1,0:T(8,128)(2,1)S(1)} %get-tuple-element.46), channel_id=1, source_target_pairs={{0,1},{1,0},{2,3},{3,2},{4,5},{5,4},{6,7},{7,6},{8,9},{9,8},{10,11... | collective-permute-start | bytes 786440 | tf_op jit(solution)/shard_map/ppermute | solution.py:271
  6.3 14.0 %collective-permute-start.5 = (bf16[2,128,1024]{2,1,0:T(8,128)(2,1)}, bf16[2,128,1024]{2,1,0:T(8,128)(2,1)S(1)}, u32[]{:S(2)}, u32[]{:S(2)}) collective-permute-start(bf16[2,128,1024]{2,1,0:T(8,128)(2,1)} %bitcast.6), channel_id=1, source_target_pairs={{4,8},{8,4},{12,16},{16,12},{20,24},{24,20},{5,9},{9,5},{13,17},{1... | collective-permute-start | bytes 1572872 | tf_op jit(solution)/shard_map/ppermute | solution.py:223
  7.0 22.3 %collective-permute-start.3 = (bf16[1,128,1024]{2,1,0:T(8,128)(2,1)S(1)}, bf16[1,128,1024]{2,1,0:T(8,128)(2,1)S(1)}, u32[]{:S(2)}, u32[]{:S(2)}) collective-permute-start(bf16[1,128,1024]{2,1,0:T(8,128)(2,1)S(1)} %get-tuple-element.45), channel_id=1, source_target_pairs={{0,1},{1,0},{2,3},{3,2},{4,5},{5,4},{6,7},{7,6},{8,9},{9,8},{10,11... | collective-permute-start | bytes 786440 | tf_op jit(solution)/shard_map/ppermute | solution.py:275
  9.1 20.5 %collective-permute-start.2 = (bf16[1,128,1024]{2,1,0:T(8,128)(2,1)S(1)}, bf16[1,128,1024]{2,1,0:T(8,128)(2,1)S(1)}, u32[]{:S(2)}, u32[]{:S(2)}) collective-permute-start(bf16[1,128,1024]{2,1,0:T(8,128)(2,1)S(1)} %get-tuple-element.46), channel_id=1, source_target_pairs={{0,3},{3,0},{1,2},{2,1},{4,7},{7,4},{5,6},{6,5},{8,11},{11,8},{9,1... | collective-permute-start | bytes 786440 | tf_op jit(solution)/shard_map/ppermute | solution.py:276
  9.2 1.0 %copy-start.2 = (bf16[1,2,128,1024]{3,2,1,0:T(8,128)(2,1)S(1)}, bf16[1,2,128,1024]{3,2,1,0:T(8,128)(2,1)}, u32[]{:S(2)}) copy-start(bf16[1,2,128,1024]{3,2,1,0:T(8,128)(2,1)} %param.4) | copy-start | bytes 1572868
  10.2 0.7 %copy-start.3 = (s32[1,2,8]{2,1,0:T(2,128)S(1)}, s32[1,2,8]{2,1,0:T(2,128)}, u32[]{:S(2)}) copy-start(s32[1,2,8]{2,1,0:T(2,128)} %tele_ref.9) | copy-start | bytes 196
  16.8 6.4 %collective-permute-start.4 = (bf16[2,128,1024]{2,1,0:T(8,128)(2,1)S(1)}, bf16[2,128,1024]{2,1,0:T(8,128)(2,1)S(1)}, u32[]{:S(2)}, u32[]{:S(2)}) collective-permute-start(bf16[2,128,1024]{2,1,0:T(8,128)(2,1)S(1)} %bitcast.8), channel_id=1, source_target_pairs={{0,4},{4,0},{8,12},{12,8},{16,20},{20,16},{24,28},{28,24},{1,5},{5... | collective-permute-start | bytes 1572872 | tf_op jit(solution)/shard_map/ppermute | solution.py:223
  19.5 18.3 %collective-permute-start.9 = (bf16[2,128,1024]{2,1,0:T(8,128)(2,1)S(1)}, bf16[2,128,1024]{2,1,0:T(8,128)(2,1)S(1)}, u32[]{:S(2)}, u32[]{:S(2)}) collective-permute-start(bf16[2,128,1024]{2,1,0:T(8,128)(2,1)S(1)} %pad_maximum_fusion), channel_id=1, source_target_pairs={{4,8},{8,4},{12,16},{16,12},{20,24},{24,20},{5,9},{9,5},{13,17},{1... | collective-permute-start | bytes 1572872 | tf_op jit(solution)/shard_map/ppermute | solution.py:223
  20.4 17.4 %collective-permute-start.8 = (bf16[2,128,1024]{2,1,0:T(8,128)(2,1)S(1)}, bf16[2,128,1024]{2,1,0:T(8,128)(2,1)S(1)}, u32[]{:S(2)}, u32[]{:S(2)}) collective-permute-start(bf16[2,128,1024]{2,1,0:T(8,128)(2,1)S(1)} %pad_maximum_fusion), channel_id=1, source_target_pairs={{0,4},{4,0},{8,12},{12,8},{16,20},{20,16},{24,28},{28,24},{1,5},{5... | collective-permute-start | bytes 1572872 | tf_op jit(solution)/shard_map/ppermute | solution.py:223
  29.6 13.0 %collective-permute-start.6 = (bf16[1,128,1024]{2,1,0:T(8,128)(2,1)S(1)}, bf16[1,128,1024]{2,1,0:T(8,128)(2,1)S(1)}, u32[]{:S(2)}, u32[]{:S(2)}) collective-permute-start(bf16[1,128,1024]{2,1,0:T(8,128)(2,1)S(1)} %get-tuple-element.30.refs_2_), channel_id=1, source_target_pairs={{0,1},{1,0},{2,3},{3,2},{4,5},{5,4},{6,7},{7,6},{8,9},{9,8},{10,11... | collective-permute-start | bytes 786440 | tf_op jit(solution)/shard_map/ppermute | solution.py:282
  31.2 12.1 %collective-permute-start.7 = (bf16[1,128,1024]{2,1,0:T(8,128)(2,1)S(1)}, bf16[1,128,1024]{2,1,0:T(8,128)(2,1)S(1)}, u32[]{:S(2)}, u32[]{:S(2)}) collective-permute-start(bf16[1,128,1024]{2,1,0:T(8,128)(2,1)S(1)} %get-tuple-element.31.refs_3_), channel_id=1, source_target_pairs={{0,1},{1,0},{2,3},{3,2},{4,5},{5,4},{6,7},{7,6},{8,9},{9,8},{10,11... | collective-permute-start | bytes 786440 | tf_op jit(solution)/shard_map/ppermute | solution.py:283
  37.7 5.6 %copy-start.1 = (bf16[1024,1024]{1,0:T(8,128)(2,1)S(1)}, bf16[1024,1024]{1,0:T(8,128)(2,1)}, u32[]{:S(2)}) copy-start(bf16[1024,1024]{1,0:T(8,128)(2,1)} %refs_4_.1) | copy-start | bytes 6291460

commit v6 on v5

--- a/solution.py
+++ b/solution.py
@@ -142,7 +142,7 @@
     if kind == "first":
         w, q_ref, o_ref, m_ref, l_ref = refs
     elif kind == "last":
-        q_ref, w, w_out, o_in, m_in, l_in, out_ref, o_ref, m_ref, l_ref, att = refs
+        q_ref, w, w_out, o_in, m_in, l_in, out_ref, o_ref, m_ref, l_ref, att, mixed, out_sems = refs
     else:
         q_ref, w, o_in, m_in, l_in, o_ref, m_ref, l_ref = refs
 
@@ -160,7 +160,14 @@
 
     groups(width, body)
     if kind == "last":
-        out_ref[...] = jnp.dot(att[...], w_out[...], preferred_element_type=jnp.float32).astype(jnp.bfloat16)
+        copies = []
+        for k in range(2):
+            part = slice(k * width // 2, (k + 1) * width // 2)
+            mixed[:, part] = jnp.dot(att[...], w_out[:, part], preferred_element_type=jnp.float32).astype(jnp.bfloat16)
+            copies.append(pltpu.make_async_copy(mixed.at[:, part], out_ref.at[:, part], out_sems.at[k]))
+            copies[k].start()
+        for copy in copies:
+            copy.wait()
 
 
 SMEM = pl.BlockSpec(memory_space=pltpu.SMEM)
@@ -186,11 +193,11 @@
         out_shape = ([q_shape] if kind == "last" else []) + out_shape
         aliases = {len(args) - 3 + k: len(out_shape) - 3 + k for k in range(3)}
         if kind == "last":
-            scratch = [pltpu.VMEM((2 * BLOCK, width), jnp.bfloat16)]
+            scratch = [pltpu.VMEM((2 * BLOCK, width), jnp.bfloat16)] * 2 + [pltpu.SemaphoreType.DMA((2,))]
     spent = tiles * COST
     return pl.pallas_call(
         functools.partial(attend_kernel, gather, users, len(xs), kind, place),
-        in_specs=[SMEM] + [VMEM] * (len(args) - 1), out_specs=[VMEM] * len(out_shape), out_shape=out_shape,
+        in_specs=[SMEM] + [VMEM] * (len(args) - 1), out_specs=([pl.BlockSpec(memory_space=pl.ANY)] if kind == "last" else [VMEM]) + [VMEM] * (len(out_shape) - 1), out_shape=out_shape,
         input_output_aliases=aliases, scratch_shapes=scratch, name=name,
         compiler_params=pltpu.CompilerParams(vmem_limit_bytes=(FIRST_VM if kind == "first" else VM) * 1024 * 1024),
         cost_estimate=pl.CostEstimate(flops=spent, bytes_accessed=0, transcendentals=0),

time: 48.6 us -> 48.7 us (level)
  no operation moved by 1% of the time
where the time goes in v6:
time: 48.7 us; the launch traced here: 48.4 us
  Pallas kernels  27.8 us (57%)
  starting transfers between devices  16.3 us (33%)
  local copies, waits for them, and re-layouts  1.73 us (4%)
  other arithmetic  1.31 us (3%)
  waiting for transfers between devices  0.99 us (2%)
    pallas_call x5, Pallas kernels, attend(): pl.pallas_call(functools.partial(attend_kernel, gather, users, len(xs), k...  27.8 us
    ppermute x4, starting transfers between devices, lat_swap(): return (lax.ppermute(array, 'lat', same), lax.ppermute(array, 'lat', other))  6.97 us
    ppermute x1, starting transfers between devices, on_device(): ring_edge = lax.ppermute(outer, 'lon', ring_pairs)  5.11 us
    ppermute x1, starting transfers between devices, on_device(): near_rest = lax.ppermute(outer, 'lon', near_pairs)  2.09 us
    unnamed x8, local copies, waits for them, and re-layouts  1.73 us
    ppermute x1, starting transfers between devices, on_device(): far_edge = lax.ppermute(ring_edge, 'lon', near_pairs)  1.65 us
    select_n x1, other arithmetic, on_device(): jnp.where(even, x[:1], x[1:])  1.22 us
  transfers between devices with their start and end apart: 10, of which 2 were waited for; matrix products, arithmetic and copies ran while one was open for 0% of the time, Pallas kernels for 47%

profile of v6, /device:TPU:0, one launch (start us, length us, event | category | flops | bytes accessed | tf_op | source)
XLA Modules:
  0.0 48.4 jit_solution(1671849714419574094)
XLA Ops:
  0.0 0.0 copy-start
  0.0 1.2 %select_bitcast_fusion = (bf16[1,128,1024]{2,1,0:T(8,128)(2,1)S(1)}, bf16[1,128,1024]{2,1,0:T(8,128)(2,1)S(1)}) fusion(pred[]{:T(512)S(6)} %eq.3, bf16[1,2,128,1024]{3,2,1,0:T(8,128)(2,1)} %param.4), kind=kLoop, calls=%fused_computation.1 | loop fusion | flops 262144 | bytes 1048577 | tf_op jit(solution)/shard_map/jit(_where)/select_n | solution.py:277
  1.2 5.1 %collective-permute-start.1 = (bf16[1,128,1024]{2,1,0:T(8,128)(2,1)S(1)}, bf16[1,128,1024]{2,1,0:T(8,128)(2,1)S(1)}, u32[]{:S(2)}, u32[]{:S(2)}) collective-permute-start(bf16[1,128,1024]{2,1,0:T(8,128)(2,1)S(1)} %get-tuple-element.45), channel_id=1, source_target_pairs={{0,3},{3,0},{1,2},{2,1},{4,7},{7,4},{5,6},{6,5},{8,11},{11,8},{9,1... | collective-permute-start | bytes 786440 | tf_op jit(solution)/shard_map/ppermute | solution.py:279
  6.3 0.0 collective-permute-start
  6.3 0.7 %collective-permute-start.5 = (bf16[2,128,1024]{2,1,0:T(8,128)(2,1)}, bf16[2,128,1024]{2,1,0:T(8,128)(2,1)S(1)}, u32[]{:S(2)}, u32[]{:S(2)}) collective-permute-start(bf16[2,128,1024]{2,1,0:T(8,128)(2,1)} %bitcast.6), channel_id=1, source_target_pairs={{4,8},{8,4},{12,16},{16,12},{20,24},{24,20},{5,9},{9,5},{13,17},{1... | collective-permute-start | bytes 1572872 | tf_op jit(solution)/shard_map/ppermute | solution.py:230
  7.0 2.1 %collective-permute-start.3 = (bf16[1,128,1024]{2,1,0:T(8,128)(2,1)S(1)}, bf16[1,128,1024]{2,1,0:T(8,128)(2,1)S(1)}, u32[]{:S(2)}, u32[]{:S(2)}) collective-permute-start(bf16[1,128,1024]{2,1,0:T(8,128)(2,1)S(1)} %get-tuple-element.45), channel_id=1, source_target_pairs={{0,1},{1,0},{2,3},{3,2},{4,5},{5,4},{6,7},{7,6},{8,9},{9,8},{10,11... | collective-permute-start | bytes 786440 | tf_op jit(solution)/shard_map/ppermute | solution.py:282
  9.1 0.1 collective-permute-start.2
  9.2 0.0 copy-start.2
  9.2 1.0 %copy-done.2 = bf16[1,2,128,1024]{3,2,1,0:T(8,128)(2,1)S(1)} copy-done((bf16[1,2,128,1024]{3,2,1,0:T(8,128)(2,1)S(1)}, bf16[1,2,128,1024]{3,2,1,0:T(8,128)(2,1)}, u32[]{:S(2)}) %copy-start.2) | copy-done | bytes 524312
  10.2 0.0 copy-start.3
  10.2 0.7 %copy-done.3 = s32[1,2,8]{2,1,0:T(2,128)S(1)} copy-done((s32[1,2,8]{2,1,0:T(2,128)S(1)}, s32[1,2,8]{2,1,0:T(2,128)}, u32[]{:S(2)}) %copy-start.3) | copy-done | bytes 88
  10.9 5.9 %own.1 = (bf16[256,1024]{1,0:T(8,128)(2,1)S(1)}, f32[256,1024]{1,0:T(8,128)S(1)}, f32[256,1024]{1,0:T(8,128)S(1)}, f32[256,1024]{1,0:T(8,128)S(1)}) custom-call(s32[1,2,8]{2,1,0:T(2,128)S(1)} %copy-done.3, bf16[2,128,1024]{2,1,0:T(8,128)(2,1)S(1)} %bitcast.7, bf16[1024,3072]{1,0:T(8,128)(2,1)} %refs_3_.5), custom_call_target="tpu_custom_call" | custom-call | tf_op jit(solution)/shard_map/own/pallas_call | solution.py:198
  16.8 0.0 collective-permute-done.1.refs_1_
  16.8 2.5 %collective-permute-start.4 = (bf16[2,128,1024]{2,1,0:T(8,128)(2,1)S(1)}, bf16[2,128,1024]{2,1,0:T(8,128)(2,1)S(1)}, u32[]{:S(2)}, u32[]{:S(2)}) collective-permute-start(bf16[2,128,1024]{2,1,0:T(8,128)(2,1)S(1)} %bitcast.8), channel_id=1, source_target_pairs={{0,4},{4,0},{8,12},{12,8},{16,20},{20,16},{24,28},{28,24},{1,5},{5... | collective-permute-start | bytes 1572872 | tf_op jit(solution)/shard_map/ppermute | solution.py:230
  19.4 0.0 collective-permute-done.refs_0_
  19.4 0.1 pad_maximum_fusion
  19.5 0.9 %collective-permute-start.9 = (bf16[2,128,1024]{2,1,0:T(8,128)(2,1)S(1)}, bf16[2,128,1024]{2,1,0:T(8,128)(2,1)S(1)}, u32[]{:S(2)}, u32[]{:S(2)}) collective-permute-start(bf16[2,128,1024]{2,1,0:T(8,128)(2,1)S(1)} %pad_maximum_fusion), channel_id=1, source_target_pairs={{4,8},{8,4},{12,16},{16,12},{20,24},{24,20},{5,9},{9,5},{13,17},{1... | collective-permute-start | bytes 1572872 | tf_op jit(solution)/shard_map/ppermute | solution.py:230
  20.4 0.0 collective-permute-done.5.refs_1_
  20.4 2.9 %collective-permute-start.8 = (bf16[2,128,1024]{2,1,0:T(8,128)(2,1)S(1)}, bf16[2,128,1024]{2,1,0:T(8,128)(2,1)S(1)}, u32[]{:S(2)}, u32[]{:S(2)}) collective-permute-start(bf16[2,128,1024]{2,1,0:T(8,128)(2,1)S(1)} %pad_maximum_fusion), channel_id=1, source_target_pairs={{0,4},{4,0},{8,12},{12,8},{16,20},{20,16},{24,28},{28,24},{1,5},{5... | collective-permute-start | bytes 1572872 | tf_op jit(solution)/shard_map/ppermute | solution.py:230
  23.3 0.0 collective-permute-done.4.refs_0_
  23.3 0.0 copy-done
  23.3 6.1 %rim.1 = (f32[256,1024]{1,0:T(8,128)S(1)}, f32[256,1024]{1,0:T(8,128)S(1)}, f32[256,1024]{1,0:T(8,128)S(1)}) custom-call(s32[1,2,8]{2,1,0:T(2,128)S(1)} %copy-done.3, bf16[2,128,1024]{2,1,0:T(8,128)(2,1)S(1)} %collective-permute-done.4.refs_0_, ...), custom_call_target="tpu_custom_call", output_to_operand_aliasing={{0}: (5, {}), {1}: (6, {}), {2}: (7, {})} | custom-call | tf_op jit(solution)/shard_map/rim/pallas_call | solution.py:198
  29.4 0.0 collective-permute-done.3.refs_2_
  29.4 0.2 collective-permute-done.2.refs_1_
  29.6 1.6 %collective-permute-start.6 = (bf16[1,128,1024]{2,1,0:T(8,128)(2,1)S(1)}, bf16[1,128,1024]{2,1,0:T(8,128)(2,1)S(1)}, u32[]{:S(2)}, u32[]{:S(2)}) collective-permute-start(bf16[1,128,1024]{2,1,0:T(8,128)(2,1)S(1)} %get-tuple-element.30.refs_2_), channel_id=1, source_target_pairs={{0,1},{1,0},{2,3},{3,2},{4,5},{5,4},{6,7},{7,6},{8,9},{9,8},{10,11... | collective-permute-start | bytes 786440 | tf_op jit(solution)/shard_map/ppermute | solution.py:289
  31.2 0.4 collective-permute-start.7
  31.6 6.1 %lon.1 = (f32[256,1024]{1,0:T(8,128)S(1)}, f32[256,1024]{1,0:T(8,128)S(1)}, f32[256,1024]{1,0:T(8,128)S(1)}) custom-call(s32[1,2,8]{2,1,0:T(2,128)S(1)} %copy-done.3, bf16[1,128,1024]{2,1,0:T(8,128)(2,1)S(1)} %get-tuple-element.32.refs_0_, ...), custom_call_target="tpu_custom_call", output_to_operand_aliasing={{0}: (7, {}), {1}: (8, {}), {2}: (9, {})} | custom-call | tf_op jit(solution)/shard_map/lon/pallas_call | solution.py:198
  37.7 0.0 copy-start.1
  37.7 0.0 collective-permute-done.9.refs_1_
  37.8 0.0 collective-permute-done.8.refs_0_
  37.8 4.8 %corner.1 = (f32[256,1024]{1,0:T(8,128)S(1)}, f32[256,1024]{1,0:T(8,128)S(1)}, f32[256,1024]{1,0:T(8,128)S(1)}) custom-call(s32[1,2,8]{2,1,0:T(2,128)S(1)} %copy-done.3, bf16[2,128,1024]{2,1,0:T(8,128)(2,1)S(1)} %collective-permute-done.8.refs_0_, ...), custom_call_target="tpu_custom_call", output_to_operand_aliasing={{0}: (5, {}), {1}: (6, {}), {2}: (7, {})} | custom-call | tf_op jit(solution)/shard_map/corner/pallas_call | solution.py:198
  42.6 0.0 collective-permute-done.6.refs_0_
  42.6 0.8 %collective-permute-done.7.refs_1_ = bf16[1,128,1024]{2,1,0:T(8,128)(2,1)S(1)} collective-permute-done((bf16[1,128,1024]{2,1,0:T(8,128)(2,1)S(1)}, bf16[1,128,1024]{2,1,0:T(8,128)(2,1)S(1)}, u32[]{:S(2)}, u32[]{:S(2)}) %collective-permute-start.7) | collective-permute-done | bytes 262176 | tf_op jit(solution)/shard_map/ppermute | solution.py:290
  43.4 0.0 copy-done.1
  43.4 4.9 %across.1 = (bf16[256,1024]{1,0:T(8,128)(2,1)}, f32[256,1024]{1,0:T(8,128)S(1)}, f32[256,1024]{1,0:T(8,128)S(1)}, f32[256,1024]{1,0:T(8,128)S(1)}) custom-call(s32[1,2,8]{2,1,0:T(2,128)S(1)} %copy-done.3, bf16[1,128,1024]{2,1,0:T(8,128)(2,1)S(1)} %collective-permute-done.6.refs_0_, ...), custom_call_target="tpu_custom_call", output_to_operand_aliasing={{1}: (6, {}), {2}: (7, {}), {3}: (8, {})} | custom-call | tf_op jit(solution)/shard_map/across/pallas_call | solution.py:198
  (3 shorter events, 0.0 us)
Async XLA Ops:
  0.0 23.3 %copy-start = (bf16[1024,3072]{1,0:T(8,128)(2,1)S(1)}, bf16[1024,3072]{1,0:T(8,128)(2,1)}, u32[]{:S(2)}) copy-start(bf16[1024,3072]{1,0:T(8,128)(2,1)} %refs_3_.5) | copy-start | bytes 18874372
  1.2 15.6 %collective-permute-start.1 = (bf16[1,128,1024]{2,1,0:T(8,128)(2,1)S(1)}, bf16[1,128,1024]{2,1,0:T(8,128)(2,1)S(1)}, u32[]{:S(2)}, u32[]{:S(2)}) collective-permute-start(bf16[1,128,1024]{2,1,0:T(8,128)(2,1)S(1)} %get-tuple-element.45), channel_id=1, source_target_pairs={{0,3},{3,0},{1,2},{2,1},{4,7},{7,4},{5,6},{6,5},{8,11},{11,8},{9,1... | collective-permute-start | bytes 786440 | tf_op jit(solution)/shard_map/ppermute | solution.py:279
  6.3 13.0 %collective-permute-start = (bf16[1,128,1024]{2,1,0:T(8,128)(2,1)S(1)}, bf16[1,128,1024]{2,1,0:T(8,128)(2,1)S(1)}, u32[]{:S(2)}, u32[]{:S(2)}) collective-permute-start(bf16[1,128,1024]{2,1,0:T(8,128)(2,1)S(1)} %get-tuple-element.46), channel_id=1, source_target_pairs={{0,1},{1,0},{2,3},{3,2},{4,5},{5,4},{6,7},{7,6},{8,9},{9,8},{10,11... | collective-permute-start | bytes 786440 | tf_op jit(solution)/shard_map/ppermute | solution.py:278
  6.3 14.0 %collective-permute-start.5 = (bf16[2,128,1024]{2,1,0:T(8,128)(2,1)}, bf16[2,128,1024]{2,1,0:T(8,128)(2,1)S(1)}, u32[]{:S(2)}, u32[]{:S(2)}) collective-permute-start(bf16[2,128,1024]{2,1,0:T(8,128)(2,1)} %bitcast.6), channel_id=1, source_target_pairs={{4,8},{8,4},{12,16},{16,12},{20,24},{24,20},{5,9},{9,5},{13,17},{1... | collective-permute-start | bytes 1572872 | tf_op jit(solution)/shard_map/ppermute | solution.py:230
  7.0 22.3 %collective-permute-start.3 = (bf16[1,128,1024]{2,1,0:T(8,128)(2,1)S(1)}, bf16[1,128,1024]{2,1,0:T(8,128)(2,1)S(1)}, u32[]{:S(2)}, u32[]{:S(2)}) collective-permute-start(bf16[1,128,1024]{2,1,0:T(8,128)(2,1)S(1)} %get-tuple-element.45), channel_id=1, source_target_pairs={{0,1},{1,0},{2,3},{3,2},{4,5},{5,4},{6,7},{7,6},{8,9},{9,8},{10,11... | collective-permute-start | bytes 786440 | tf_op jit(solution)/shard_map/ppermute | solution.py:282
  9.1 20.5 %collective-permute-start.2 = (bf16[1,128,1024]{2,1,0:T(8,128)(2,1)S(1)}, bf16[1,128,1024]{2,1,0:T(8,128)(2,1)S(1)}, u32[]{:S(2)}, u32[]{:S(2)}) collective-permute-start(bf16[1,128,1024]{2,1,0:T(8,128)(2,1)S(1)} %get-tuple-element.46), channel_id=1, source_target_pairs={{0,3},{3,0},{1,2},{2,1},{4,7},{7,4},{5,6},{6,5},{8,11},{11,8},{9,1... | collective-permute-start | bytes 786440 | tf_op jit(solution)/shard_map/ppermute | solution.py:283
  9.2 1.0 %copy-start.2 = (bf16[1,2,128,1024]{3,2,1,0:T(8,128)(2,1)S(1)}, bf16[1,2,128,1024]{3,2,1,0:T(8,128)(2,1)}, u32[]{:S(2)}) copy-start(bf16[1,2,128,1024]{3,2,1,0:T(8,128)(2,1)} %param.4) | copy-start | bytes 1572868
  10.2 0.7 %copy-start.3 = (s32[1,2,8]{2,1,0:T(2,128)S(1)}, s32[1,2,8]{2,1,0:T(2,128)}, u32[]{:S(2)}) copy-start(s32[1,2,8]{2,1,0:T(2,128)} %tele_ref.9) | copy-start | bytes 196
  16.8 6.4 %collective-permute-start.4 = (bf16[2,128,1024]{2,1,0:T(8,128)(2,1)S(1)}, bf16[2,128,1024]{2,1,0:T(8,128)(2,1)S(1)}, u32[]{:S(2)}, u32[]{:S(2)}) collective-permute-start(bf16[2,128,1024]{2,1,0:T(8,128)(2,1)S(1)} %bitcast.8), channel_id=1, source_target_pairs={{0,4},{4,0},{8,12},{12,8},{16,20},{20,16},{24,28},{28,24},{1,5},{5... | collective-permute-start | bytes 1572872 | tf_op jit(solution)/shard_map/ppermute | solution.py:230
  19.5 18.3 %collective-permute-start.9 = (bf16[2,128,1024]{2,1,0:T(8,128)(2,1)S(1)}, bf16[2,128,1024]{2,1,0:T(8,128)(2,1)S(1)}, u32[]{:S(2)}, u32[]{:S(2)}) collective-permute-start(bf16[2,128,1024]{2,1,0:T(8,128)(2,1)S(1)} %pad_maximum_fusion), channel_id=1, source_target_pairs={{4,8},{8,4},{12,16},{16,12},{20,24},{24,20},{5,9},{9,5},{13,17},{1... | collective-permute-start | bytes 1572872 | tf_op jit(solution)/shard_map/ppermute | solution.py:230
  20.4 17.4 %collective-permute-start.8 = (bf16[2,128,1024]{2,1,0:T(8,128)(2,1)S(1)}, bf16[2,128,1024]{2,1,0:T(8,128)(2,1)S(1)}, u32[]{:S(2)}, u32[]{:S(2)}) collective-permute-start(bf16[2,128,1024]{2,1,0:T(8,128)(2,1)S(1)} %pad_maximum_fusion), channel_id=1, source_target_pairs={{0,4},{4,0},{8,12},{12,8},{16,20},{20,16},{24,28},{28,24},{1,5},{5... | collective-permute-start | bytes 1572872 | tf_op jit(solution)/shard_map/ppermute | solution.py:230
  29.6 13.0 %collective-permute-start.6 = (bf16[1,128,1024]{2,1,0:T(8,128)(2,1)S(1)}, bf16[1,128,1024]{2,1,0:T(8,128)(2,1)S(1)}, u32[]{:S(2)}, u32[]{:S(2)}) collective-permute-start(bf16[1,128,1024]{2,1,0:T(8,128)(2,1)S(1)} %get-tuple-element.30.refs_2_), channel_id=1, source_target_pairs={{0,1},{1,0},{2,3},{3,2},{4,5},{5,4},{6,7},{7,6},{8,9},{9,8},{10,11... | collective-permute-start | bytes 786440 | tf_op jit(solution)/shard_map/ppermute | solution.py:289
  31.2 12.1 %collective-permute-start.7 = (bf16[1,128,1024]{2,1,0:T(8,128)(2,1)S(1)}, bf16[1,128,1024]{2,1,0:T(8,128)(2,1)S(1)}, u32[]{:S(2)}, u32[]{:S(2)}) collective-permute-start(bf16[1,128,1024]{2,1,0:T(8,128)(2,1)S(1)} %get-tuple-element.31.refs_3_), channel_id=1, source_target_pairs={{0,1},{1,0},{2,3},{3,2},{4,5},{5,4},{6,7},{7,6},{8,9},{9,8},{10,11... | collective-permute-start | bytes 786440 | tf_op jit(solution)/shard_map/ppermute | solution.py:290
  37.7 5.6 %copy-start.1 = (bf16[1024,1024]{1,0:T(8,128)(2,1)S(1)}, bf16[1024,1024]{1,0:T(8,128)(2,1)}, u32[]{:S(2)}) copy-start(bf16[1024,1024]{1,0:T(8,128)(2,1)} %refs_4_.1) | copy-start | bytes 6291460
